TPU v7x, 32 devices: a whole 2x2x4 slice. The times are simulated.
32 devices in a mesh: rows: 4 (over x, core), seq: 8 (over z, y).
Axes of the slice: x: 2, y: 2, z: 4, core: 2. Of those that a mesh axis runs over, the one named last changes fastest.
Arguments:
- hidden_in: bfloat16 [16, 512, 1024], P('rows', 'seq'), may hold values from -6 to 6
- segment_ids: int32 [16, 512], P('rows', 'seq'), may hold values from 0 to 6, as said below
- positions: int32 [16, 512], P('rows', 'seq'), may hold values from 0 to 385, as said below
- expert_ids: int32 [16, 512, 8], P('rows', 'seq'), may hold values from 0 to 31, all different within a row; in each aligned block of 64 rows (0 to 63, 64 to 127, ..., all dimensions but the last counted through in order) at most 32 rows name the same one
- first_gain: float32 [1024], replicated, may hold values from 0.25 to 1.75
- query_weight: bfloat16 [1024, 1024], replicated, may hold values from -0.1875 to 0.1875
- key_weight: bfloat16 [1024, 512], replicated, may hold values from -0.1875 to 0.1875
- value_weight: bfloat16 [1024, 512], replicated, may hold values from -0.1875 to 0.1875
- output_weight: bfloat16 [1024, 1024], replicated, may hold values from -0.75 to 0.75
- second_gain: float32 [1024], replicated, may hold values from 0.25 to 1.75
- router_weight: bfloat16 [1024, 32], replicated, may hold values from -0.09375 to 0.09375
- gate_weight: bfloat16 [32, 1024, 512], P('seq'), may hold values from -0.1875 to 0.1875
- up_weight: bfloat16 [32, 1024, 512], P('seq'), may hold values from -0.1875 to 0.1875
- down_weight: bfloat16 [32, 512, 1024], P('seq'), may hold values from -1 to 1
- out_grad: bfloat16 [16, 512, 1024], P('rows', 'seq'), may hold values from -6 to 6
Outputs:
- hidden_out: bfloat16 [16, 512, 1024], P('rows', 'seq')
- grad_hidden: float32 [16, 512, 1024], P('rows', 'seq')
- grad_first: float32 [1024], replicated
- grad_query: float32 [1024, 1024], replicated
- grad_key: float32 [1024, 512], replicated
- grad_value: float32 [1024, 512], replicated
- grad_output: float32 [1024, 1024], replicated
- grad_second: float32 [1024], replicated
- grad_router: float32 [1024, 32], replicated
- grad_gate: float32 [32, 1024, 512], P('seq')
- grad_up: float32 [32, 1024, 512], P('seq')
- grad_down: float32 [32, 512, 1024], P('seq')
Inputs may be any that keep to these rules, and one draw needn't show every extreme that they name: `segment_ids`: along each row the ids start at 0, never fall and rise by one at each of 6 boundaries; a document is a run of equal ids. In each group of 4 rows on one index of rows, one row holds a document that begins within the row's first 64 tokens and ends within its last 64. `positions`: each token's offset from the first token of its document. `expert_ids`: each token names 8 different experts. Among the 64 tokens of one row on one device no expert is named by more than 32 tokens, and in some such block one expert is named by exactly 32.
All inputs are finite; a program needn't handle non-finite values.
Results may differ from a plain program's by a relative error of at most 0.023.
Values may be sent and summed in bfloat16 or wider, within the bound.
No kernel may reach another device: no remote copies, remote signals or barrier semaphores. Data moves between devices by JAX's collectives and lax.ppermute only.
A program may use at most 256 MiB of HBM per device.

v0:
```python
import math

import jax
import jax.numpy as jnp
from jax import lax
from jax.sharding import PartitionSpec as P

HEADS = 16
KV_HEADS = 8
HEAD_DIM = 64
TOPK = 8
MOST = 32


EPS = 1e-06
THETA = 10000.0
NEG = -1e30


def rope_tables(places, head_size):
    middle = head_size // 2
    frequency = jnp.exp(
        jnp.arange(middle, dtype=jnp.float32) * (-2.0 * math.log(THETA) / head_size)
    )
    angles = places.astype(jnp.float32)[..., None, None] * frequency
    return (jnp.cos(angles), jnp.sin(angles))


def rotate(values, cosine, sine_part):
    middle = values.shape[-1] // 2
    first = values[..., :middle]
    second = values[..., middle:]
    return jnp.concatenate(
        [first * cosine - second * sine_part, second * cosine + first * sine_part], axis=-1
    )


def unrotate(values, cosine, sine_part):
    middle = values.shape[-1] // 2
    first = values[..., :middle]
    second = values[..., middle:]
    return jnp.concatenate(
        [first * cosine + second * sine_part, second * cosine - first * sine_part], axis=-1
    )


def slice_all(arrays, offset_at, span):
    return tuple((lax.dynamic_slice_in_dim(member, offset_at, span, 1) for member in arrays))


def attend_piece(carry, piece, queries, query_seg, query_pos):
    count = piece[0].shape[1]
    span = math.gcd(count, 512)
    scale = queries.shape[-1] ** (-0.5)

    def one_step(counter, state):
        running_sum, running_max, total_mass = state
        offset_at = counter * span
        key_blk, value_blk, seg_blk = slice_all(piece, offset_at, span)
        key_pos = offset_at + jnp.arange(span, dtype=jnp.int32)
        allowed = (key_pos[None, None, :] <= query_pos[None, :, None]) & (
            seg_blk[:, None, :] == query_seg[:, :, None]
        )
        allowed = allowed[:, :, None, None, :]
        scores = (
            jnp.einsum("rqgjd,rkgd->rqgjk", queries, key_blk, preferred_element_type=jnp.float32)
            * scale
        )
        scores = jnp.where(allowed, scores, NEG)
        new_max = jnp.maximum(running_max, jnp.max(scores, axis=-1))
        weights = jnp.where(allowed, jnp.exp(scores - new_max[..., None]), 0.0)
        shrink = jnp.exp(running_max - new_max)
        total_mass = total_mass * shrink + jnp.sum(weights, axis=-1)
        running_sum = running_sum * shrink[..., None] + jnp.einsum(
            "rqgjk,rkgd->rqgjd",
            weights.astype(jnp.bfloat16),
            value_blk,
            preferred_element_type=jnp.float32,
        )
        return (running_sum, new_max, total_mass)

    return lax.fori_loop(0, count // span, one_step, carry)


def pair_grads(query_side, key_side, query_pos, key_pos):
    queries, grad_att, logsum, delta, query_seg = query_side
    key_rows, value_rows, key_seg = key_side
    scale = queries.shape[-1] ** (-0.5)
    allowed = (key_pos[None, None, :] <= query_pos[None, :, None]) & (
        key_seg[:, None, :] == query_seg[:, :, None]
    )
    allowed = allowed[:, :, None, None, :]
    scores = (
        jnp.einsum("rqgjd,rkgd->rqgjk", queries, key_rows, preferred_element_type=jnp.float32)
        * scale
    )
    probs = jnp.where(allowed, jnp.exp(scores - logsum[..., None]), 0.0)
    grad_probs = jnp.einsum(
        "rqgjd,rkgd->rqgjk", grad_att, value_rows, preferred_element_type=jnp.float32
    )
    grad_scores = (probs * (grad_probs - delta[..., None]) * scale).astype(jnp.bfloat16)
    query_grad = jnp.einsum(
        "rqgjk,rkgd->rqgjd", grad_scores, key_rows, preferred_element_type=jnp.float32
    )
    key_grad = jnp.einsum(
        "rqgjk,rqgjd->rkgd", grad_scores, queries, preferred_element_type=jnp.float32
    )
    value_grad = jnp.einsum(
        "rqgjk,rqgjd->rkgd",
        probs.astype(jnp.bfloat16),
        grad_att,
        preferred_element_type=jnp.float32,
    )
    return (query_grad, key_grad, value_grad)


def local(
    hidden_in,
    segment_ids,
    positions,
    expert_ids,
    first_gain,
    query_weight,
    key_weight,
    value_weight,
    output_weight,
    second_gain,
    router_weight,
    gate_weight,
    up_weight,
    down_weight,
    out_grad,
):
    row_count, block_size, model_width = hidden_in.shape
    token_count = row_count * block_size
    group_size = HEADS // KV_HEADS
    shard_count = lax.axis_size("seq")
    offset = lax.axis_index("seq") * block_size
    query_pos = offset + jnp.arange(block_size, dtype=jnp.int32)
    inputs = hidden_in.astype(jnp.float32).reshape(token_count, model_width)
    scale_one = lax.rsqrt(jnp.mean(inputs * inputs, axis=-1, keepdims=True) + EPS)
    normed_one = inputs * scale_one
    mixer_input = (normed_one * first_gain).astype(jnp.bfloat16)
    query_pre = jnp.dot(mixer_input, query_weight, preferred_element_type=jnp.float32).reshape(
        row_count, block_size, HEADS, HEAD_DIM
    )
    key_pre = jnp.dot(mixer_input, key_weight, preferred_element_type=jnp.float32).reshape(
        row_count, block_size, KV_HEADS, HEAD_DIM
    )
    value_pre = jnp.dot(mixer_input, value_weight, preferred_element_type=jnp.float32).reshape(
        row_count, block_size, KV_HEADS, HEAD_DIM
    )
    cosine, sine_part = rope_tables(positions, HEAD_DIM)
    queries = (
        rotate(query_pre, cosine, sine_part)
        .astype(jnp.bfloat16)
        .reshape(row_count, block_size, KV_HEADS, group_size, HEAD_DIM)
    )
    key_rows = rotate(key_pre, cosine, sine_part).astype(jnp.bfloat16)
    value_rows = value_pre.astype(jnp.bfloat16)
    start_state = (
        jnp.zeros((row_count, block_size, KV_HEADS, group_size, HEAD_DIM), jnp.float32),
        jnp.full((row_count, block_size, KV_HEADS, group_size), NEG, jnp.float32),
        jnp.zeros((row_count, block_size, KV_HEADS, group_size), jnp.float32),
    )
    running_sum, running_max, total_mass = attend_piece(
        start_state,
        (
            lax.all_gather(key_rows, "seq", axis=1, tiled=True),
            lax.all_gather(value_rows, "seq", axis=1, tiled=True),
            lax.all_gather(segment_ids, "seq", axis=1, tiled=True),
        ),
        queries,
        segment_ids,
        query_pos,
    )
    attended = running_sum / total_mass[..., None]
    logsum = running_max + jnp.log(total_mass)
    mixed_low = attended.astype(jnp.bfloat16).reshape(token_count, HEADS * HEAD_DIM)
    residual = inputs + jnp.dot(mixed_low, output_weight, preferred_element_type=jnp.float32)
    scale_two = lax.rsqrt(jnp.mean(residual * residual, axis=-1, keepdims=True) + EPS)
    normed_two = residual * scale_two
    expert_input = (normed_two * second_gain).astype(jnp.bfloat16)
    router_full = router_weight.astype(jnp.float32)
    logits = jnp.dot(expert_input, router_weight, preferred_element_type=jnp.float32)
    routes = expert_ids.reshape(token_count, TOPK)
    gates = jax.nn.softmax(jnp.take_along_axis(logits, routes, axis=1), axis=-1)
    expert_count = router_weight.shape[1]
    expert_range = jnp.arange(expert_count, dtype=jnp.int32)
    one_hot = (routes.reshape(row_count, block_size * TOPK)[..., None] == expert_range).astype(
        jnp.int32
    )
    ranks = jnp.cumsum(one_hot, axis=1, dtype=jnp.int32) - 1
    slots = jnp.sum(ranks * one_hot, axis=-1, dtype=jnp.int32).reshape(token_count, TOPK)
    row_index = jnp.broadcast_to(
        (jnp.arange(token_count, dtype=jnp.int32) // block_size)[:, None], routes.shape
    )
    flat_index = jnp.arange(token_count * TOPK, dtype=jnp.int32).reshape(token_count, TOPK)
    slot_table = (
        jnp.full((expert_count, row_count, MOST), token_count * TOPK, jnp.int32)
        .at[routes, row_index, slots]
        .set(flat_index)
    )
    slot_token = slot_table // TOPK
    slot_flat = (routes * row_count + row_index) * MOST + slots
    local_count = gate_weight.shape[0]
    padded_in = jnp.concatenate([expert_input, jnp.zeros((1, model_width), jnp.bfloat16)], axis=0)
    dispatch = padded_in[slot_token].reshape(shard_count, local_count, row_count, MOST, model_width)
    received = lax.all_to_all(dispatch, "seq", split_axis=0, concat_axis=0, tiled=True)
    gate_pre = jnp.einsum(
        "secmd,edf->secmf", received, gate_weight, preferred_element_type=jnp.float32
    )
    up_pre = jnp.einsum("secmd,edf->secmf", received, up_weight, preferred_element_type=jnp.float32)
    hidden_act = (jax.nn.silu(gate_pre) * up_pre).astype(jnp.bfloat16)
    produced = jnp.einsum(
        "secmf,efd->secmd", hidden_act, down_weight, preferred_element_type=jnp.float32
    ).astype(jnp.bfloat16)
    returned = lax.all_to_all(produced, "seq", split_axis=0, concat_axis=0, tiled=True)
    expert_out, received, gate_pre, up_pre = (returned, received, gate_pre, up_pre)
    picked_full = expert_out.reshape(-1, model_width)[slot_flat].astype(jnp.float32)
    combined = jnp.einsum("tkd,tk->td", picked_full, gates)
    hidden_out = (
        (residual + combined).astype(jnp.bfloat16).reshape(row_count, block_size, model_width)
    )
    upstream = out_grad.astype(jnp.float32).reshape(token_count, model_width)
    grad_gates = jnp.einsum("tkd,td->tk", picked_full, upstream)
    grad_chosen = gates * (grad_gates - jnp.sum(gates * grad_gates, axis=-1, keepdims=True))
    route_hot = (routes[..., None] == expert_range).astype(jnp.float32)
    grad_logits = jnp.einsum("tke,tk->te", route_hot, grad_chosen)
    router_part = jnp.dot(
        expert_input.astype(jnp.float32).T, grad_logits, precision=lax.Precision.HIGHEST
    )
    grad_normed = jnp.dot(grad_logits, router_full.T, precision=lax.Precision.HIGHEST)
    gate_pad = jnp.concatenate([gates.reshape(-1), jnp.zeros((1,), jnp.float32)], axis=0)
    slot_gate = gate_pad[slot_table]
    upstream_pad = jnp.concatenate([upstream, jnp.zeros((1, model_width), jnp.float32)], axis=0)
    slot_grad = (upstream_pad[slot_token] * slot_gate[..., None]).astype(jnp.bfloat16)
    slot_grad = slot_grad.reshape(shard_count, local_count, row_count, MOST, model_width)
    arrived = lax.all_to_all(slot_grad, "seq", split_axis=0, concat_axis=0, tiled=True)
    sigmoid_gate = jax.nn.sigmoid(gate_pre)
    silu_gate = gate_pre * sigmoid_gate
    hidden_act = (silu_gate * up_pre).astype(jnp.bfloat16)
    grad_act = jnp.einsum(
        "secmd,efd->secmf", arrived, down_weight, preferred_element_type=jnp.float32
    )
    down_part = jnp.einsum(
        "secmf,secmd->efd", hidden_act, arrived, preferred_element_type=jnp.float32
    )
    grad_gate_pre = (
        grad_act * up_pre * sigmoid_gate * (1.0 + gate_pre * (1.0 - sigmoid_gate))
    ).astype(jnp.bfloat16)
    grad_up_pre = (grad_act * silu_gate).astype(jnp.bfloat16)
    gate_part = jnp.einsum(
        "secmd,secmf->edf", received, grad_gate_pre, preferred_element_type=jnp.float32
    )
    up_part = jnp.einsum(
        "secmd,secmf->edf", received, grad_up_pre, preferred_element_type=jnp.float32
    )
    grad_received = (
        jnp.einsum(
            "secmf,edf->secmd", grad_gate_pre, gate_weight, preferred_element_type=jnp.float32
        )
        + jnp.einsum("secmf,edf->secmd", grad_up_pre, up_weight, preferred_element_type=jnp.float32)
    ).astype(jnp.bfloat16)
    sent_back = lax.all_to_all(grad_received, "seq", split_axis=0, concat_axis=0, tiled=True)
    grad_normed = grad_normed + jnp.sum(
        sent_back.reshape(-1, model_width)[slot_flat].astype(jnp.float32), axis=1
    )
    scaled_two = grad_normed * second_gain
    second_part = jnp.sum(grad_normed * normed_two, axis=0)
    grad_residual = upstream + scale_two * (
        scaled_two - normed_two * jnp.mean(scaled_two * normed_two, axis=-1, keepdims=True)
    )
    grad_mixed = grad_residual.astype(jnp.bfloat16)
    output_part = jnp.einsum("td,te->de", mixed_low, grad_mixed, preferred_element_type=jnp.float32)
    grad_att = jnp.einsum(
        "te,de->td", grad_mixed, output_weight, preferred_element_type=jnp.float32
    )
    grad_att = grad_att.astype(jnp.bfloat16).reshape(
        row_count, block_size, KV_HEADS, group_size, HEAD_DIM
    )
    delta = jnp.sum(grad_att.astype(jnp.float32) * attended, axis=-1)
    query_side = (queries, grad_att, logsum, delta, segment_ids)
    query_zero = jnp.zeros((row_count, block_size, KV_HEADS, group_size, HEAD_DIM), jnp.float32)
    whole_rows = (
        lax.all_gather(key_rows, "seq", axis=1, tiled=True),
        lax.all_gather(value_rows, "seq", axis=1, tiled=True),
        lax.all_gather(segment_ids, "seq", axis=1, tiled=True),
    )
    total_len = whole_rows[0].shape[1]
    span = math.gcd(total_len, 512)

    def back_step(counter, state):
        query_acc, key_acc, value_acc = state
        offset_at = counter * span
        key_block = slice_all(whole_rows, offset_at, span)
        key_pos = offset_at + jnp.arange(span, dtype=jnp.int32)
        query_grad, key_grad, value_grad = pair_grads(query_side, key_block, query_pos, key_pos)
        key_acc = lax.dynamic_update_slice_in_dim(key_acc, key_grad, offset_at, 1)
        value_acc = lax.dynamic_update_slice_in_dim(value_acc, value_grad, offset_at, 1)
        return (query_acc + query_grad, key_acc, value_acc)

    full_zero = jnp.zeros((row_count, total_len, KV_HEADS, HEAD_DIM), jnp.float32)
    grad_queries, key_acc, value_acc = lax.fori_loop(
        0, total_len // span, back_step, (query_zero, full_zero, full_zero)
    )
    grad_keys, grad_values = (
        lax.psum_scatter(
            key_acc.astype(jnp.bfloat16), "seq", scatter_dimension=1, tiled=True
        ).astype(jnp.float32),
        lax.psum_scatter(
            value_acc.astype(jnp.bfloat16), "seq", scatter_dimension=1, tiled=True
        ).astype(jnp.float32),
    )
    grad_query_pre = unrotate(
        grad_queries.reshape(row_count, block_size, HEADS, HEAD_DIM), cosine, sine_part
    )
    grad_query_pre = grad_query_pre.astype(jnp.bfloat16).reshape(token_count, HEADS * HEAD_DIM)
    grad_key_pre = (
        unrotate(grad_keys, cosine, sine_part)
        .astype(jnp.bfloat16)
        .reshape(token_count, KV_HEADS * HEAD_DIM)
    )
    grad_value_pre = grad_values.astype(jnp.bfloat16).reshape(token_count, KV_HEADS * HEAD_DIM)
    query_part = jnp.einsum(
        "td,te->de", mixer_input, grad_query_pre, preferred_element_type=jnp.float32
    )
    key_part = jnp.einsum(
        "td,te->de", mixer_input, grad_key_pre, preferred_element_type=jnp.float32
    )
    value_part = jnp.einsum(
        "td,te->de", mixer_input, grad_value_pre, preferred_element_type=jnp.float32
    )
    grad_mixer = (
        jnp.einsum("te,de->td", grad_query_pre, query_weight, preferred_element_type=jnp.float32)
        + jnp.einsum("te,de->td", grad_key_pre, key_weight, preferred_element_type=jnp.float32)
        + jnp.einsum("te,de->td", grad_value_pre, value_weight, preferred_element_type=jnp.float32)
    )
    scaled_one = grad_mixer * first_gain
    first_part = jnp.sum(grad_mixer * normed_one, axis=0)
    grad_input = grad_residual + scale_one * (
        scaled_one - normed_one * jnp.mean(scaled_one * normed_one, axis=-1, keepdims=True)
    )
    shared = lax.psum(
        (first_part, query_part, key_part, value_part, output_part, second_part, router_part),
        ("rows", "seq"),
    )
    local_sums = (
        lax.psum(gate_part.astype(jnp.bfloat16), "rows").astype(jnp.float32),
        lax.psum(up_part.astype(jnp.bfloat16), "rows").astype(jnp.float32),
        lax.psum(down_part.astype(jnp.bfloat16), "rows").astype(jnp.float32),
    )
    return (
        hidden_out,
        grad_input.reshape(row_count, block_size, model_width),
        shared[0],
        shared[1],
        shared[2],
        shared[3],
        shared[4],
        shared[5],
        shared[6],
        local_sums[0],
        local_sums[1],
        local_sums[2],
    )


def solution(mesh):
    placed = (
        P("rows", "seq", None),
        P("rows", "seq"),
        P("rows", "seq"),
        P("rows", "seq", None),
        P(),
        P(),
        P(),
        P(),
        P(),
        P(),
        P(),
        P("seq", None, None),
        P("seq", None, None),
        P("seq", None, None),
        P("rows", "seq", None),
    )
    return jax.shard_map(
        local,
        mesh=mesh,
        in_specs=placed,
        out_specs=(
            P("rows", "seq", None),
            P("rows", "seq", None),
            P(),
            P(),
            P(),
            P(),
            P(),
            P(),
            P(),
            P("seq", None, None),
            P("seq", None, None),
            P("seq", None, None),
        ),
        check_vma=False,
    )
```

profile of v0, /device:TPU:0, one launch (start us, length us, event | category | flops | bytes accessed | tf_op | source)
XLA Modules:
  0.0 1695.8 jit_solution(3441458120258700389)
XLA Ops:
  30.9 4.6 reduce-window.6
  36.3 28.3 %all-gather = s32[8,64,4]{1,2,0:T(4,128)S(1)} all-gather(s32[1,64,4]{1,2,0:T(4,128)S(1)} %bitcast.333), channel_id=1, replica_groups=mesh['rows'=4,'seq'=8] {'seq'}, dimensions={0}, use_global_device_ids=true | all-gather | bytes 9216 | tf_op jit(solution)/shard_map/all_gather | solution.py:171
  70.3 8.5 scatter_custom_fusion
  79.4 14.2 all-gather.4.cloned.1.call-done
  93.7 5.4 copy.195
  107.2 60.9 %all-gather.6.cloned.1.call-done = bf16[4,512,8,64]{3,1,2,0:T(8,128)(2,1)} async-done(((bf16[4,64,8,64]{3,1,2,0:T(8,128)(2,1)}), bf16[4,512,8,64]{3,1,2,0:T(8,128)(2,1)}) %all-gather.6.cloned.1.call-update) | async-done | bytes 2097168 | tf_op jit(solution)/shard_map/all_gather | solution.py:170
  168.0 8.9 fusion.107
  186.8 18.1 %gather_fusion = bf16[4096,1024]{1,0:T(8,128)(2,1)} fusion(bf16[257,1024]{1,0:T(8,128)(2,1)S(1)} %concatenate.35, s32[4096]{0:T(1024)S(1)} %broadcast_clamp_fusion.1), kind=kCustom, calls=%fused_computation | custom fusion | bytes 16793600 | tf_op jit(solution)/shard_map/gather | solution.py:208
  204.9 5.1 all-to-all-start
  210.4 18.7 %gather_fusion.2 = f32[4096,1024]{1,0:T(8,128)} fusion(f32[257,1024]{1,0:T(8,128)S(1)} %concatenate.37, s32[4096]{0:T(1024)S(1)} %broadcast_clamp_fusion.1), kind=kCustom, calls=%fused_computation.2 | custom fusion | bytes 33570816 | tf_op jit(solution)/shard_map/gather | solution.py:237
  230.7 16.8 gather_fusion.5
  248.4 23.0 %gather_fusion.3 = f32[4096]{0:T(1024)S(1)} fusion(f32[2049]{0:T(1024)S(1)} %pad_maximum_fusion.4, s32[4096]{0:T(1024)S(1)} %broadcast_clamp_fusion), kind=kCustom, calls=%fused_computation.3 | custom fusion | bytes 49152 | tf_op jit(solution)/shard_map/gather | solution.py:235
  271.6 9.1 multiply_convert_fusion
  280.6 111.6 %all-to-all-done = bf16[8,4,4,32,1024]{4,3,2,1,0:T(8,128)(2,1)} async-done(((bf16[8,4,4,32,1024]{4,3,2,1,0:T(8,128)(2,1)}), bf16[8,4,4,32,1024]{4,3,2,1,0:T(8,128)(2,1)}, u32[]{:S(2)}, u32[]{:S(2)}) %all-to-all-start) | async-done | bytes 8388640 | tf_op jit(solution)/shard_map/all_to_all | solution.py:209
  392.2 5.2 all-to-all-start.2
  397.4 12.6 fusion.20
  410.0 10.1 fusion.18
  420.1 159.2 %all-to-all-done.2 = bf16[8,4,4,32,1024]{4,3,2,1,0:T(8,128)(2,1)} async-done(((bf16[8,4,4,32,1024]{4,3,2,1,0:T(8,128)(2,1)}), bf16[8,4,4,32,1024]{4,3,2,1,0:T(8,128)(2,1)}, u32[]{:S(2)}, u32[]{:S(2)}) %all-to-all-start.2) | async-done | bytes 8388640 | tf_op jit(solution)/shard_map/all_to_all | solution.py:239
  579.3 16.6 fusion.7
  595.9 13.7 fusion.34
  609.6 12.8 fusion
  622.5 8.6 copy.170
  631.1 5.0 all-to-all-start.3
  636.1 11.4 convert_bitcast_fusion
  647.5 8.5 copy.158
  656.0 162.3 %all-to-all-done.3 = bf16[8,4,4,32,1024]{4,3,2,1,0:T(8,128)(2,1)} async-done(((bf16[8,4,4,32,1024]{4,3,2,1,0:T(8,128)(2,1)}), bf16[8,4,4,32,1024]{4,3,2,1,0:T(8,128)(2,1)}, u32[]{:S(2)}, u32[]{:S(2)}) %all-to-all-start.3) | async-done | bytes 8388640 | tf_op jit(solution)/shard_map/all_to_all | solution.py:265
  818.3 5.0 all-to-all-start.1
  824.0 15.8 gather_fusion.4
  839.8 6.4 convert_reduce_fusion
  846.2 159.3 %all-to-all-done.1 = bf16[8,4,4,32,1024]{4,3,2,1,0:T(8,128)(2,1)} async-done(((bf16[8,4,4,32,1024]{4,3,2,1,0:T(8,128)(2,1)}), bf16[8,4,4,32,1024]{4,3,2,1,0:T(8,128)(2,1)}, u32[]{:S(2)}, u32[]{:S(2)}) %all-to-all-start.1) | async-done | bytes 8388640 | tf_op jit(solution)/shard_map/all_to_all | solution.py:218
  1005.5 15.4 gather_fusion.1
  1020.9 4.7 fusion.41
  1045.1 7.3 fusion.3
  1056.9 7.4 copy.208
  1064.3 6.7 reshape.621
  1071.1 11.1 bitcast_convert_fusion.2
  1082.2 6.5 fusion.66
  1088.7 7.6 copy.210
  1096.3 6.8 reshape.623
  1103.2 11.2 bitcast_convert_fusion.1
  1114.4 11.3 bitcast_convert_fusion
  1126.2 4.9 fusion.109
  1157.0 51.2 %reduce-scatter.9.cloned.1.call-done = bf16[64,2048]{1,0:T(8,128)(2,1)} async-done(((bf16[512,2048]{1,0:T(8,128)(2,1)}), bf16[64,2048]{1,0:T(8,128)(2,1)}) %reduce-scatter.9.cloned.1.call-update) | async-done | bytes 262160
  1220.3 211.4 %all-reduce.10.cloned.1.call-done = (bf16[4,1024,512]{2,1,0:T(8,128)(2,1)}, bf16[4,1024,512]{2,1,0:T(8,128)(2,1)}, bf16[4,512,1024]{2,1,0:T(8,128)(2,1)}) async-done(((bf16[4,1024,512]{2,1,0:T(8,128)(2,1)}, bf16[4,1024,512]{2,1,0:T(8,128)(2,1)}, bf16[4,512,1024]{2,1,0:T(8,128)(2,1)}), (bf16[4,1024,512]{2,1,0:T(8,128)(2,1)}, bf16[4,1024,512]{2,1,0:T(8,128)(2,1)}, ...) | async-done | bytes 12582928 | tf_op jit(solution)/shard_map/psum | solution.py:349
  1431.8 6.9 convert_element_type.189
  1451.1 40.9 %all-reduce.2 = (f32[1024]{0:T(1024)}, f32[1024]{0:T(1024)}) all-reduce(f32[1024]{0:T(1024)S(1)} %get-tuple-element.75, f32[1024]{0:T(1024)S(1)} %copy-done.50), channel_id=1, replica_groups=mesh['rows'=4,'seq'=8] {'rows','seq'}, use_global_device_ids=true, to_apply=%region_18.19 | all-reduce | flops 2048 | bytes 16384 | tf_op jit(solution)/shard_map/psum | solution.py:344
  1494.7 182.8 %all-reduce.8.cloned.1.call-done = (f32[1024,1024]{1,0:T(8,128)}, f32[1024,512]{1,0:T(8,128)}, f32[1024,512]{1,0:T(8,128)}, f32[1024,1024]{1,0:T(8,128)}, f32[1024,32]{0,1:T(8,128)}) async-done(((f32[1024,1024]{1,0:T(8,128)}, f32[1024,512]{1,0:T(8,128)}, f32[1024,512]{1,0:T(8,128)}, f32[1024,1024]{1,0:T(8,128)}, f32[1024,32]{0,1:T(8,128)}), (f32[1024,1024]{1,0:T(8,128)}, f32[1024,512]{1,0:T(8,128)}, ...) | async-done | bytes 12714000 | tf_op jit(solution)/shard_map/psum | solution.py:344
  1677.4 4.9 copy.246
  (258 shorter events, 135.5 us)
Async XLA Ops:
  7.2 176.8 %copy-start = (bf16[1024,1024]{1,0:T(8,128)(2,1)S(1)}, bf16[1024,1024]{1,0:T(8,128)(2,1)}, u32[]{:S(2)}) copy-start(bf16[1024,1024]{1,0:T(8,128)(2,1)} %param.23) | copy-start | bytes 6291460
  7.2 86.5 %all-gather.4.cloned.1.call-start = ((), (), s32[]{:S(2)}) async-start(), calls=%async_computation.6 | async-start | bytes 4718592 | tf_op jit(solution)/shard_map/all_gather | solution.py:169
  12.8 13.7 copy-start.9
  15.3 14.3 copy-start.31
  15.3 14.3 copy-start.33
  15.5 6.8 copy-start.39
  17.2 150.9 %all-gather.6.cloned.1.call-start = ((), (), s32[]{:S(2)}) async-start(), calls=%async_computation.7 | async-start | bytes 4718592 | tf_op jit(solution)/shard_map/all_gather | solution.py:170
  26.5 9.7 copy-start.53
  29.6 40.2 %copy-start.54 = (s32[3]{0:T(128)S(1)}, s32[3]{0:T(128)}, u32[]{:S(2)}) copy-start(s32[3]{0:T(128)} %constant.137) | copy-start | bytes 40
  29.6 40.2 %copy-start.55 = (s32[3]{0:T(128)S(1)}, s32[3]{0:T(128)}, u32[]{:S(2)}) copy-start(s32[3]{0:T(128)} %constant.140) | copy-start | bytes 40
  36.2 32.6 %copy-start.40 = (s32[4,64,8]{1,0,2:T(4,128)}, s32[4,64,8]{1,0,2:T(4,128)S(1)}, u32[]{:S(2)}) copy-start(s32[4,64,8]{1,0,2:T(4,128)S(1)} %copy.148) | copy-start | bytes 24580
  66.1 33.0 %copy-start.10 = (bf16[4,64,8,2,32]{4,1,3,2,0:T(8,128)(2,1)}, bf16[4,64,8,2,32]{4,1,3,2,0:T(8,128)(2,1)S(1)}, u32[]{:S(2)}) copy-start(bf16[4,64,8,2,32]{4,1,3,2,0:T(8,128)(2,1)S(1)} %copy.143) | copy-start | bytes 786436
  79.4 88.6 %copy-start.35 = (pred[4,64,512]{2,1,0:T(8,128)(4,1)}, pred[4,64,512]{2,1,0:T(8,128)(4,1)S(1)}, u32[]{:S(2)}) copy-start(pred[4,64,512]{2,1,0:T(8,128)(4,1)S(1)} %compare_and_fusion) | copy-start | bytes 393220
  168.0 15.9 copy-start.7
  176.9 8.8 copy-start.43
  184.8 20.1 %copy-start.51 = (f32[256]{0:T(256)}, f32[256]{0:T(256)S(1)}, u32[]{:S(2)}) copy-start(f32[256]{0:T(256)S(1)} %add_rsqrt_fusion.1) | copy-start | bytes 3076
  204.9 5.2 copy-start.29
  204.9 187.3 %all-to-all-start = ((bf16[8,4,4,32,1024]{4,3,2,1,0:T(8,128)(2,1)}), bf16[8,4,4,32,1024]{4,3,2,1,0:T(8,128)(2,1)}, u32[]{:S(2)}, u32[]{:S(2)}) async-start(bf16[8,4,4,32,1024]{4,3,2,1,0:T(8,128)(2,1)} %bitcast.310), calls=%async_computation | async-start | bytes 16777216 | tf_op jit(solution)/shard_map/all_to_all | solution.py:209
  210.4 19.1 %copy-start.37 = (bf16[1024,32]{0,1:T(8,128)(2,1)S(1)}, bf16[1024,32]{0,1:T(8,128)(2,1)}, u32[]{:S(2)}) copy-start(bf16[1024,32]{0,1:T(8,128)(2,1)} %param.25) | copy-start | bytes 196612
  392.2 187.1 %all-to-all-start.2 = ((bf16[8,4,4,32,1024]{4,3,2,1,0:T(8,128)(2,1)}), bf16[8,4,4,32,1024]{4,3,2,1,0:T(8,128)(2,1)}, u32[]{:S(2)}, u32[]{:S(2)}) async-start(bf16[8,4,4,32,1024]{4,3,2,1,0:T(8,128)(2,1)} %multiply_convert_fusion), calls=%async_computation.2 | async-start | bytes 16777216 | tf_op jit(solution)/shard_map/all_to_all | solution.py:239
  397.4 12.6 copy-start.25
  631.1 187.2 %all-to-all-start.3 = ((bf16[8,4,4,32,1024]{4,3,2,1,0:T(8,128)(2,1)}), bf16[8,4,4,32,1024]{4,3,2,1,0:T(8,128)(2,1)}, u32[]{:S(2)}, u32[]{:S(2)}) async-start(bf16[8,4,4,32,1024]{4,3,2,1,0:T(8,128)(2,1)} %copy.170), calls=%async_computation.3 | async-start | bytes 16777216 | tf_op jit(solution)/shard_map/all_to_all | solution.py:265
  656.0 167.3 %copy-start.41 = (s32[4,64,8]{1,0,2:T(4,128)S(1)}, s32[4,64,8]{1,0,2:T(4,128)}, u32[]{:S(2)}) copy-start(s32[4,64,8]{1,0,2:T(4,128)} %copy-done.40) | copy-start | bytes 24580
  656.0 167.4 %copy-start.47 = (s32[256,8,1]{0,1,2:T(8,128)S(1)}, s32[256,8,1]{0,1,2:T(8,128)}, u32[]{:S(2)}) copy-start(s32[256,8,1]{0,1,2:T(8,128)} %get-tuple-element.123) | copy-start | bytes 24580
  818.3 187.2 %all-to-all-start.1 = ((bf16[8,4,4,32,1024]{4,3,2,1,0:T(8,128)(2,1)}), bf16[8,4,4,32,1024]{4,3,2,1,0:T(8,128)(2,1)}, u32[]{:S(2)}, u32[]{:S(2)}) async-start(bf16[8,4,4,32,1024]{4,3,2,1,0:T(8,128)(2,1)} %copy.158), calls=%async_computation.1 | async-start | bytes 16777216 | tf_op jit(solution)/shard_map/all_to_all | solution.py:218
  823.3 322.6 %reduce-scatter.7.cloned.1.call-start = ((), (), s32[]{:S(2)}) async-start(), calls=%async_computation.8 | async-start | bytes 2359296
  1020.9 7.1 copy-start.4
  1020.9 7.1 copy-start.38
  1020.9 7.1 copy-start.44
  1020.9 7.1 copy-start.52
  1038.4 6.6 copy-start.36
  1038.4 6.6 copy-start.46
  1045.1 9.3 copy-start.11
  1045.1 9.3 copy-start.12
  1071.1 137.2 %reduce-scatter.9.cloned.1.call-start = ((), (), s32[]{:S(2)}) async-start(), calls=%async_computation.9 | async-start | bytes 2359296
  1103.2 328.6 %all-reduce.10.cloned.1.call-start = ((), (), s32[]{:S(2)}) async-start(), calls=%async_computation.11 | async-start | bytes 25165824 | tf_op jit(solution)/shard_map/psum | solution.py:349
  1125.7 5.4 copy-start.32
  1125.7 5.4 copy-start.34
  1125.7 551.7 %all-reduce.8.cloned.1.call-start = ((), (), s32[]{:S(2)}) async-start(), calls=%async_computation.10 | async-start | bytes 25427968 | tf_op jit(solution)/shard_map/psum | solution.py:344
  1131.1 6.8 copy-start.15
  1139.0 4.1 copy-start.18
  1431.8 6.9 copy-start.20
  1438.7 4.6 copy-start.19
  1443.3 4.5 copy-start.13
  1443.3 4.5 copy-start.16
  1443.3 5.3 copy-start.26
  1677.4 4.9 copy-start.28
  1677.4 6.3 copy-start.27
  (18 other events, 37.1 us)
Sparse Core Ops, SparseCore 0:
  17.3 76.3 all-gather.3
  96.4 71.5 all-gather.5
  1071.2 66.8 reduce-scatter.6
  1141.5 66.7 reduce-scatter.8
  1211.4 220.3 all-reduce.9
  1439.2 238.2 all-reduce.7
where the time goes:
time: 1700 us
  waiting for transfers between devices  1110 us (65%)
  local copies, waits for them, and re-layouts  236 us (14%)
  matrix products  185 us (11%)
  blocking collectives  69.1 us (4%)
  other arithmetic  56 us (3%)
  starting transfers between devices  20.9 us (1%)
    psum x1, waiting for transfers between devices, local(): lax.psum(gate_part.astype(jnp.bfloat16), 'rows').astype(jnp.float32)  211 us
    psum x1, waiting for transfers between devices, local(): lax.psum((first_part, query_part, key_part, value_part, output_part, seco...  183 us
    all_to_all x1, waiting for transfers between devices, local(): lax.all_to_all(grad_received, 'seq', split_axis=0, concat_axis=0, tiled=T...  162 us
    all_to_all x1, waiting for transfers between devices, local(): lax.all_to_all(produced, 'seq', split_axis=0, concat_axis=0, tiled=True)  159 us
    all_to_all x1, waiting for transfers between devices, local(): lax.all_to_all(slot_grad, 'seq', split_axis=0, concat_axis=0, tiled=True)  159 us
    all_to_all x1, waiting for transfers between devices, local(): lax.all_to_all(dispatch, 'seq', split_axis=0, concat_axis=0, tiled=True)  112 us
    unnamed x133, local copies, waits for them, and re-layouts  71.1 us
    all_gather x1, waiting for transfers between devices, local(): lax.all_gather(value_rows, 'seq', axis=1, tiled=True)  60.9 us
  transfers between devices with their start and end apart: 10, of which 9 were waited for; matrix products, arithmetic and copies ran while one was open for 18% of the time, Pallas kernels for 0%

commit v1 on v0

v1 whole, which is shorter than its diff:
```python
import functools
import math

import jax
import jax.numpy as jnp
from jax import lax
from jax.experimental import pallas as pl
from jax.experimental.pallas import tpu as pltpu
from jax.sharding import PartitionSpec as P

HEADS = 16
KV_HEADS = 8
HEAD_DIM = 64
TOPK = 8
MOST = 32
BLOCK = 64
LANES = 128
TILES = KV_HEADS * HEAD_DIM // LANES
PAIR = 2
PAD = 16

EPS = 1e-06
THETA = 10000.0
NEG = -1e30
F32 = jnp.float32
BF16 = jnp.bfloat16
EXACT = lax.Precision.HIGHEST
NN = (((1,), (0,)), ((), ()))
NT = (((1,), (1,)), ((), ()))
TN = (((0,), (0,)), ((), ()))


def mul(left, right, dims=NN, precision=None):
    return lax.dot_general(left, right, dims, precision=precision, preferred_element_type=F32)


def params(megabytes):
    return pltpu.CompilerParams(vmem_limit_bytes=megabytes << 20)


def whole():
    return pl.BlockSpec(memory_space=pltpu.VMEM)


def scalars():
    return pl.BlockSpec(memory_space=pltpu.SMEM)


def struct(shape, dtype):
    return jax.ShapeDtypeStruct(shape, dtype)


def cost(flops, moved):
    return pl.CostEstimate(flops=int(flops), bytes_accessed=int(moved), transcendentals=0)


def low_half(shape):
    return lax.broadcasted_iota(jnp.int32, shape, 1) < HEAD_DIM


def swap_halves(tile):
    lane = lax.broadcasted_iota(jnp.int32, tile.shape, 1)
    quarter = HEAD_DIM // 2
    forward = pltpu.roll(tile, LANES - quarter, 1)
    backward = pltpu.roll(tile, quarter, 1)
    return jnp.where(lane % HEAD_DIM < quarter, forward, backward)


def rotate(tile, cosine, signed_sine):
    return tile * cosine + swap_halves(tile) * signed_sine


def unrotate(tile, cosine, signed_sine):
    return tile * cosine - swap_halves(tile) * signed_sine


def spread_heads(first, second):
    low = low_half(first.shape)
    return jnp.concatenate(
        [
            jnp.where(low, first, 0.0),
            jnp.where(low, pltpu.roll(first, HEAD_DIM, 1), 0.0),
            jnp.where(low, 0.0, pltpu.roll(second, HEAD_DIM, 1)),
            jnp.where(low, 0.0, second),
        ],
        axis=0,
    )


def gather_heads(stacked):
    low = low_half((BLOCK, LANES))
    one, two, three, four = (stacked[i * BLOCK : (i + 1) * BLOCK] for i in range(4))
    first = jnp.where(low, one, pltpu.roll(two, HEAD_DIM, 1))
    second = jnp.where(low, pltpu.roll(three, HEAD_DIM, 1), four)
    return first, second


def allowed_keys(piece, members, member, pos_ref):
    keys = (piece + 1) * members * BLOCK
    start = (piece * members + member) * BLOCK
    place = start + lax.broadcasted_iota(jnp.int32, (BLOCK, keys), 0)
    key = lax.broadcasted_iota(jnp.int32, (BLOCK, keys), 1)
    opening = place - pos_ref[piece * BLOCK : (piece + 1) * BLOCK, :]
    return (key <= place) & (key >= opening)


def probabilities(stacked, key_tile, allowed):
    keys = key_tile.shape[0]
    scores = mul(stacked, key_tile, NT) * HEAD_DIM**-0.5
    scores = scores.reshape(4, BLOCK, keys)
    scores = jnp.where(allowed[None], scores, NEG)
    weights = jnp.exp(scores - jnp.max(scores, axis=-1, keepdims=True))
    probs = weights * (1.0 / jnp.sum(weights, axis=-1, keepdims=True))
    return probs.reshape(4 * BLOCK, keys)


def two_parts(values):
    high = values.astype(BF16).astype(F32)
    return jnp.concatenate([high, values - high], axis=0).astype(BF16)


def front_kernel(
    members,
    me_ref,
    h_ref,
    cos_ref,
    sin_ref,
    pos_ref,
    ids_ref,
    gain_one_ref,
    wq_ref,
    wk_ref,
    wv_ref,
    wo_ref,
    gain_two_ref,
    router_ref,
    mix_ref,
    own_ref,
    qz_ref,
    k_ref,
    v_ref,
    att_ref,
    res_ref,
    xg_ref,
    gates_ref,
):
    member = me_ref[0]
    length, width = h_ref.shape
    tokens = own_ref.shape[0]
    pieces = tokens // BLOCK
    step = 256

    def keys_step(i, carry):
        rows = pl.ds(pl.multiple_of(i * step, step), step)
        x = h_ref[rows, :].astype(F32)
        scale = lax.rsqrt(jnp.mean(x * x, axis=-1, keepdims=True) + EPS)
        mix = (x * scale * gain_one_ref[...]).astype(BF16)
        mix_ref[rows, :] = mix
        v_ref[rows, :] = mul(mix, wv_ref[...]).astype(BF16)
        pre = mul(mix, wk_ref[...])
        cosine, sine = cos_ref[rows, :], sin_ref[rows, :]
        for tile in range(TILES):
            lanes = slice(tile * LANES, (tile + 1) * LANES)
            k_ref[rows, lanes] = rotate(pre[:, lanes], cosine, sine).astype(BF16)
        return carry

    lax.fori_loop(0, length // step, keys_step, 0)
    own = [pl.ds(pl.multiple_of((p * members + member) * BLOCK, BLOCK), BLOCK) for p in range(pieces)]
    for piece in range(pieces):
        own_ref[piece * BLOCK : (piece + 1) * BLOCK, :] = mix_ref[own[piece], :]

    def query_step(tile, carry):
        pre = mul(own_ref[...], wq_ref[:, pl.ds(pl.multiple_of(tile * 256, 256), 256)])
        for piece in range(pieces):
            rows = slice(piece * BLOCK, (piece + 1) * BLOCK)
            cosine, sine = cos_ref[own[piece], :], sin_ref[own[piece], :]
            first = rotate(pre[rows, :LANES], cosine, sine)
            second = rotate(pre[rows, LANES:], cosine, sine)
            qz_ref[piece, tile] = spread_heads(first, second).astype(BF16)
        return carry

    lax.fori_loop(0, TILES, query_step, 0)
    for piece in range(pieces):
        allowed = allowed_keys(piece, members, member, pos_ref)
        keys = allowed.shape[1]
        rows = slice(piece * BLOCK, (piece + 1) * BLOCK)

        def attend(tile, carry):
            lanes = pl.ds(pl.multiple_of(tile * LANES, LANES), LANES)
            probs = probabilities(qz_ref[piece, tile], k_ref[:keys, lanes], allowed)
            first, second = gather_heads(mul(probs.astype(BF16), v_ref[:keys, lanes]))
            at = pl.multiple_of(tile * 256, 256)
            att_ref[rows, pl.ds(at, LANES)] = first.astype(BF16)
            att_ref[rows, pl.ds(at + LANES, LANES)] = second.astype(BF16)
            return carry

        lax.fori_loop(0, TILES, attend, 0)
    mixed = mul(att_ref[...], wo_ref[...])
    for piece in range(pieces):
        rows = slice(piece * BLOCK, (piece + 1) * BLOCK)
        res_ref[rows, :] = h_ref[own[piece], :].astype(F32) + mixed[rows]
    residual = res_ref[...]
    scale = lax.rsqrt(jnp.mean(residual * residual, axis=-1, keepdims=True) + EPS)
    chosen = (residual * scale * gain_two_ref[...]).astype(BF16)
    xg_ref[:tokens, :] = chosen
    logits = mul(router_ref[...], chosen, NT)
    expert = lax.broadcasted_iota(jnp.int32, logits.shape, 0)
    named = expert == ids_ref[0:1, :]
    for k in range(1, TOPK):
        named = named | (expert == ids_ref[k : k + 1, :])
    logits = jnp.where(named, logits, NEG)
    weights = jnp.where(named, jnp.exp(logits - jnp.max(logits, axis=0, keepdims=True)), 0.0)
    gates = weights / jnp.sum(weights, axis=0, keepdims=True)
    gates_ref[...] = gates
    for part in range(logits.shape[0] // 8):
        lanes = slice(part * tokens, (part + 1) * tokens)
        xg_ref[tokens:, lanes] = two_parts(gates[part * 8 : (part + 1) * 8])


def one_hot(slot_row, rows):
    slot = lax.broadcasted_iota(jnp.int32, (rows, slot_row.shape[1]), 0).astype(F32)
    return slot == slot_row


def upstream_kernel(named_ref, u_ref, wd_ref, slot_ref, ug_ref, v_ref):
    experts = wd_ref.shape[0]
    tokens = named_ref.shape[2]
    width = wd_ref.shape[2]
    rows = tokens * MOST // BLOCK
    earlier = lax.broadcasted_iota(jnp.int32, (tokens, tokens), 0)
    later = lax.broadcasted_iota(jnp.int32, (tokens, tokens), 1)
    before = (earlier < later).astype(F32).astype(BF16)
    for c in range(PAIR):
        named = named_ref[c]
        rank = mul(named.astype(BF16), before)
        slot_ref[c] = jnp.where(named > 0, rank, -1.0)

    def expert_step(e, carry):
        at = pl.ds(pl.multiple_of(e * rows, rows), rows)
        both = []
        for c in range(PAIR):
            pick = one_hot(slot_ref[c, pl.ds(e, 1), :], rows).astype(F32).astype(BF16)
            picked = mul(pick, u_ref[:, c, 0].reshape(tokens, width)).astype(BF16)
            ug_ref[c, at, :] = picked
            both.append(picked)
        product = mul(jnp.concatenate(both, axis=0), wd_ref[e], NT)
        for c in range(PAIR):
            v_ref[c, at, :] = product[c * rows : (c + 1) * rows]
        return carry

    lax.fori_loop(0, experts, expert_step, 0)


def expert_kernel(
    me_ref,
    xg_ref,
    slot_ref,
    v_ref,
    wg_ref,
    wu_ref,
    wd_ref,
    dx_ref,
    y_ref,
    xs_ref,
    hs_ref,
    dg_ref,
    du_ref,
    dxs_ref,
    ys_ref,
    pick_ref,
    gates_ref,
    back_ref,
):
    experts = wd_ref.shape[0]
    tokens = slot_ref.shape[2]
    rows = tokens * MOST // BLOCK
    first = me_ref[1] * experts
    back_ref[...] = jnp.zeros_like(back_ref)

    def expert_step(e, carry):
        at = pl.ds(pl.multiple_of(e * rows, rows), rows)
        number = first + e
        row = lax.rem(number, 8)
        lanes = pl.ds(pl.multiple_of(lax.div(number, 8) * tokens, tokens), tokens)
        entering, gate = [], []
        for c in range(PAIR):
            hot = one_hot(slot_ref[c, pl.ds(e, 1), :], rows)
            pick = hot.astype(F32).astype(BF16)
            pick_ref[c, at, :] = pick
            picked = mul(pick, xg_ref[c, :tokens, :]).astype(BF16)
            xs_ref[c, at, :] = picked
            entering.append(picked)
            sent = xg_ref[c, tokens:, lanes].astype(F32)
            gates_ref[...] = sent[:8] + sent[8:]
            gate.append(jnp.sum(jnp.where(hot, gates_ref[pl.ds(row, 1), :], 0.0), axis=1, keepdims=True))
        entering = jnp.concatenate(entering, axis=0)
        gate = jnp.concatenate(gate, axis=0)
        gate_pre = mul(entering, wg_ref[e])
        up_pre = mul(entering, wu_ref[e])
        share = 1.0 / (1.0 + jnp.exp(-gate_pre))
        silu = gate_pre * share
        hidden = silu * up_pre
        product = jnp.concatenate([v_ref[c, at, :] for c in range(PAIR)], axis=0)
        grad_gate = jnp.sum(hidden * product, axis=1, keepdims=True)
        grad_act = gate * product
        grad_gate_pre = (grad_act * up_pre * share * (1.0 + gate_pre * (1.0 - share))).astype(BF16)
        grad_up_pre = (grad_act * silu).astype(BF16)
        gated = (gate * hidden).astype(BF16)
        grad_rows = (mul(grad_gate_pre, wg_ref[e], NT) + mul(grad_up_pre, wu_ref[e], NT)).astype(BF16)
        out_rows = mul(gated, wd_ref[e]).astype(BF16)
        for c in range(PAIR):
            part = slice(c * rows, (c + 1) * rows)
            hs_ref[c, at, :] = gated[part]
            dg_ref[c, at, :] = grad_gate_pre[part]
            du_ref[c, at, :] = grad_up_pre[part]
            dxs_ref[c, at, :] = grad_rows[part]
            ys_ref[c, at, :] = out_rows[part]
            hot = one_hot(slot_ref[c, pl.ds(e, 1), :], rows)
            returned = jnp.sum(jnp.where(hot, grad_gate[part], 0.0), axis=0, keepdims=True)
            high = returned.astype(BF16).astype(F32)
            back_ref[c, pl.ds(row, 1), lanes] = high
            back_ref[c, pl.ds(row + 8, 1), lanes] = returned - high
        return carry

    lax.fori_loop(0, experts, expert_step, 0)
    for c in range(PAIR):
        dx_ref[c, :tokens, :] = mul(pick_ref[c], dxs_ref[c], TN).astype(BF16)
        dx_ref[c, tokens:, :] = back_ref[c].astype(BF16)
        y_ref[c] = mul(pick_ref[c], ys_ref[c], TN).astype(BF16)


def expert_grads_kernel(
    xs_ref, us_ref, hs_ref, dg_ref, du_ref, gate_ref, up_ref, down_ref, gate_acc, up_acc, down_acc
):
    count = pl.num_programs(1)
    group, rows, width = xs_ref.shape
    inner = hs_ref.shape[2]
    flat = lambda ref: ref[...].reshape(group * rows, ref.shape[2])

    @pl.when(pl.program_id(1) == 0)
    def _():
        gate_acc[...] = jnp.zeros_like(gate_acc)
        up_acc[...] = jnp.zeros_like(up_acc)
        down_acc[...] = jnp.zeros_like(down_acc)

    step = 256
    for at in range(0, width, step):
        entering = xs_ref[:, :, at : at + step].reshape(group * rows, step)
        gate_acc[at : at + step, :] += mul(entering, flat(dg_ref), TN)
        up_acc[at : at + step, :] += mul(entering, flat(du_ref), TN)
    for at in range(0, inner, step):
        gated = hs_ref[:, :, at : at + step].reshape(group * rows, step)
        down_acc[at : at + step, :] += mul(gated, flat(us_ref), TN)

    @pl.when(pl.program_id(1) == count - 1)
    def _():
        gate_ref[0] = gate_acc[...].astype(BF16)
        up_ref[0] = up_acc[...].astype(BF16)
        down_ref[0] = down_acc[...].astype(BF16)


def middle_kernel(
    dx_ref,
    u_ref,
    xg_ref,
    res_ref,
    gates_ref,
    gain_two_ref,
    router_ref,
    wo_ref,
    att_ref,
    output_ref,
    vectors_ref,
    gres_ref,
    gaz_ref,
):
    tokens, width = u_ref.shape
    experts = gates_ref.shape[0]
    pieces = tokens // BLOCK
    parts = []
    for part in range(experts // 8):
        sent = dx_ref[tokens:, part * tokens : (part + 1) * tokens].astype(F32)
        parts.append(sent[:8] + sent[8:])
    grad_gates = jnp.concatenate(parts, axis=0)
    gates = gates_ref[...]
    grad_logits = gates * (grad_gates - jnp.sum(gates * grad_gates, axis=0, keepdims=True))
    grad_normed = dx_ref[:tokens, :].astype(F32) + mul(
        grad_logits, router_ref[...].astype(F32), TN, EXACT
    )
    router = mul(grad_logits, xg_ref[:tokens, :].astype(F32), NN, EXACT)
    residual = res_ref[...]
    scale = lax.rsqrt(jnp.mean(residual * residual, axis=-1, keepdims=True) + EPS)
    normed = residual * scale
    second = jnp.sum(grad_normed * normed, axis=0, keepdims=True)
    vectors_ref[...] = jnp.concatenate(
        [router, second, jnp.zeros((vectors_ref.shape[0] - experts - 1, width), F32)], axis=0
    ).astype(BF16)
    scaled = grad_normed * gain_two_ref[...]
    grad_residual = u_ref[...].astype(F32) + scale * (
        scaled - normed * jnp.mean(scaled * normed, axis=-1, keepdims=True)
    )
    gres_ref[...] = grad_residual
    grad_mixed = grad_residual.astype(BF16)
    output_ref[...] = mul(att_ref[...], grad_mixed, TN).astype(BF16)
    for tile in range(TILES):
        grad_att = mul(grad_mixed, wo_ref[tile * 256 : (tile + 1) * 256, :], NT)
        for piece in range(pieces):
            rows = slice(piece * BLOCK, (piece + 1) * BLOCK)
            gaz_ref[piece, tile] = spread_heads(
                grad_att[rows, :LANES], grad_att[rows, LANES:]
            ).astype(BF16)


def attention_back_kernel(
    members,
    me_ref,
    qz_ref,
    gaz_ref,
    k_ref,
    v_ref,
    pos_ref,
    cos_ref,
    sin_ref,
    mix_ref,
    own_ref,
    dq_ref,
    dkv_ref,
    query_ref,
    keyval_ref,
    dk_acc,
    dv_acc,
    row_ref,
):
    member = me_ref[0]
    tokens = own_ref.shape[0]
    pieces = tokens // BLOCK
    length = k_ref.shape[0]
    inner = k_ref.shape[1]
    dk_acc[...] = jnp.zeros_like(dk_acc)
    dv_acc[...] = jnp.zeros_like(dv_acc)
    for piece in range(pieces):
        allowed = allowed_keys(piece, members, member, pos_ref)
        keys = allowed.shape[1]
        rows = slice(piece * BLOCK, (piece + 1) * BLOCK)
        at = pl.ds(pl.multiple_of((piece * members + member) * BLOCK, BLOCK), BLOCK)

        def step(tile, carry):
            lanes = pl.ds(pl.multiple_of(tile * LANES, LANES), LANES)
            stacked, grads = qz_ref[piece, tile], gaz_ref[piece, tile]
            key_tile = k_ref[:keys, lanes]
            probs = probabilities(stacked, key_tile, allowed)
            grad_probs = mul(grads, v_ref[:keys, lanes], NT)
            delta = jnp.sum(probs * grad_probs, axis=-1, keepdims=True)
            grad_scores = (probs * (grad_probs - delta) * HEAD_DIM**-0.5).astype(BF16)
            dk_acc[:keys, lanes] += mul(grad_scores, stacked, TN)
            dv_acc[:keys, lanes] += mul(probs.astype(BF16), grads, TN)
            first, second = gather_heads(mul(grad_scores, key_tile))
            cosine, sine = cos_ref[at, :], sin_ref[at, :]
            out = pl.multiple_of(tile * 256, 256)
            dq_ref[rows, pl.ds(out, LANES)] = unrotate(first, cosine, sine).astype(BF16)
            dq_ref[rows, pl.ds(out + LANES, LANES)] = unrotate(second, cosine, sine).astype(BF16)
            return carry

        lax.fori_loop(0, TILES, step, 0)
    for block in range(length // BLOCK):
        rows = slice(block * BLOCK, (block + 1) * BLOCK)
        cosine, sine = cos_ref[rows, :], sin_ref[rows, :]
        for tile in range(TILES):
            lanes = slice(tile * LANES, (tile + 1) * LANES)
            row_ref[rows, lanes] = unrotate(dk_acc[rows, lanes], cosine, sine).astype(BF16)
        row_ref[rows, inner:] = dv_acc[rows, :].astype(BF16)
        piece, owner = block // members, block % members
        dkv_ref[owner, piece * BLOCK : (piece + 1) * BLOCK, :] = row_ref[rows, :]
    query_ref[...] = mul(own_ref[...], dq_ref[...], TN).astype(BF16)
    keyval_ref[...] = mul(mix_ref[...], row_ref[...], TN).astype(BF16)


def last_kernel(
    members, me_ref, dq_ref, dkv_ref, wq_ref, wk_ref, wv_ref, h_ref, gres_ref, gain_one_ref, gh_ref, first_ref
):
    member = me_ref[0]
    tokens = dq_ref.shape[0]
    inner = wk_ref.shape[1]
    grad_kv = dkv_ref[0].astype(F32)
    for other in range(1, members):
        grad_kv = grad_kv + dkv_ref[other].astype(F32)
    grad_kv = grad_kv.astype(BF16)
    grad_mixer = (
        mul(dq_ref[...], wq_ref[...], NT)
        + mul(grad_kv[:, :inner], wk_ref[...], NT)
        + mul(grad_kv[:, inner:], wv_ref[...], NT)
    )
    x = jnp.concatenate(
        [
            h_ref[pl.ds(pl.multiple_of((p * members + member) * BLOCK, BLOCK), BLOCK), :]
            for p in range(tokens // BLOCK)
        ],
        axis=0,
    ).astype(F32)
    scale = lax.rsqrt(jnp.mean(x * x, axis=-1, keepdims=True) + EPS)
    normed = x * scale
    first_ref[...] = jnp.broadcast_to(
        jnp.sum(grad_mixer * normed, axis=0, keepdims=True), first_ref.shape
    ).astype(first_ref.dtype)
    scaled = grad_mixer * gain_one_ref[...]
    gh_ref[...] = (
        gres_ref[...]
        + scale * (scaled - normed * jnp.mean(scaled * normed, axis=-1, keepdims=True))
    ).astype(gh_ref.dtype)


def rope_tables(places):
    middle = HEAD_DIM // 2
    frequency = jnp.exp(jnp.arange(middle, dtype=F32) * (-2.0 * math.log(THETA) / HEAD_DIM))
    angles = places.astype(F32)[:, None] * frequency
    cosine, sine = jnp.cos(angles), jnp.sin(angles)
    return (
        jnp.concatenate([cosine] * 4, axis=1),
        jnp.concatenate([-sine, sine, -sine, sine], axis=1),
    )


def local(
    hidden_in,
    segment_ids,
    positions,
    expert_ids,
    first_gain,
    query_weight,
    key_weight,
    value_weight,
    output_weight,
    second_gain,
    router_weight,
    gate_weight,
    up_weight,
    down_weight,
    out_grad,
):
    rows_here, block, width = hidden_in.shape
    tokens = rows_here * block
    shards = lax.axis_size("seq")
    members = shards // rows_here
    length = shards * block
    inner = key_weight.shape[1]
    expert_count = router_weight.shape[1]
    experts, _, hidden = gate_weight.shape
    me = lax.axis_index("seq")
    row, member = me // members, me % members
    me_pair = jnp.stack([member, me]).astype(jnp.int32)
    same_member = [[r * members + m for r in range(rows_here)] for m in range(members)]
    same_row = [[r * members + m for m in range(members)] for r in range(rows_here)]
    slots = tokens * MOST // BLOCK
    groups = shards // PAIR

    meta = jnp.concatenate(
        [positions.reshape(1, tokens), expert_ids.reshape(tokens, TOPK).T], axis=0
    )
    meta = lax.all_to_all(
        jnp.broadcast_to(meta[None], (shards,) + meta.shape), "seq", 0, 0, tiled=True
    )
    row_in = lax.all_to_all(jnp.repeat(hidden_in, members, axis=0), "seq", 0, 0, tiled=True)
    row_in = row_in.reshape(length, width)
    upstream = lax.all_gather(out_grad, "seq", axis=0, tiled=False)

    meta = meta.reshape(rows_here, members, TOPK + 1, rows_here, block)
    row_meta = lax.dynamic_index_in_dim(meta, row, 3, keepdims=False)
    own_meta = lax.dynamic_index_in_dim(row_meta, member, 1, keepdims=False)
    cosine, sine = rope_tables(row_meta[:, :, 0].reshape(length))
    own_pos = own_meta[:, 0].reshape(tokens, 1)
    own_ids = own_meta[:, 1:].transpose(1, 0, 2).reshape(TOPK, tokens)
    lane = jnp.arange(8, dtype=jnp.int32)
    wanted = jnp.where(lane < experts, me * experts + lane, -1)
    named = jnp.any(
        meta[:, :, 1:, None] == wanted[None, None, None, :, None, None], axis=2
    )
    named = named.transpose(3, 1, 2, 0, 4).reshape(shards, 8, tokens).astype(F32)

    gain_one, gain_two = first_gain.reshape(1, width), second_gain.reshape(1, width)
    router = router_weight.T
    mix, own_mix, qz, k_row, v_row, att, residual, xg, gates = pl.pallas_call(
        functools.partial(front_kernel, members),
        out_shape=[
            struct((length, width), BF16),
            struct((tokens, width), BF16),
            struct((rows_here, TILES, 4 * BLOCK, LANES), BF16),
            struct((length, inner), BF16),
            struct((length, inner), BF16),
            struct((tokens, width), BF16),
            struct((tokens, width), F32),
            struct((tokens + PAD, width), BF16),
            struct((expert_count, tokens), F32),
        ],
        in_specs=[scalars()] + [whole()] * 12,
        out_specs=[whole()] * 9,
        compiler_params=params(56),
        cost_estimate=cost(5e9, 12e6),
        name="front",
    )(
        me_pair,
        row_in,
        cosine,
        sine,
        own_pos,
        own_ids,
        gain_one,
        query_weight,
        key_weight,
        value_weight,
        output_weight,
        gain_two,
        router,
    )

    constant = lambda shape: pl.BlockSpec(
        shape, lambda i: (0,) * len(shape), pipeline_mode=pl.Buffered(1)
    )
    grouped = lambda *shape: pl.BlockSpec((PAIR,) + shape, lambda i: (i,) + (0,) * len(shape))
    per_row = members // PAIR
    upstream = upstream.reshape(rows_here, members, rows_here, block, width)
    slot, us, product = pl.pallas_call(
        upstream_kernel,
        grid=(groups,),
        out_shape=[
            struct((shards, 8, tokens), F32),
            struct((shards, experts * slots, width), BF16),
            struct((shards, experts * slots, hidden), F32),
        ],
        in_specs=[
            grouped(8, tokens),
            pl.BlockSpec(
                (rows_here, PAIR, 1, block, width),
                lambda i: (0, i % per_row, i // per_row, 0, 0),
            ),
            constant((experts, hidden, width)),
        ],
        out_specs=[
            grouped(8, tokens),
            grouped(experts * slots, width),
            grouped(experts * slots, hidden),
        ],
        compiler_params=params(48),
        cost_estimate=cost(6e9, 20e6),
        name="upstream",
    )(named, upstream, down_weight)

    gathered = lax.all_gather(xg, "seq", axis=0, tiled=False)
    dx, y, xs, hs, dgs, dus = pl.pallas_call(
        expert_kernel,
        grid=(groups,),
        out_shape=[
            struct((shards, tokens + PAD, width), BF16),
            struct((shards, tokens, width), BF16),
            struct((shards, experts * slots, width), BF16),
            struct((shards, experts * slots, hidden), BF16),
            struct((shards, experts * slots, hidden), BF16),
            struct((shards, experts * slots, hidden), BF16),
        ],
        in_specs=[
            scalars(),
            grouped(tokens + PAD, width),
            grouped(8, tokens),
            grouped(experts * slots, hidden),
            constant((experts, width, hidden)),
            constant((experts, width, hidden)),
            constant((experts, hidden, width)),
        ],
        out_specs=[
            grouped(tokens + PAD, width),
            grouped(tokens, width),
            grouped(experts * slots, width),
            grouped(experts * slots, hidden),
            grouped(experts * slots, hidden),
            grouped(experts * slots, hidden),
        ],
        scratch_shapes=[
            pltpu.VMEM((PAIR, experts * slots, width), BF16),
            pltpu.VMEM((PAIR, experts * slots, width), BF16),
            pltpu.VMEM((PAIR, experts * slots, tokens), BF16),
            pltpu.VMEM((8, tokens), F32),
            pltpu.VMEM((PAIR, PAD, width), F32),
        ],
        compiler_params=params(58),
        cost_estimate=cost(30e9, 50e6),
        name="experts",
    )(me_pair, gathered, slot, product, gate_weight, up_weight, down_weight)
    dx_sum = lax.psum_scatter(dx, "seq", scatter_dimension=0, tiled=False)

    step = 8
    one_expert = lambda w: pl.BlockSpec((step, slots, w), lambda e, i: (i, e, 0))
    grad_spec = lambda a, b: pl.BlockSpec((1, a, b), lambda e, i: (e, 0, 0))
    gate_part, up_part, down_part = pl.pallas_call(
        expert_grads_kernel,
        grid=(experts, shards // step),
        out_shape=[
            struct((experts, width, hidden), BF16),
            struct((experts, width, hidden), BF16),
            struct((experts, hidden, width), BF16),
        ],
        in_specs=[
            one_expert(width),
            one_expert(width),
            one_expert(hidden),
            one_expert(hidden),
            one_expert(hidden),
        ],
        out_specs=[grad_spec(width, hidden), grad_spec(width, hidden), grad_spec(hidden, width)],
        scratch_shapes=[
            pltpu.VMEM((width, hidden), F32),
            pltpu.VMEM((width, hidden), F32),
            pltpu.VMEM((hidden, width), F32),
        ],
        compiler_params=params(48),
        cost_estimate=cost(13e9, 45e6),
        name="expert_grads",
    )(xs, us, hs, dgs, dus)
    gate_sum, up_sum, down_sum = lax.psum((gate_part, up_part, down_part), "rows")
    y_sum = lax.psum_scatter(y, "seq", scatter_dimension=0, tiled=False)

    own_upstream = lax.dynamic_index_in_dim(upstream, row, 2, keepdims=False)
    own_upstream = lax.dynamic_index_in_dim(own_upstream, member, 1, keepdims=False)
    own_upstream = own_upstream.reshape(tokens, width)
    output_part, vectors, grad_residual, gaz = pl.pallas_call(
        middle_kernel,
        out_shape=[
            struct((width, width), BF16),
            struct((expert_count + PAD, width), BF16),
            struct((tokens, width), F32),
            struct((rows_here, TILES, 4 * BLOCK, LANES), BF16),
        ],
        in_specs=[whole()] * 9,
        out_specs=[whole()] * 4,
        compiler_params=params(48),
        cost_estimate=cost(2e9, 10e6),
        name="middle",
    )(dx_sum, own_upstream, xg, residual, gates, gain_two, router, output_weight, att)

    dq, dkv, query_part, keyval_part = pl.pallas_call(
        functools.partial(attention_back_kernel, members),
        out_shape=[
            struct((tokens, width), BF16),
            struct((members, tokens, width), BF16),
            struct((width, width), BF16),
            struct((width, width), BF16),
        ],
        in_specs=[scalars()] + [whole()] * 9,
        out_specs=[whole()] * 4,
        scratch_shapes=[
            pltpu.VMEM((length, inner), F32),
            pltpu.VMEM((length, inner), F32),
            pltpu.VMEM((length, width), BF16),
        ],
        compiler_params=params(58),
        cost_estimate=cost(5e9, 12e6),
        name="attention_back",
    )(me_pair, qz, gaz, k_row, v_row, own_pos, cosine, sine, mix, own_mix)
    dkv = lax.all_to_all(dkv, "seq", 0, 0, tiled=True, axis_index_groups=same_row)
    grad_in, first_part = pl.pallas_call(
        functools.partial(last_kernel, members),
        out_shape=[struct((tokens, width), BF16), struct((PAD, width), BF16)],
        in_specs=[scalars()] + [whole()] * 8,
        out_specs=[whole()] * 2,
        compiler_params=params(48),
        cost_estimate=cost(1e9, 8e6),
        name="last",
    )(me_pair, dq, dkv, query_weight, key_weight, value_weight, row_in, grad_residual, gain_one)

    shared = lax.psum((output_part, query_part, keyval_part, vectors, first_part), ("rows", "seq"))
    output_sum, query_sum, keyval_sum, vector_sum, first_sum = (s.astype(F32) for s in shared)
    hidden_out = (residual + y_sum.astype(F32)).astype(BF16)
    back = lambda values: lax.all_to_all(
        values.reshape(rows_here, block, width), "seq", 0, 0, tiled=True, axis_index_groups=same_member
    )
    return (
        back(hidden_out),
        back(grad_in).astype(F32),
        first_sum[0],
        query_sum,
        keyval_sum[:, :inner],
        keyval_sum[:, inner:],
        output_sum,
        vector_sum[expert_count],
        vector_sum[:expert_count].T,
        gate_sum.astype(F32),
        up_sum.astype(F32),
        down_sum.astype(F32),
    )


def solution(mesh):
    placed = (
        P("rows", "seq", None),
        P("rows", "seq"),
        P("rows", "seq"),
        P("rows", "seq", None),
        P(),
        P(),
        P(),
        P(),
        P(),
        P(),
        P(),
        P("seq", None, None),
        P("seq", None, None),
        P("seq", None, None),
        P("rows", "seq", None),
    )
    return jax.shard_map(
        local,
        mesh=mesh,
        in_specs=placed,
        out_specs=(
            P("rows", "seq", None),
            P("rows", "seq", None),
            P(),
            P(),
            P(),
            P(),
            P(),
            P(),
            P(),
            P("seq", None, None),
            P("seq", None, None),
            P("seq", None, None),
        ),
        check_vma=False,
    )
```

time: 1700 us -> 820 us (0.48)
  waiting for transfers between devices: 1110 us -> 547 us
  local copies, waits for them, and re-layouts: 236 us -> 25.5 us
  matrix products: 185 us -> 0 us
  Pallas kernels: 0 us -> 130 us
  other arithmetic: 56 us -> 30.5 us
    all_to_all x4, waiting for transfers between devices: 592 us -> 42.5 us  [the longest x1 34.6 us: local(): lax.all_to_all(jnp.repeat(hidden_in, members, axis=0), 'seq', 0, 0, tiled...]
    dot_general x33 -> x0, matrix products: 185 us -> none  [the longest x1 16.6 us: local(): jnp.einsum('secmd,efd->secmf', arrived, down_weight, preferred_element_ty...]
    pallas_call x0 -> x7, Pallas kernels: none -> 130 us  [the longest x1 45.2 us: local(): pl.pallas_call(expert_kernel, grid=(groups,), out_shape=[struct((shards,...]
    reduce_scatter x0 -> x2, waiting for transfers between devices: none -> 128 us  [the longest x1 67.5 us: local(): dx_sum = lax.psum_scatter(dx, 'seq', scatter_dimension=0, tiled=False)]
    gather x12 -> x0, local copies, waits for them, and re-layouts: 108 us -> none  [the longest x1 23 us: local(): slot_gate = gate_pad[slot_table]]
    psum x2, waiting for transfers between devices: 394 us -> 307 us  [the longest x1 200 us: local(): lax.psum((gate_part, up_part, down_part), 'rows')]
    unnamed x133 -> x50, local copies, waits for them, and re-layouts: 71.1 us -> 14.6 us
    unnamed x8 -> x6, waiting for transfers between devices: 51.3 us -> 1.27 us
  transfers between devices with their start and end apart: 10 -> 10, of which waited for: 9 -> 8; matrix products, arithmetic and copies ran while one was open for 18% -> 4% of each run, Pallas kernels for 0% -> 10%
where the time goes in v1:
time: 820 us; the launch traced here: 819 us
  waiting for transfers between devices  547 us (67%)
  Pallas kernels  130 us (16%)
  blocking collectives  55.9 us (7%)
  other arithmetic  30.5 us (4%)
  local copies, waits for them, and re-layouts  25.5 us (3%)
  starting transfers between devices  15.6 us (2%)
  between operations  14.5 us (2%)
    psum x1, waiting for transfers between devices, local(): lax.psum((gate_part, up_part, down_part), 'rows')  200 us
    psum x1, waiting for transfers between devices, local(): lax.psum((output_part, query_part, keyval_part, vectors, first_part), ('r...  107 us
    reduce_scatter x1, waiting for transfers between devices, local(): dx_sum = lax.psum_scatter(dx, 'seq', scatter_dimension=0, tiled=False)  67.5 us
    reduce_scatter x1, waiting for transfers between devices, local(): y_sum = lax.psum_scatter(y, 'seq', scatter_dimension=0, tiled=False)  60.2 us
    all_gather x1, waiting for transfers between devices, local(): gathered = lax.all_gather(xg, 'seq', axis=0, tiled=False)  59.5 us
    pallas_call x1, Pallas kernels, local(): pl.pallas_call(expert_kernel, grid=(groups,), out_shape=[struct((shards,...  45.2 us
    psum x1, blocking collectives, local(): lax.psum((output_part, query_part, keyval_part, vectors, first_part), ('r...  41.4 us
    all_to_all x1, waiting for transfers between devices, local(): lax.all_to_all(jnp.repeat(hidden_in, members, axis=0), 'seq', 0, 0, tiled...  34.6 us
  transfers between devices with their start and end apart: 10, of which 8 were waited for; matrix products, arithmetic and copies ran while one was open for 4% of the time, Pallas kernels for 10%

profile of v1, /device:TPU:0, one launch (start us, length us, event | category | flops | bytes accessed | tf_op | source)
XLA Modules:
  0.0 819.1 jit_solution(3501808859101183676)
XLA Ops:
  7.9 0.8 reshape.92
  8.7 0.7 copy.44
  9.5 14.5 %all_to_all.25 = s32[8,9,256]{2,1,0:T(8,128)S(1)} all-to-all(s32[8,9,256]{2,1,0:T(8,128)S(1)} %broadcast_in_dim.9), channel_id=1, replica_groups=mesh['rows'=4,'seq'=8] {'seq'}, dimensions={0} | all-to-all | bytes 147456 | tf_op jit(solution)/shard_map/all_to_all | solution.py:559
  24.0 2.1 broadcast_in_dim.7
  26.2 3.6 all-to-all-start
  31.4 0.8 reshape_squeeze.5.pos_ref
  32.2 1.0 fusion.1
  33.2 1.3 pad_maximum_fusion
  34.5 34.6 %all-to-all-done = bf16[8,64,1024]{2,1,0:T(8,128)(2,1)S(1)} async-done(((bf16[8,64,1024]{2,1,0:T(8,128)(2,1)}), bf16[8,64,1024]{2,1,0:T(8,128)(2,1)S(1)}, u32[]{:S(2)}, u32[]{:S(2)}) %all-to-all-start) | async-done | bytes 1048608 | tf_op jit(solution)/shard_map/all_to_all | solution.py:562
  69.1 1.0 copy-done.1
  70.1 19.5 %front.1 = (bf16[512,1024]{1,0:T(8,128)(2,1)}, bf16[256,1024]{1,0:T(8,128)(2,1)}, bf16[4,4,256,128]{3,2,1,0:T(8,128)(2,1)}, bf16[512,512]{1,0:T(8,128)(2,1)}, bf...) custom-call(s32[2]{0:T(128)} %pad_add_fusion.1.me_ref, ...), custom_call_target="tpu_custom_call" | custom-call | flops 5000000000 | bytes 12000000 | tf_op jit(solution)/shard_map/front/pallas_call | solution.py:581
  90.2 9.4 %all-gather.7.cloned.1.call-done = bf16[32,64,1024]{2,1,0:T(8,128)(2,1)} async-done(((bf16[4,64,1024]{2,1,0:T(8,128)(2,1)}), bf16[32,64,1024]{2,1,0:T(8,128)(2,1)}) %all-gather.7.cloned.1.call-update) | async-done | bytes 4194320 | tf_op jit(solution)/shard_map/all_gather | solution.py:564
  99.6 2.2 copy-done.10
  101.8 15.4 %upstream.1 = (f32[8,8,256]{2,1,0:T(8,128)S(1)}, bf16[8,512,1024]{2,1,0:T(8,128)(2,1)}, f32[8,512,512]{2,1,0:T(8,128)}) custom-call(f32[8,8,256]{2,1,0:T(8,128)S(1)} %reshape.102.named_ref, bf16[4,2,4,64,1024]{4,3,2,1,0:T(8,128)(2,1)S(1)} %bitcast.40, bf16[4,512,1024]{2,1,0:T(8,128)(2,1)} %wd_ref.3), custom_call_target="tpu_custom_call" | custom-call | flops 6000000000 | bytes 20000000 | tf_op jit(solution)/shard_map/upstream/pallas_call | solution.py:621
  117.8 59.5 %all-gather.5.cloned.1.call-done = bf16[2176,1024]{1,0:T(8,128)(2,1)} async-done(((bf16[272,1024]{1,0:T(8,128)(2,1)}), bf16[2176,1024]{1,0:T(8,128)(2,1)}) %all-gather.5.cloned.1.call-update) | async-done | bytes 4456464 | tf_op jit(solution)/shard_map/all_gather | solution.py:647
  177.3 45.2 %experts.1 = (bf16[8,272,1024]{2,1,0:T(8,128)(2,1)}, bf16[8,256,1024]{2,1,0:T(8,128)(2,1)}, bf16[8,512,1024]{2,1,0:T(8,128)(2,1)}, bf16[8,512,512]{2,1,0:T(8,128...) custom-call(s32[2]{0:T(128)} %pad_add_fusion.1.me_ref, bf16[8,272,1024]{2,1,0:T(8,128)(2,1)} %bitcast.55, ...), custom_call_target="tpu_custom_call" | custom-call | flops 30000001024 | bytes 50000000 | tf_op jit(solution)/shard_map/experts/pallas_call | solution.py:648
  223.4 18.3 %expert_grads.1 = (bf16[4,1024,512]{2,1,0:T(8,128)(2,1)S(1)}, bf16[4,1024,512]{2,1,0:T(8,128)(2,1)}, bf16[4,512,1024]{2,1,0:T(8,128)(2,1)}) custom-call(bf16[8,512,1024]{2,1,0:T(8,128)(2,1)} %get-tuple-element.66.xs_ref, bf16[8,512,1024]{2,1,0:T(8,128)(2,1)} %get-tuple-element.67.us_ref, bf16[8,512,512]{2,1,0:T(8,128)(2,1)} %get-tuple-element.68.hs_ref, ...), custom_call_target="tpu_custom_call" | custom-call | flops 12999999488 | bytes 45000000 | tf_op jit(solution)/shard_map/expert_grads/pallas_call | solution.py:692
  241.7 2.0 copy-done
  243.8 1.2 constant_dynamic-slice_fusion
  245.1 67.5 %reduce-scatter.5.cloned.1.call-done = bf16[1,272,1024]{2,1,0:T(8,128)(2,1)} async-done(((bf16[8,272,1024]{2,1,0:T(8,128)(2,1)}), bf16[1,272,1024]{2,1,0:T(8,128)(2,1)}) %reduce-scatter.5.cloned.1.call-update) | async-done | bytes 557072 | tf_op jit(solution)/shard_map/reduce_scatter | solution.py:687
  312.6 1.0 copy-done.13
  313.7 5.8 middle.1
  319.5 1.0 copy-done.5
  320.6 1.0 copy-done.16
  321.5 21.6 %attention_back.1 = (bf16[256,1024]{1,0:T(8,128)(2,1)}, bf16[2,256,1024]{2,1,0:T(8,128)(2,1)}, bf16[1024,1024]{1,0:T(8,128)(2,1)}, bf16[1024,1024]{1,0:T(8,128)(2,1)}) custom-call(s32[2]{0:T(128)} %pad_add_fusion.1.me_ref, bf16[4,4,256,128]{3,2,1,0:T(8,128)(2,1)} %get-tuple-element.48.qz_ref, bf16[4,4,256,128]{3,2,1,0:T(8,128)(2,1)} %copy-done.16, ...), custom_call_target="tpu_custom_call" | custom-call | flops 5000000000 | bytes 12000000 | tf_op jit(solution)/shard_map/attention_back/pallas_call | solution.py:738
  343.2 3.7 all-to-all-start.3
  346.9 60.2 %reduce-scatter.3.cloned.1.call-done = bf16[1,256,1024]{2,1,0:T(8,128)(2,1)} async-done(((bf16[8,256,1024]{2,1,0:T(8,128)(2,1)}), bf16[1,256,1024]{2,1,0:T(8,128)(2,1)}) %reduce-scatter.3.cloned.1.call-update) | async-done | bytes 524304 | tf_op jit(solution)/shard_map/reduce_scatter | solution.py:718
  407.1 2.3 fusion
  409.4 4.2 all-to-all-start.2
  413.6 1.2 copy-done.4
  414.8 1.1 copy-done.8
  415.9 3.8 last.1
  419.7 0.8 copy-done.9
  420.5 7.9 all-to-all-done.2
  428.4 3.7 all-to-all-start.4
  432.1 199.9 %all-reduce.7.cloned.1.call-done = (bf16[4,1024,512]{2,1,0:T(8,128)(2,1)}, bf16[4,1024,512]{2,1,0:T(8,128)(2,1)}, bf16[4,512,1024]{2,1,0:T(8,128)(2,1)}) async-done(((bf16[4,1024,512]{2,1,0:T(8,128)(2,1)}, bf16[4,1024,512]{2,1,0:T(8,128)(2,1)}, bf16[4,512,1024]{2,1,0:T(8,128)(2,1)}), (bf16[4,1024,512]{2,1,0:T(8,128)(2,1)}, bf16[4,1024,512]{2,1,0:T(8,128)(2,1)}, ...) | async-done | bytes 12582928 | tf_op jit(solution)/shard_map/psum | solution.py:717
  632.0 6.9 convert_element_type.64
  638.9 4.6 convert_element_type.65
  643.5 4.4 convert_element_type.66
  647.9 41.4 %psum.56 = bf16[16,1024]{1,0:T(8,128)(2,1)S(1)} all-reduce(bf16[16,1024]{1,0:T(8,128)(2,1)S(1)} %get-tuple-element.61), channel_id=1, replica_groups=mesh['rows'=4,'seq'=8] {'rows','seq'}, use_global_device_ids=true, to_apply=%region_3.4 | all-reduce | flops 16384 | bytes 65536 | tf_op jit(solution)/shard_map/psum | solution.py:768
  689.9 1.1 convert_element_type.59
  691.0 107.3 %all-reduce.5.cloned.1.call-done = (bf16[1024,1024]{1,0:T(8,128)(2,1)}, bf16[1024,1024]{1,0:T(8,128)(2,1)}, bf16[1024,1024]{1,0:T(8,128)(2,1)}, bf16[48,1024]{1,0:T(8,128)(2,1)}) async-done(((bf16[1024,1024]{1,0:T(8,128)(2,1)}, bf16[1024,1024]{1,0:T(8,128)(2,1)}, bf16[1024,1024]{1,0:T(8,128)(2,1)}, bf16[48,1024]{1,0:T(8,128)(2,1)}), (bf16[1024,1024]{1,0:T(8,128)(2,1)}, bf16[1024,1024]{1,0:T(8,128)(2,1)}, ...) | async-done | bytes 6389776 | tf_op jit(solution)/shard_map/psum | solution.py:768
  798.2 1.5 slice.44
  799.7 0.9 convert_element_type.63
  801.3 4.1 convert_element_type.60
  805.4 2.5 convert_element_type.62
  807.8 2.6 fusion.2
  810.4 1.9 copy.61
  (74 shorter events, 5.8 us)
Async XLA Ops:
  7.2 92.4 %all-gather.7.cloned.1.call-start = ((), (), s32[]{:S(2)}) async-start(), calls=%async_computation.10 | async-start | bytes 4718592 | tf_op jit(solution)/shard_map/all_gather | solution.py:564
  26.2 43.0 %all-to-all-start = ((bf16[8,64,1024]{2,1,0:T(8,128)(2,1)}), bf16[8,64,1024]{2,1,0:T(8,128)(2,1)S(1)}, u32[]{:S(2)}, u32[]{:S(2)}) async-start(bf16[8,64,1024]{2,1,0:T(8,128)(2,1)} %bitcast.2), calls=%async_computation | async-start | bytes 2097152 | tf_op jit(solution)/shard_map/all_to_all | solution.py:562
  29.7 147.6 %all-gather.5.cloned.1.call-start = ((), (), s32[]{:S(2)}) async-start(), calls=%async_computation.9 | async-start | bytes 5013504 | tf_op jit(solution)/shard_map/all_gather | solution.py:647
  69.1 1.0 copy-start.1
  89.7 222.9 %reduce-scatter.5.cloned.1.call-start = ((), (), s32[]{:S(2)}) async-start(), calls=%async_computation.8 | async-start | bytes 5013504 | tf_op jit(solution)/shard_map/reduce_scatter | solution.py:687
  99.6 2.2 copy-start.10
  117.2 0.6 copy-start.19
  222.6 184.5 %reduce-scatter.3.cloned.1.call-start = ((), (), s32[]{:S(2)}) async-start(), calls=%async_computation.7 | async-start | bytes 4718592 | tf_op jit(solution)/shard_map/reduce_scatter | solution.py:718
  223.2 408.8 %all-reduce.7.cloned.1.call-start = ((), (), s32[]{:S(2)}) async-start(), calls=%async_computation.12 | async-start | bytes 25165824 | tf_op jit(solution)/shard_map/psum | solution.py:717
  241.7 2.0 copy-start
  243.7 68.9 %copy-start.6 = (f32[256,1024]{1,0:T(8,128)S(1)}, f32[256,1024]{1,0:T(8,128)}, u32[]{:S(2)}) copy-start(f32[256,1024]{1,0:T(8,128)} %get-tuple-element.43.res_ref) | copy-start | bytes 3145732
  243.7 68.9 %copy-start.7 = (bf16[272,1024]{1,0:T(8,128)(2,1)S(1)}, bf16[272,1024]{1,0:T(8,128)(2,1)}, u32[]{:S(2)}) copy-start(bf16[272,1024]{1,0:T(8,128)(2,1)} %get-tuple-element.44.xg_ref) | copy-start | bytes 1671172
  243.7 68.9 %copy-start.14 = (bf16[1024,32]{0,1:T(8,128)(2,1)S(1)}, bf16[1024,32]{0,1:T(8,128)(2,1)}, u32[]{:S(2)}) copy-start(bf16[1024,32]{0,1:T(8,128)(2,1)} %param.24) | copy-start | bytes 196612
  243.7 68.9 %copy-start.15 = (f32[1024]{0:T(1024)S(1)}, f32[1024]{0:T(1024)}, u32[]{:S(2)}) copy-start(f32[1024]{0:T(1024)} %param.23) | copy-start | bytes 12292
  243.7 68.9 %copy-start.17 = (bf16[256,1024]{1,0:T(8,128)(2,1)S(1)}, bf16[256,1024]{1,0:T(8,128)(2,1)}, u32[]{:S(2)}) copy-start(bf16[256,1024]{1,0:T(8,128)(2,1)} %get-tuple-element.51.att_ref) | copy-start | bytes 1572868
  243.7 68.9 %copy-start.18 = (f32[32,256]{1,0:T(8,128)S(1)}, f32[32,256]{1,0:T(8,128)}, u32[]{:S(2)}) copy-start(f32[32,256]{1,0:T(8,128)} %get-tuple-element.50.gates_ref) | copy-start | bytes 98308
  243.8 554.5 %all-reduce.5.cloned.1.call-start = ((), (), s32[]{:S(2)}) async-start(), calls=%async_computation.11 | async-start | bytes 12779520 | tf_op jit(solution)/shard_map/psum | solution.py:768
  312.6 1.1 copy-start.13
  319.5 1.0 copy-start.5
  320.6 1.0 copy-start.16
  343.1 70.4 %copy-start.2 = (bf16[8,64,1024]{2,1,0:T(8,128)(2,1)S(1)}, bf16[8,64,1024]{2,1,0:T(8,128)(2,1)}, u32[]{:S(2)}) copy-start(bf16[8,64,1024]{2,1,0:T(8,128)(2,1)} %copy-done.1) | copy-start | bytes 3145732
  343.1 70.4 %copy-start.3 = (bf16[1024,512]{1,0:T(8,128)(2,1)S(1)}, bf16[1024,512]{1,0:T(8,128)(2,1)}, u32[]{:S(2)}) copy-start(bf16[1024,512]{1,0:T(8,128)(2,1)} %wk_ref.3) | copy-start | bytes 3145732
  343.1 70.4 %copy-start.11 = (f32[1024]{0:T(1024)S(1)}, f32[1024]{0:T(1024)}, u32[]{:S(2)}) copy-start(f32[1024]{0:T(1024)} %param.18) | copy-start | bytes 12292
  343.2 70.4 %copy-start.12 = (s32[2]{0:T(128)S(1)}, s32[2]{0:T(128)}, u32[]{:S(2)}) copy-start(s32[2]{0:T(128)} %pad_add_fusion.1.me_ref) | copy-start | bytes 28
  343.2 66.2 %all-to-all-start.3 = ((bf16[2,256,1024]{2,1,0:T(8,128)(2,1)}), bf16[2,256,1024]{2,1,0:T(8,128)(2,1)S(1)}, u32[]{:S(2)}, u32[]{:S(2)}) async-start(bf16[2,256,1024]{2,1,0:T(8,128)(2,1)} %get-tuple-element.58), calls=%async_computation.5 | async-start | bytes 2097152 | tf_op jit(solution)/shard_map/all_to_all | solution.py:757
  409.4 19.0 %all-to-all-start.2 = ((bf16[4,64,1024]{2,1,0:T(8,128)(2,1)}), bf16[4,64,1024]{2,1,0:T(8,128)(2,1)}, u32[]{:S(2)}, u32[]{:S(2)}) async-start(bf16[4,64,1024]{2,1,0:T(8,128)(2,1)} %bitcast.48), calls=%async_computation.3 | async-start | bytes 1048576 | tf_op jit(solution)/shard_map/all_to_all | solution.py:771
  413.6 1.2 copy-start.4
  414.8 1.1 copy-start.8
  419.7 0.8 copy-start.9
  428.4 261.5 %all-to-all-start.4 = ((bf16[4,64,1024]{2,1,0:T(8,128)(2,1)}), bf16[4,64,1024]{2,1,0:T(8,128)(2,1)S(1)}, u32[]{:S(2)}, u32[]{:S(2)}) async-start(bf16[4,64,1024]{2,1,0:T(8,128)(2,1)} %bitcast.38), calls=%async_computation.6 | async-start | bytes 1048576 | tf_op jit(solution)/shard_map/all_to_all | solution.py:771
  632.0 6.9 copy-start.22
  638.9 4.6 copy-start.21
  798.2 7.1 copy-start.23
  805.4 2.5 copy-start.20
Sparse Core Ops, SparseCore 0:
  10.1 89.3 all-gather.6
  102.3 74.9 all-gather.4
  222.7 89.8 reduce-scatter.4
  317.1 89.9 reduce-scatter.2
  410.8 221.1 all-reduce.6
  638.6 159.5 all-reduce.4

commit v2 on v1

--- a/solution.py
+++ b/solution.py
@@ -16,6 +16,7 @@
 BLOCK = 64
 LANES = 128
 TILES = KV_HEADS * HEAD_DIM // LANES
+EXTRA = 128
 PAIR = 2
 PAD = 16
 
@@ -50,8 +51,8 @@
     return jax.ShapeDtypeStruct(shape, dtype)
 
 
-def cost(flops, moved):
-    return pl.CostEstimate(flops=int(flops), bytes_accessed=int(moved), transcendentals=0)
+def took(microseconds):
+    return pl.CostEstimate(flops=int(microseconds * 0.5e9), bytes_accessed=0, transcendentals=0)
 
 
 def low_half(shape):
@@ -121,8 +122,17 @@
 
 def front_kernel(
     members,
+    blocks,
     me_ref,
-    h_ref,
+    *refs,
+):
+    front_body(members, me_ref, refs[:blocks], *refs[blocks:])
+
+
+def front_body(
+    members,
+    me_ref,
+    block_refs,
     cos_ref,
     sin_ref,
     pos_ref,
@@ -143,12 +153,16 @@
     res_ref,
     xg_ref,
     gates_ref,
+    input_ref,
+    h_ref,
 ):
     member = me_ref[0]
     length, width = h_ref.shape
     tokens = own_ref.shape[0]
     pieces = tokens // BLOCK
     step = 256
+    for i, block_ref in enumerate(block_refs):
+        h_ref[pl.ds(pl.multiple_of(me_ref[2 + i] * BLOCK, BLOCK), BLOCK), :] = block_ref[...]
 
     def keys_step(i, carry):
         rows = pl.ds(pl.multiple_of(i * step, step), step)
@@ -167,7 +181,9 @@
     lax.fori_loop(0, length // step, keys_step, 0)
     own = [pl.ds(pl.multiple_of((p * members + member) * BLOCK, BLOCK), BLOCK) for p in range(pieces)]
     for piece in range(pieces):
-        own_ref[piece * BLOCK : (piece + 1) * BLOCK, :] = mix_ref[own[piece], :]
+        rows = slice(piece * BLOCK, (piece + 1) * BLOCK)
+        own_ref[rows, :] = mix_ref[own[piece], :]
+        input_ref[rows, :] = h_ref[own[piece], :]
 
     def query_step(tile, carry):
         pre = mul(own_ref[...], wq_ref[:, pl.ds(pl.multiple_of(tile * 256, 256), 256)])
@@ -196,10 +212,8 @@
 
         lax.fori_loop(0, TILES, attend, 0)
     mixed = mul(att_ref[...], wo_ref[...])
-    for piece in range(pieces):
-        rows = slice(piece * BLOCK, (piece + 1) * BLOCK)
-        res_ref[rows, :] = h_ref[own[piece], :].astype(F32) + mixed[rows]
-    residual = res_ref[...]
+    residual = input_ref[...].astype(F32) + mixed
+    res_ref[...] = residual
     scale = lax.rsqrt(jnp.mean(residual * residual, axis=-1, keepdims=True) + EPS)
     chosen = (residual * scale * gain_two_ref[...]).astype(BF16)
     xg_ref[:tokens, :] = chosen
@@ -222,7 +236,7 @@
     return slot == slot_row
 
 
-def upstream_kernel(named_ref, u_ref, wd_ref, slot_ref, ug_ref, v_ref):
+def upstream_kernel(named_ref, u_ref, wd_ref, tied_ref, slot_ref, ug_ref, v_ref):
     experts = wd_ref.shape[0]
     tokens = named_ref.shape[2]
     width = wd_ref.shape[2]
@@ -252,111 +266,140 @@
 
 
 def expert_kernel(
-    me_ref,
-    xg_ref,
+    kept,
+    info_ref,
+    xa_ref,
+    xb_ref,
     slot_ref,
     v_ref,
     wg_ref,
     wu_ref,
     wd_ref,
-    dx_ref,
-    y_ref,
-    xs_ref,
-    hs_ref,
-    dg_ref,
-    du_ref,
-    dxs_ref,
-    ys_ref,
-    pick_ref,
-    gates_ref,
-    back_ref,
+    *rest,
 ):
-    experts = wd_ref.shape[0]
+    (dxa_ref, dxb_ref, ya_ref, yb_ref, xs_ref, hs_ref, dg_ref, du_ref) = rest[kept : kept + 8]
+    (dxs_ref, ys_ref, pick_ref, gates_ref, back_ref) = rest[kept + 8 :]
+    e = pl.program_id(0)
+    experts = pl.num_programs(0)
     tokens = slot_ref.shape[2]
     rows = tokens * MOST // BLOCK
-    first = me_ref[1] * experts
-    back_ref[...] = jnp.zeros_like(back_ref)
-
-    def expert_step(e, carry):
-        at = pl.ds(pl.multiple_of(e * rows, rows), rows)
-        number = first + e
-        row = lax.rem(number, 8)
-        lanes = pl.ds(pl.multiple_of(lax.div(number, 8) * tokens, tokens), tokens)
-        entering, gate = [], []
-        for c in range(PAIR):
-            hot = one_hot(slot_ref[c, pl.ds(e, 1), :], rows)
-            pick = hot.astype(F32).astype(BF16)
-            pick_ref[c, at, :] = pick
-            picked = mul(pick, xg_ref[c, :tokens, :]).astype(BF16)
-            xs_ref[c, at, :] = picked
-            entering.append(picked)
-            sent = xg_ref[c, tokens:, lanes].astype(F32)
-            gates_ref[...] = sent[:8] + sent[8:]
-            gate.append(jnp.sum(jnp.where(hot, gates_ref[pl.ds(row, 1), :], 0.0), axis=1, keepdims=True))
-        entering = jnp.concatenate(entering, axis=0)
-        gate = jnp.concatenate(gate, axis=0)
-        gate_pre = mul(entering, wg_ref[e])
-        up_pre = mul(entering, wu_ref[e])
-        share = 1.0 / (1.0 + jnp.exp(-gate_pre))
-        silu = gate_pre * share
-        hidden = silu * up_pre
-        product = jnp.concatenate([v_ref[c, at, :] for c in range(PAIR)], axis=0)
-        grad_gate = jnp.sum(hidden * product, axis=1, keepdims=True)
-        grad_act = gate * product
-        grad_gate_pre = (grad_act * up_pre * share * (1.0 + gate_pre * (1.0 - share))).astype(BF16)
-        grad_up_pre = (grad_act * silu).astype(BF16)
-        gated = (gate * hidden).astype(BF16)
-        grad_rows = (mul(grad_gate_pre, wg_ref[e], NT) + mul(grad_up_pre, wu_ref[e], NT)).astype(BF16)
-        out_rows = mul(gated, wd_ref[e]).astype(BF16)
-        for c in range(PAIR):
-            part = slice(c * rows, (c + 1) * rows)
-            hs_ref[c, at, :] = gated[part]
-            dg_ref[c, at, :] = grad_gate_pre[part]
-            du_ref[c, at, :] = grad_up_pre[part]
-            dxs_ref[c, at, :] = grad_rows[part]
-            ys_ref[c, at, :] = out_rows[part]
-            hot = one_hot(slot_ref[c, pl.ds(e, 1), :], rows)
-            returned = jnp.sum(jnp.where(hot, grad_gate[part], 0.0), axis=0, keepdims=True)
-            high = returned.astype(BF16).astype(F32)
-            back_ref[c, pl.ds(row, 1), lanes] = high
-            back_ref[c, pl.ds(row + 8, 1), lanes] = returned - high
-        return carry
-
-    lax.fori_loop(0, experts, expert_step, 0)
+    places = [(info_ref[0] + c) % PAIR for c in range(PAIR)]
+    sources = (xa_ref, xb_ref)
+
+    @pl.when(e == 0)
+    def _():
+        back_ref[...] = jnp.zeros_like(back_ref)
+
+    at = pl.ds(pl.multiple_of(e * rows, rows), rows)
+    number = info_ref[1] * experts + e
+    row = lax.rem(number, 8)
+    lanes = pl.ds(pl.multiple_of(lax.div(number, 8) * tokens, tokens), tokens)
+    entering, gate = [], []
     for c in range(PAIR):
-        dx_ref[c, :tokens, :] = mul(pick_ref[c], dxs_ref[c], TN).astype(BF16)
-        dx_ref[c, tokens:, :] = back_ref[c].astype(BF16)
-        y_ref[c] = mul(pick_ref[c], ys_ref[c], TN).astype(BF16)
+        hot = one_hot(slot_ref[places[c], pl.ds(e, 1), :], rows)
+        pick = hot.astype(F32).astype(BF16)
+        pick_ref[c, at, :] = pick
+        picked = mul(pick, sources[c][:tokens, :]).astype(BF16)
+        xs_ref[places[c]] = picked
+        entering.append(picked)
+        sent = sources[c][tokens:, lanes].astype(F32)
+        gates_ref[...] = sent[:8] + sent[8:]
+        gate.append(jnp.sum(jnp.where(hot, gates_ref[pl.ds(row, 1), :], 0.0), axis=1, keepdims=True))
+    entering = jnp.concatenate(entering, axis=0)
+    gate = jnp.concatenate(gate, axis=0)
+    gate_pre = mul(entering, wg_ref[0])
+    up_pre = mul(entering, wu_ref[0])
+    share = 1.0 / (1.0 + jnp.exp(-gate_pre))
+    silu = gate_pre * share
+    hidden = silu * up_pre
+    product = jnp.concatenate([v_ref[places[c]] for c in range(PAIR)], axis=0)
+    grad_gate = jnp.sum(hidden * product, axis=1, keepdims=True)
+    grad_act = gate * product
+    grad_gate_pre = (grad_act * up_pre * share * (1.0 + gate_pre * (1.0 - share))).astype(BF16)
+    grad_up_pre = (grad_act * silu).astype(BF16)
+    gated = (gate * hidden).astype(BF16)
+    grad_rows = (mul(grad_gate_pre, wg_ref[0], NT) + mul(grad_up_pre, wu_ref[0], NT)).astype(BF16)
+    out_rows = mul(gated, wd_ref[0]).astype(BF16)
+    for c in range(PAIR):
+        part = slice(c * rows, (c + 1) * rows)
+        hs_ref[places[c]] = gated[part]
+        dg_ref[places[c]] = grad_gate_pre[part]
+        du_ref[places[c]] = grad_up_pre[part]
+        dxs_ref[c, at, :] = grad_rows[part]
+        ys_ref[c, at, :] = out_rows[part]
+        hot = one_hot(slot_ref[places[c], pl.ds(e, 1), :], rows)
+        returned = jnp.sum(jnp.where(hot, grad_gate[part], 0.0), axis=0, keepdims=True)
+        high = returned.astype(BF16).astype(F32)
+        back_ref[c, pl.ds(row, 1), lanes] = high
+        back_ref[c, pl.ds(row + 8, 1), lanes] = returned - high
+
+    @pl.when(e == experts - 1)
+    def _():
+        for c, (dx_ref, y_ref) in enumerate(((dxa_ref, ya_ref), (dxb_ref, yb_ref))):
+            dx_ref[:tokens, :] = mul(pick_ref[c], dxs_ref[c], TN).astype(BF16)
+            dx_ref[tokens:, :] = back_ref[c].astype(BF16)
+            y_ref[...] = mul(pick_ref[c], ys_ref[c], TN).astype(BF16)
 
 
 def expert_grads_kernel(
-    xs_ref, us_ref, hs_ref, dg_ref, du_ref, gate_ref, up_ref, down_ref, gate_acc, up_acc, down_acc
+    info_ref, xs_ref, us_ref, hs_ref, dg_ref, du_ref, earlier_ref, tied_ref, sent_ref, keep_ref, send_ref
 ):
-    count = pl.num_programs(1)
+    core = info_ref[3]
     group, rows, width = xs_ref.shape
     inner = hs_ref.shape[2]
     flat = lambda ref: ref[...].reshape(group * rows, ref.shape[2])
 
-    @pl.when(pl.program_id(1) == 0)
-    def _():
-        gate_acc[...] = jnp.zeros_like(gate_acc)
-        up_acc[...] = jnp.zeros_like(up_acc)
-        down_acc[...] = jnp.zeros_like(down_acc)
-
-    step = 256
-    for at in range(0, width, step):
-        entering = xs_ref[:, :, at : at + step].reshape(group * rows, step)
-        gate_acc[at : at + step, :] += mul(entering, flat(dg_ref), TN)
-        up_acc[at : at + step, :] += mul(entering, flat(du_ref), TN)
-    for at in range(0, inner, step):
-        gated = hs_ref[:, :, at : at + step].reshape(group * rows, step)
-        down_acc[at : at + step, :] += mul(gated, flat(us_ref), TN)
-
-    @pl.when(pl.program_id(1) == count - 1)
-    def _():
-        gate_ref[0] = gate_acc[...].astype(BF16)
-        up_ref[0] = up_acc[...].astype(BF16)
-        down_ref[0] = down_acc[...].astype(BF16)
+    for half, out_ref in ((core, keep_ref), (1 - core, send_ref)):
+        step = min(256, width // 2)
+        for at in range(0, width // 2, step):
+            lanes = pl.ds(pl.multiple_of(half * (width // 2) + at, LANES), step)
+            entering = xs_ref[:, :, lanes].reshape(group * rows, step)
+            out_ref[0, 0, at : at + step, :] = mul(entering, flat(dg_ref), TN).astype(BF16)
+            out_ref[0, 1, at : at + step, :] = mul(entering, flat(du_ref), TN).astype(BF16)
+        step = inner // 2
+        lanes = pl.ds(pl.multiple_of(half * step, LANES), step)
+        gated = hs_ref[:, :, lanes].reshape(group * rows, step)
+        product = mul(gated, flat(us_ref), TN).astype(BF16)
+        out_ref[0, 2, :step, :] = product[:, :inner]
+        out_ref[0, 2, step:, :] = product[:, inner:]
+
+
+def finish_kernel(kept, info_ref, mine_ref, other_ref, *rest):
+    gate_ref, up_ref, down_ref = rest[kept:]
+    core = info_ref[3]
+    half = mine_ref.shape[1]
+    inner = mine_ref.shape[2]
+    for source, place in ((mine_ref, core), (other_ref, 1 - core)):
+        rows = pl.ds(pl.multiple_of(place * half, half), half)
+        gate_ref[0, rows, :] = source[0].astype(F32)
+        up_ref[0, rows, :] = source[1].astype(F32)
+        rows = pl.ds(pl.multiple_of(place * (half // 2), half // 2), half // 2)
+        down_ref[0, rows, :inner] = source[2, : half // 2].astype(F32)
+        down_ref[0, rows, inner:] = source[2, half // 2 :].astype(F32)
+
+
+def add(*terms):
+    return sum(term.astype(F32) for term in terms).astype(terms[0].dtype)
+
+
+def after(values, *others):
+    anywhere = pl.BlockSpec(memory_space=pl.ANY)
+    return pl.pallas_call(
+        lambda *refs: None,
+        out_shape=[struct(v.shape, v.dtype) for v in values],
+        in_specs=[anywhere] * (len(values) + len(others)),
+        out_specs=[anywhere] * len(values),
+        input_output_aliases={i: i for i in range(len(values))},
+        name="after",
+    )(*values, *others)
+
+
+def put_block(whole_array, block, *at):
+    for _ in range(whole_array.ndim - block.ndim):
+        block = block[None]
+    return lax.dynamic_update_slice(
+        whole_array, block, tuple(at) + (0,) * (whole_array.ndim - len(at))
+    )
 
 
 def middle_kernel(
@@ -368,9 +411,9 @@
     gain_two_ref,
     router_ref,
     wo_ref,
-    att_ref,
-    output_ref,
+    queued_ref,
     vectors_ref,
+    mixed_ref,
     gres_ref,
     gaz_ref,
 ):
@@ -392,16 +435,15 @@
     scale = lax.rsqrt(jnp.mean(residual * residual, axis=-1, keepdims=True) + EPS)
     normed = residual * scale
     second = jnp.sum(grad_normed * normed, axis=0, keepdims=True)
-    vectors_ref[...] = jnp.concatenate(
-        [router, second, jnp.zeros((vectors_ref.shape[0] - experts - 1, width), F32)], axis=0
-    ).astype(BF16)
+    spare = jnp.zeros((vectors_ref.shape[0] - experts - 1, width), F32)
+    vectors_ref[...] = jnp.concatenate([router, second, spare], axis=0).astype(BF16)
     scaled = grad_normed * gain_two_ref[...]
     grad_residual = u_ref[...].astype(F32) + scale * (
         scaled - normed * jnp.mean(scaled * normed, axis=-1, keepdims=True)
     )
     gres_ref[...] = grad_residual
     grad_mixed = grad_residual.astype(BF16)
-    output_ref[...] = mul(att_ref[...], grad_mixed, TN).astype(BF16)
+    mixed_ref[...] = grad_mixed
     for tile in range(TILES):
         grad_att = mul(grad_mixed, wo_ref[tile * 256 : (tile + 1) * 256, :], NT)
         for piece in range(pieces):
@@ -423,10 +465,13 @@
     sin_ref,
     mix_ref,
     own_ref,
+    att_ref,
+    mixed_ref,
+    vectors_ref,
+    queued_ref,
     dq_ref,
     dkv_ref,
-    query_ref,
-    keyval_ref,
+    weights_ref,
     dk_acc,
     dv_acc,
     row_ref,
@@ -471,15 +516,29 @@
         row_ref[rows, inner:] = dv_acc[rows, :].astype(BF16)
         piece, owner = block // members, block % members
         dkv_ref[owner, piece * BLOCK : (piece + 1) * BLOCK, :] = row_ref[rows, :]
-    query_ref[...] = mul(own_ref[...], dq_ref[...], TN).astype(BF16)
-    keyval_ref[...] = mul(mix_ref[...], row_ref[...], TN).astype(BF16)
+    width = dq_ref.shape[1]
+    for i, (left_ref, right_ref) in enumerate(
+        ((own_ref, dq_ref), (mix_ref, row_ref), (att_ref, mixed_ref))
+    ):
+        product = mul(left_ref[...], right_ref[...], TN)
+        weights_ref[i * width : (i + 1) * width, :] = product.astype(BF16)
+    weights_ref[3 * width :, :] = vectors_ref[...]
 
 
 def last_kernel(
-    members, me_ref, dq_ref, dkv_ref, wq_ref, wk_ref, wv_ref, h_ref, gres_ref, gain_one_ref, gh_ref, first_ref
+    members,
+    dq_ref,
+    dkv_ref,
+    wq_ref,
+    wk_ref,
+    wv_ref,
+    input_ref,
+    gres_ref,
+    gain_one_ref,
+    tied_ref,
+    gh_ref,
+    first_ref,
 ):
-    member = me_ref[0]
-    tokens = dq_ref.shape[0]
     inner = wk_ref.shape[1]
     grad_kv = dkv_ref[0].astype(F32)
     for other in range(1, members):
@@ -490,13 +549,7 @@
         + mul(grad_kv[:, :inner], wk_ref[...], NT)
         + mul(grad_kv[:, inner:], wv_ref[...], NT)
     )
-    x = jnp.concatenate(
-        [
-            h_ref[pl.ds(pl.multiple_of((p * members + member) * BLOCK, BLOCK), BLOCK), :]
-            for p in range(tokens // BLOCK)
-        ],
-        axis=0,
-    ).astype(F32)
+    x = input_ref[...].astype(F32)
     scale = lax.rsqrt(jnp.mean(x * x, axis=-1, keepdims=True) + EPS)
     normed = x * scale
     first_ref[...] = jnp.broadcast_to(
@@ -556,12 +609,49 @@
     meta = jnp.concatenate(
         [positions.reshape(1, tokens), expert_ids.reshape(tokens, TOPK).T], axis=0
     )
-    meta = lax.all_to_all(
-        jnp.broadcast_to(meta[None], (shards,) + meta.shape), "seq", 0, 0, tiled=True
-    )
     row_in = lax.all_to_all(jnp.repeat(hidden_in, members, axis=0), "seq", 0, 0, tiled=True)
     row_in = row_in.reshape(length, width)
+    def onward(values, count):
+        to = lambda j: (j // members + count) % rows_here * members + j % members
+        return lax.ppermute(values, "seq", [(j, to(j)) for j in range(shards)])
+
+    def across(values, other):
+        return lax.ppermute(values, "seq", [(j, j ^ other) for j in range(shards)])
+
+    def row_swap(values, other):
+        count = lax.axis_size("rows")
+        return lax.ppermute(values, "rows", [(j, j ^ other) for j in range(count)])
+
+    def gather(values):
+        found = []
+        for k in range(rows_here):
+            values = onward(values, 1) if k else values
+            found.append([values] + [across(values, other) for other in range(1, members)])
+        return found
+
+    def joined(part):
+        return add(part[0], *(across(part[o], o) for o in range(1, members)))
+
+    def scatter(sums):
+        return add(*(onward(total, rows_here - k) if k else total for k, total in enumerate(sums)))
+
+    core = lax.axis_index("rows") % 2
+
+    of_row = lambda k: lax.dynamic_index_in_dim(hidden_in, (row + k) % rows_here, 0, keepdims=False)
+    row_in = [of_row(k) for k in range(rows_here)]
+    meta = after([jnp.broadcast_to(meta[None], (shards,) + meta.shape)], *row_in)[0]
+    meta = lax.all_to_all(meta, "seq", 0, 0, tiled=True)
+    row_in = row_in[:1] + [onward(row_in[k], k) for k in range(1, rows_here)]
+    row_in = [[v] + [across(v, other) for other in range(1, members)] for v in row_in]
+    row_in = [v for blocks in row_in for v in blocks]
+    places = [
+        (row - k) % rows_here * members + (member ^ other)
+        for k in range(rows_here)
+        for other in range(members)
+    ]
+    me_row = jnp.stack([member, me] + places).astype(jnp.int32)
     upstream = lax.all_gather(out_grad, "seq", axis=0, tiled=False)
+    upstream = upstream.reshape(rows_here, members, rows_here, block, width)
 
     meta = meta.reshape(rows_here, members, TOPK + 1, rows_here, block)
     row_meta = lax.dynamic_index_in_dim(meta, row, 3, keepdims=False)
@@ -578,8 +668,8 @@
 
     gain_one, gain_two = first_gain.reshape(1, width), second_gain.reshape(1, width)
     router = router_weight.T
-    mix, own_mix, qz, k_row, v_row, att, residual, xg, gates = pl.pallas_call(
-        functools.partial(front_kernel, members),
+    mix, own_mix, qz, k_row, v_row, att, residual, xg, gates, own_in = pl.pallas_call(
+        functools.partial(front_kernel, members, shards),
         out_shape=[
             struct((length, width), BF16),
             struct((tokens, width), BF16),
@@ -590,15 +680,17 @@
             struct((tokens, width), F32),
             struct((tokens + PAD, width), BF16),
             struct((expert_count, tokens), F32),
+            struct((tokens, width), BF16),
         ],
-        in_specs=[scalars()] + [whole()] * 12,
-        out_specs=[whole()] * 9,
+        in_specs=[scalars()] + [whole()] * (shards + 11),
+        out_specs=[whole()] * 10,
+        scratch_shapes=[pltpu.VMEM((length, width), BF16)],
         compiler_params=params(56),
-        cost_estimate=cost(5e9, 12e6),
+        cost_estimate=took(19.5),
         name="front",
     )(
-        me_pair,
-        row_in,
+        me_row,
+        *row_in,
         cosine,
         sine,
         own_pos,
@@ -617,7 +709,11 @@
     )
     grouped = lambda *shape: pl.BlockSpec((PAIR,) + shape, lambda i: (i,) + (0,) * len(shape))
     per_row = members // PAIR
-    upstream = upstream.reshape(rows_here, members, rows_here, block, width)
+    one_on = onward(xg, 1)
+    beside = [across(xg, other) for other in range(1, members)]
+    one_on = after([one_on], *beside)[0]
+    sets = [[xg] + beside, [one_on] + [across(one_on, other) for other in range(1, members)]]
+    two_on = onward(one_on, 1)
     slot, us, product = pl.pallas_call(
         upstream_kernel,
         grid=(groups,),
@@ -633,147 +729,218 @@
                 lambda i: (0, i % per_row, i // per_row, 0, 0),
             ),
             constant((experts, hidden, width)),
-        ],
+        ]
+        + [pl.BlockSpec(memory_space=pl.ANY)],
         out_specs=[
             grouped(8, tokens),
             grouped(experts * slots, width),
             grouped(experts * slots, hidden),
         ],
         compiler_params=params(48),
-        cost_estimate=cost(6e9, 20e6),
+        cost_estimate=took(15.5),
         name="upstream",
-    )(named, upstream, down_weight)
-
-    gathered = lax.all_gather(xg, "seq", axis=0, tiled=False)
-    dx, y, xs, hs, dgs, dus = pl.pallas_call(
-        expert_kernel,
-        grid=(groups,),
-        out_shape=[
-            struct((shards, tokens + PAD, width), BF16),
-            struct((shards, tokens, width), BF16),
-            struct((shards, experts * slots, width), BF16),
-            struct((shards, experts * slots, hidden), BF16),
-            struct((shards, experts * slots, hidden), BF16),
-            struct((shards, experts * slots, hidden), BF16),
-        ],
-        in_specs=[
-            scalars(),
-            grouped(tokens + PAD, width),
-            grouped(8, tokens),
-            grouped(experts * slots, hidden),
-            constant((experts, width, hidden)),
-            constant((experts, width, hidden)),
-            constant((experts, hidden, width)),
-        ],
-        out_specs=[
-            grouped(tokens + PAD, width),
-            grouped(tokens, width),
-            grouped(experts * slots, width),
-            grouped(experts * slots, hidden),
-            grouped(experts * slots, hidden),
-            grouped(experts * slots, hidden),
-        ],
-        scratch_shapes=[
-            pltpu.VMEM((PAIR, experts * slots, width), BF16),
-            pltpu.VMEM((PAIR, experts * slots, width), BF16),
-            pltpu.VMEM((PAIR, experts * slots, tokens), BF16),
-            pltpu.VMEM((8, tokens), F32),
-            pltpu.VMEM((PAIR, PAD, width), F32),
-        ],
-        compiler_params=params(58),
-        cost_estimate=cost(30e9, 50e6),
-        name="experts",
-    )(me_pair, gathered, slot, product, gate_weight, up_weight, down_weight)
-    dx_sum = lax.psum_scatter(dx, "seq", scatter_dimension=0, tiled=False)
-
-    step = 8
-    one_expert = lambda w: pl.BlockSpec((step, slots, w), lambda e, i: (i, e, 0))
-    grad_spec = lambda a, b: pl.BlockSpec((1, a, b), lambda e, i: (e, 0, 0))
-    gate_part, up_part, down_part = pl.pallas_call(
-        expert_grads_kernel,
-        grid=(experts, shards // step),
-        out_shape=[
-            struct((experts, width, hidden), BF16),
-            struct((experts, width, hidden), BF16),
-            struct((experts, hidden, width), BF16),
-        ],
-        in_specs=[
-            one_expert(width),
-            one_expert(width),
-            one_expert(hidden),
-            one_expert(hidden),
-            one_expert(hidden),
-        ],
-        out_specs=[grad_spec(width, hidden), grad_spec(width, hidden), grad_spec(hidden, width)],
-        scratch_shapes=[
-            pltpu.VMEM((width, hidden), F32),
-            pltpu.VMEM((width, hidden), F32),
-            pltpu.VMEM((hidden, width), F32),
-        ],
-        compiler_params=params(48),
-        cost_estimate=cost(13e9, 45e6),
-        name="expert_grads",
-    )(xs, us, hs, dgs, dus)
-    gate_sum, up_sum, down_sum = lax.psum((gate_part, up_part, down_part), "rows")
-    y_sum = lax.psum_scatter(y, "seq", scatter_dimension=0, tiled=False)
-
+    )(named, upstream, down_weight, one_on)
+
+    wide, narrow = experts * slots, hidden
+    kept = []
+    values = after([two_on], slot)[0]
+    for k in range(2, rows_here):
+        values = onward(values, 1) if k > 2 else values
+        sets.append([values] + [across(values, other) for other in range(1, members)])
+    order = list(range(rows_here))
+    dx_parts, y_parts, dx_sums = [[] for _ in sets], [[] for _ in sets], []
+    for k in order:
+        group = sets[k]
+        tied = []
+        for later, member_of in ((k + 1, -1), (k + 2, 0)):
+            tied += [sets[later][member_of]] if later < rows_here else []
+        tied += dx_sums[k - 2 : k - 1] if k > 1 else []
+        for q in range(members // PAIR):
+            pair = (row - k) % rows_here * per_row + ((member // PAIR) ^ q)
+            info = jnp.stack([member % PAIR, me, pair, core]).astype(jnp.int32)
+            flat = lambda *shape: pl.BlockSpec(shape, lambda e, info: (0,) * len(shape))
+            of_pair = lambda w: pl.BlockSpec((PAIR, slots, w), lambda e, info: (info[2], e, 0))
+            of_expert = lambda a, b: pl.BlockSpec((1, a, b), lambda e, info: (e, 0, 0))
+            outcome = pl.pallas_call(
+                functools.partial(expert_kernel, len(kept) + len(tied)),
+                grid_spec=pltpu.PrefetchScalarGridSpec(
+                    num_scalar_prefetch=1,
+                    grid=(experts,),
+                    in_specs=[
+                        flat(tokens + PAD, width),
+                        flat(tokens + PAD, width),
+                        pl.BlockSpec((PAIR, 8, tokens), lambda e, info: (info[2], 0, 0)),
+                        of_pair(hidden),
+                        of_expert(width, hidden),
+                        of_expert(width, hidden),
+                        of_expert(hidden, width),
+                    ]
+                    + [pl.BlockSpec(memory_space=pl.ANY)] * (len(kept) + len(tied)),
+                    out_specs=[
+                        flat(tokens + PAD, width),
+                        flat(tokens + PAD, width),
+                        flat(tokens, width),
+                        flat(tokens, width),
+                        of_pair(width),
+                        of_pair(hidden),
+                        of_pair(hidden),
+                        of_pair(hidden),
+                    ],
+                    scratch_shapes=[
+                        pltpu.VMEM((PAIR, wide, width), BF16),
+                        pltpu.VMEM((PAIR, wide, width), BF16),
+                        pltpu.VMEM((PAIR, wide, tokens), BF16),
+                        pltpu.VMEM((8, tokens), F32),
+                        pltpu.VMEM((PAIR, PAD, width), F32),
+                    ],
+                ),
+                out_shape=[
+                    struct((tokens + PAD, width), BF16),
+                    struct((tokens + PAD, width), BF16),
+                    struct((tokens, width), BF16),
+                    struct((tokens, width), BF16),
+                    struct((shards, wide, width), BF16),
+                    struct((shards, wide, hidden), BF16),
+                    struct((shards, wide, hidden), BF16),
+                    struct((shards, wide, hidden), BF16),
+                ],
+                input_output_aliases={8 + i: 4 + i for i in range(len(kept))},
+                compiler_params=params(40),
+                cost_estimate=took(13.3),
+                name="experts",
+            )(info, group[2 * q], group[2 * q + 1], slot, product, gate_weight, up_weight, down_weight, *kept, *tied)
+            dx_parts[k] += outcome[:2]
+            y_parts[k] += outcome[2:4]
+            kept = outcome[4:]
+        dx_sums.append(joined(dx_parts[k]))
+    sent = [dx_sums[0]] + [onward(dx_sums[k], rows_here - k) for k in range(1, rows_here)]
+    dx_sum = add(*sent)
+
+    info = jnp.stack([member % PAIR, me, me, core]).astype(jnp.int32)
+    halves = (3, width // 2, hidden)
+    mine, keep = [], us
+    for first, count in ((0, 1), (1, experts - 1)):
+        if not count:
+            continue
+        one_expert = lambda w: pl.BlockSpec((shards, slots, w), lambda i, at=first: (0, at + i, 0))
+        half = pl.BlockSpec((1,) + halves, lambda i: (i, 0, 0, 0))
+        keep, send = pl.pallas_call(
+            expert_grads_kernel,
+            grid=(count,),
+            out_shape=[struct((count,) + halves, BF16)] * 2,
+            in_specs=[scalars(), one_expert(width), one_expert(width)]
+            + [one_expert(hidden)] * 3
+            + [pl.BlockSpec(memory_space=pl.ANY)] * 3,
+            out_specs=[half] * 2,
+            compiler_params=params(60),
+            cost_estimate=took(4.6 * count + 1.5),
+            name="expert_grads",
+        )(info, kept[0], us, *kept[1:], keep, dx_sums[2 if first == 0 else 3], sent[1 if first == 0 else 2])
+        received = row_swap(send, 1)
+        mine += [add(keep[i], received[i]) for i in range(count)]
+    queued = mine[-1]
+    crossed = []
+    for e in range(experts):
+        bit = 2
+        while bit < lax.axis_size("rows"):
+            crossed.append(row_swap(mine[e], bit))
+            mine[e] = add(mine[e], crossed[-1])
+            bit *= 2
+    finished = []
+    for e in range(experts):
+        grad_spec = lambda a, b: pl.BlockSpec((1, a, b), lambda i, e=e: (e, 0, 0))
+        half = pl.BlockSpec(halves, lambda i: (0, 0, 0))
+        finished = pl.pallas_call(
+            functools.partial(finish_kernel, len(finished)),
+            grid=(1,),
+            out_shape=[
+                struct((experts, width, hidden), F32),
+                struct((experts, width, hidden), F32),
+                struct((experts, hidden, width), F32),
+            ],
+            in_specs=[scalars(), half, half]
+            + [pl.BlockSpec(memory_space=pl.ANY)] * len(finished),
+            out_specs=[grad_spec(width, hidden), grad_spec(width, hidden), grad_spec(hidden, width)],
+            input_output_aliases={3 + i: i for i in range(len(finished))},
+            compiler_params=params(32),
+            cost_estimate=took(4.6),
+            name="finish",
+        )(info, mine[e], row_swap(mine[e], 1), *finished)
+    later = after([y for part in y_parts for y in part[1:]], dx_sum)
+    later = [later[k * (members - 1) : (k + 1) * (members - 1)] for k in range(rows_here)]
     own_upstream = lax.dynamic_index_in_dim(upstream, row, 2, keepdims=False)
     own_upstream = lax.dynamic_index_in_dim(own_upstream, member, 1, keepdims=False)
     own_upstream = own_upstream.reshape(tokens, width)
-    output_part, vectors, grad_residual, gaz = pl.pallas_call(
+    vectors, grad_mixed, grad_residual, gaz = pl.pallas_call(
         middle_kernel,
         out_shape=[
-            struct((width, width), BF16),
-            struct((expert_count + PAD, width), BF16),
+            struct((EXTRA, width), BF16),
+            struct((tokens, width), BF16),
             struct((tokens, width), F32),
             struct((rows_here, TILES, 4 * BLOCK, LANES), BF16),
         ],
-        in_specs=[whole()] * 9,
+        in_specs=[whole()] * 8 + [pl.BlockSpec(memory_space=pl.ANY)],
         out_specs=[whole()] * 4,
         compiler_params=params(48),
-        cost_estimate=cost(2e9, 10e6),
+        cost_estimate=took(6),
         name="middle",
-    )(dx_sum, own_upstream, xg, residual, gates, gain_two, router, output_weight, att)
-
-    dq, dkv, query_part, keyval_part = pl.pallas_call(
+    )(dx_sum, own_upstream, xg, residual, gates, gain_two, router, output_weight, dx_sums[0])
+
+    dq, dkv, weights = pl.pallas_call(
         functools.partial(attention_back_kernel, members),
         out_shape=[
             struct((tokens, width), BF16),
             struct((members, tokens, width), BF16),
-            struct((width, width), BF16),
-            struct((width, width), BF16),
+            struct((3 * width + EXTRA, width), BF16),
         ],
-        in_specs=[scalars()] + [whole()] * 9,
-        out_specs=[whole()] * 4,
+        in_specs=[scalars()] + [whole()] * 12 + [pl.BlockSpec(memory_space=pl.ANY)],
+        out_specs=[whole()] * 3,
         scratch_shapes=[
             pltpu.VMEM((length, inner), F32),
             pltpu.VMEM((length, inner), F32),
             pltpu.VMEM((length, width), BF16),
         ],
         compiler_params=params(58),
-        cost_estimate=cost(5e9, 12e6),
+        cost_estimate=took(21.5),
         name="attention_back",
-    )(me_pair, qz, gaz, k_row, v_row, own_pos, cosine, sine, mix, own_mix)
+    )(me_pair, qz, gaz, k_row, v_row, own_pos, cosine, sine, mix, own_mix, att, grad_mixed, vectors, vectors)
     dkv = lax.all_to_all(dkv, "seq", 0, 0, tiled=True, axis_index_groups=same_row)
     grad_in, first_part = pl.pallas_call(
         functools.partial(last_kernel, members),
-        out_shape=[struct((tokens, width), BF16), struct((PAD, width), BF16)],
-        in_specs=[scalars()] + [whole()] * 8,
+        out_shape=[struct((tokens, width), BF16), struct((8, width), F32)],
+        in_specs=[whole()] * 8 + [pl.BlockSpec(memory_space=pl.ANY)],
         out_specs=[whole()] * 2,
         compiler_params=params(48),
-        cost_estimate=cost(1e9, 8e6),
+        cost_estimate=took(3.1),
         name="last",
-    )(me_pair, dq, dkv, query_weight, key_weight, value_weight, row_in, grad_residual, gain_one)
-
-    shared = lax.psum((output_part, query_part, keyval_part, vectors, first_part), ("rows", "seq"))
-    output_sum, query_sum, keyval_sum, vector_sum, first_sum = (s.astype(F32) for s in shared)
-    hidden_out = (residual + y_sum.astype(F32)).astype(BF16)
+    )(dq, dkv, query_weight, key_weight, value_weight, own_in, grad_residual, gain_one, crossed[0])
+
+    steps = [crossed[min(i, experts - 1)] for i in range(4)]
+    first_sum, bit = after([first_part], steps[2])[0], 1
+    while bit < shards:
+        first_sum = first_sum + across(first_sum, bit)
+        bit *= 2
+    bit = 1
+    while bit < lax.axis_size("rows"):
+        first_sum = first_sum + row_swap(first_sum, bit)
+        bit *= 2
+    y_sum = scatter(
+        [joined([y, *rest]) for y, rest in zip(after([p[0] for p in y_parts], dq), later)]
+    )
+    steps = [crossed[min(i, experts - 1)] for i in range(4)]
+    hidden_out = after([(residual + y_sum.astype(F32)).astype(BF16)], steps[1])[0]
     back = lambda values: lax.all_to_all(
         values.reshape(rows_here, block, width), "seq", 0, 0, tiled=True, axis_index_groups=same_member
     )
+    hidden_out, grad_in = back(hidden_out), back(grad_in)
+    shared = lax.psum(weights, ("rows", "seq"))
+    shared = after([shared], hidden_out, grad_in, first_sum, finished[0])[0]
+    query_sum, keyval_sum, output_sum, vector_sum = (
+        shared[i * width : (i + 1) * width].astype(F32) for i in range(4)
+    )
     return (
-        back(hidden_out),
-        back(grad_in).astype(F32),
+        hidden_out,
+        grad_in.astype(F32),
         first_sum[0],
         query_sum,
         keyval_sum[:, :inner],
@@ -781,9 +948,7 @@
         output_sum,
         vector_sum[expert_count],
         vector_sum[:expert_count].T,
-        gate_sum.astype(F32),
-        up_sum.astype(F32),
-        down_sum.astype(F32),
+        *finished,
     )
 
 

time: 820 us -> 567 us (0.69)
  waiting for transfers between devices: 547 us -> 229 us
  blocking collectives: 55.9 us -> 0 us
  starting transfers between devices: 15.6 us -> 70.1 us
  Pallas kernels: 130 us -> 162 us
  other arithmetic: 30.5 us -> 49.1 us
  local copies, waits for them, and re-layouts: 25.5 us -> 34.6 us
    psum x2 -> x1, waiting for transfers between devices: 307 us -> 38.4 us  [local(): shared = lax.psum(weights, ('rows', 'seq'))]
    ppermute x0 -> x43, waiting for transfers between devices: none -> 154 us  [the longest x12 74.3 us: row_swap(): return lax.ppermute(values, 'rows', [(j, j ^ other) for j in range(count)])]
    reduce_scatter x2 -> x0, waiting for transfers between devices: 128 us -> none  [the longest x1 67.5 us: local(): dx_sum = lax.psum_scatter(dx, 'seq', scatter_dimension=0, tiled=False)]
    all_gather x1 -> x0, waiting for transfers between devices: 59.5 us -> none  [local(): gathered = lax.all_gather(xg, 'seq', axis=0, tiled=False)]
    ppermute x0 -> x43, starting transfers between devices: none -> 53.2 us  [the longest x19 27.6 us: across(): return lax.ppermute(values, 'seq', [(j, j ^ other) for j in range(shards)])]
    psum x1 -> x0, blocking collectives: 41.4 us -> none  [local(): lax.psum((output_part, query_part, keyval_part, vectors, first_part), ('r...]
    pallas_call x4 -> x20, Pallas kernels: 88.9 us -> 120 us  [the longest x4 53.8 us: local(): pl.pallas_call(functools.partial(expert_kernel, len(kept) + len(tied)), g...]
    all_to_all x1, waiting for transfers between devices: 34.6 us -> 10.6 us  [local(): meta = lax.all_to_all(meta, 'seq', 0, 0, tiled=True)]
  transfers between devices with their start and end apart: 10 -> 49, of which waited for: 8 -> 18; matrix products, arithmetic and copies ran while one was open for 4% -> 9% of each run, Pallas kernels for 10% -> 26%
where the time goes in v2:
time: 567 us; the launch traced here: 559 us
  waiting for transfers between devices  229 us (40%)
  Pallas kernels  162 us (29%)
  starting transfers between devices  70.1 us (12%)
  other arithmetic  49.1 us (9%)
  local copies, waits for them, and re-layouts  34.6 us (6%)
  between operations  15.2 us (3%)
    ppermute x12, waiting for transfers between devices, row_swap(): return lax.ppermute(values, 'rows', [(j, j ^ other) for j in range(count)])  74.3 us
    pallas_call x4, Pallas kernels, local(): pl.pallas_call(functools.partial(expert_kernel, len(kept) + len(tied)), g...  53.8 us
    ppermute x12, waiting for transfers between devices, onward(): return lax.ppermute(values, 'seq', [(j, to(j)) for j in range(shards)])  50.5 us
    psum x1, waiting for transfers between devices, local(): shared = lax.psum(weights, ('rows', 'seq'))  38.4 us
    convert_element_type x14, other arithmetic, add(): return sum((term.astype(F32) for term in terms)).astype(terms[0].dtype)  31.1 us
    ppermute x19, waiting for transfers between devices, across(): return lax.ppermute(values, 'seq', [(j, j ^ other) for j in range(shards)])  29.2 us
    ppermute x19, starting transfers between devices, across(): return lax.ppermute(values, 'seq', [(j, j ^ other) for j in range(shards)])  27.6 us
    unnamed x128, local copies, waits for them, and re-layouts  23.9 us
  transfers between devices with their start and end apart: 49, of which 18 were waited for; matrix products, arithmetic and copies ran while one was open for 9% of the time, Pallas kernels for 26%

profile of v2, /device:TPU:0, one launch (start us, length us, event | category | flops | bytes accessed | tf_op | source)
XLA Modules:
  0.0 559.1 jit_solution(7460237030148637870)
XLA Ops:
  9.2 5.1 collective-permute-start.5
  19.1 4.7 all-to-all-start
  25.3 10.6 %all-to-all-done = s32[8,9,256]{2,1,0:T(8,128)S(1)} async-done(((s32[8,9,256]{2,1,0:T(8,128)}), s32[8,9,256]{2,1,0:T(8,128)S(1)}, u32[]{:S(2)}, u32[]{:S(2)}) %all-to-all-start) | async-done | bytes 73760 | tf_op jit(solution)/shard_map/all_to_all | solution.py:643
  45.9 19.5 %front.1 = (bf16[512,1024]{1,0:T(8,128)(2,1)}, bf16[256,1024]{1,0:T(8,128)(2,1)}, bf16[4,4,256,128]{3,2,1,0:T(8,128)(2,1)}, bf16[512,512]{1,0:T(8,128)(2,1)}, bf...) custom-call(s32[10]{0:T(128)} %stack.95.me_ref, ...), custom_call_target="tpu_custom_call" | custom-call | flops 9749999616 | tf_op jit(solution)/shard_map/front/pallas_call | solution.py:671
  67.6 22.2 %collective-permute-done.8.refs_0_ = bf16[272,1024]{1,0:T(8,128)(2,1)S(1)} collective-permute-done((bf16[272,1024]{1,0:T(8,128)(2,1)}, bf16[272,1024]{1,0:T(8,128)(2,1)S(1)}, u32[]{:S(2)}, u32[]{:S(2)}) %collective-permute-start.8) | collective-permute-done | bytes 557088 | tf_op jit(solution)/shard_map/ppermute | solution.py:616
  91.4 2.9 collective-permute-start.9
  94.3 14.0 %all-gather.3.cloned.1.call-done = bf16[32,64,1024]{2,1,0:T(8,128)(2,1)} async-done(((bf16[4,64,1024]{2,1,0:T(8,128)(2,1)}), bf16[32,64,1024]{2,1,0:T(8,128)(2,1)}) %all-gather.3.cloned.1.call-update) | async-done | bytes 4194320 | tf_op jit(solution)/shard_map/all_gather | solution.py:653
  111.5 15.5 %upstream.1 = (f32[8,8,256]{2,1,0:T(8,128)S(1)}, bf16[8,512,1024]{2,1,0:T(8,128)(2,1)}, f32[8,512,512]{2,1,0:T(8,128)}) custom-call(f32[8,8,256]{2,1,0:T(8,128)S(1)} %reshape.108.named_ref, bf16[4,2,4,64,1024]{4,3,2,1,0:T(8,128)(2,1)S(1)} %bitcast.63, bf16[4,512,1024]{2,1,0:T(8,128)(2,1)} %wd_ref.9, bf16[272,1024]{1,0:T(8,128)(2,1)S(1)} %copy-done.4), custom_call_target="tpu_custom_call" | custom-call | flops 7750000128 | tf_op jit(solution)/shard_map/upstream/pallas_call | solution.py:717
  131.4 13.6 %experts.4 = (bf16[272,1024]{1,0:T(8,128)(2,1)S(1)}, bf16[272,1024]{1,0:T(8,128)(2,1)S(1)}, bf16[256,1024]{1,0:T(8,128)(2,1)S(1)}, bf16[256,1024]{1,0:T(8,128)(2...) custom-call(s32[4]{0:T(128)S(1)} %get-tuple-element.188.info_ref, ...), custom_call_target="tpu_custom_call" | custom-call | flops 6649999872 | tf_op jit(solution)/shard_map/experts/pallas_call | solution.py:764
  147.9 13.2 %experts.5 = (bf16[272,1024]{1,0:T(8,128)(2,1)S(1)}, bf16[272,1024]{1,0:T(8,128)(2,1)S(1)}, bf16[256,1024]{1,0:T(8,128)(2,1)S(1)}, bf16[256,1024]{1,0:T(8,128)(2...) custom-call(s32[4]{0:T(128)S(1)} %get-tuple-element.187.info_ref, ...), custom_call_target="tpu_custom_call", output_to_operand_aliasing={{4}: (8, {}), {5}: (9, {}), {6}: (10, {}), {7}: (11, {})} | custom-call | flops 6649999872 | tf_op jit(solution)/shard_map/experts/pallas_call | solution.py:764
  163.4 10.0 %collective-permute-done.13.rest_4_.xb_ref = bf16[272,1024]{1,0:T(8,128)(2,1)S(1)} collective-permute-done((bf16[272,1024]{1,0:T(8,128)(2,1)S(1)}, bf16[272,1024]{1,0:T(8,128)(2,1)S(1)}, u32[]{:S(2)}, u32[]{:S(2)}) %collective-permute-start.13) | collective-permute-done | bytes 557088 | tf_op jit(solution)/shard_map/ppermute | solution.py:619
  173.4 13.2 %experts.6 = (bf16[272,1024]{1,0:T(8,128)(2,1)S(1)}, bf16[272,1024]{1,0:T(8,128)(2,1)S(1)}, bf16[256,1024]{1,0:T(8,128)(2,1)S(1)}, bf16[256,1024]{1,0:T(8,128)(2...) custom-call(s32[4]{0:T(128)S(1)} %get-tuple-element.186.info_ref, ...), custom_call_target="tpu_custom_call", output_to_operand_aliasing={{4}: (8, {}), {5}: (9, {}), {6}: (10, {}), {7}: (11, {})} | custom-call | flops 6649999872 | tf_op jit(solution)/shard_map/experts/pallas_call | solution.py:764
  189.6 13.7 %experts.7 = (bf16[272,1024]{1,0:T(8,128)(2,1)S(1)}, bf16[272,1024]{1,0:T(8,128)(2,1)S(1)}, bf16[256,1024]{1,0:T(8,128)(2,1)S(1)}, bf16[256,1024]{1,0:T(8,128)(2...) custom-call(s32[4]{0:T(128)S(1)} %get-tuple-element.185.info_ref, ...), custom_call_target="tpu_custom_call", output_to_operand_aliasing={{4}: (8, {}), {5}: (9, {}), {6}: (10, {}), {7}: (11, {})} | custom-call | flops 6649999872 | tf_op jit(solution)/shard_map/experts/pallas_call | solution.py:764
  208.0 2.9 collective-permute-start.16
  212.2 5.2 collective-permute-done.19
  218.4 5.5 collective-permute-done.16.sent_ref
  224.8 7.7 %expert_grads.2 = (bf16[1,3,512,512]{3,2,1,0:T(8,128)(2,1)}, bf16[1,3,512,512]{3,2,1,0:T(8,128)(2,1)}) custom-call(s32[4]{0:T(128)} %get-tuple-element.168.info_ref, bf16[8,512,1024]{2,1,0:T(8,128)(2,1)} %get-tuple-element.141.xs_ref, bf16[8,512,1024]{2,1,0:T(8,128)(2,1)} %get-tuple-element.142.us_ref.earlier_ref, bf16[8,512,512]{2,1,0:T(8,128)(2,1)} %copy-done, ...), custom_call_target="tpu_custom_call" | custom-call | flops 3049999872 | tf_op jit(solution)/shard_map/expert_grads/pallas_call | solution.py:827
  232.5 10.2 %collective-permute-done.18.sent_ref = bf16[272,1024]{1,0:T(8,128)(2,1)S(1)} collective-permute-done((bf16[272,1024]{1,0:T(8,128)(2,1)S(1)}, bf16[272,1024]{1,0:T(8,128)(2,1)S(1)}, u32[]{:S(2)}, u32[]{:S(2)}) %collective-permute-start.18) | collective-permute-done | bytes 557088 | tf_op jit(solution)/shard_map/ppermute | solution.py:616
  243.6 15.7 %expert_grads.3 = (bf16[3,3,512,512]{3,2,1,0:T(8,128)(2,1)}, bf16[3,3,512,512]{3,2,1,0:T(8,128)(2,1)}) custom-call(s32[4]{0:T(128)} %get-tuple-element.168.info_ref, bf16[8,512,1024]{2,1,0:T(8,128)(2,1)} %get-tuple-element.141.xs_ref, bf16[8,512,1024]{2,1,0:T(8,128)(2,1)} %get-tuple-element.142.us_ref.earlier_ref, bf16[8,512,512]{2,1,0:T(8,128)(2,1)} %copy-done, ...), custom_call_target="tpu_custom_call" | custom-call | flops 7649999872 | tf_op jit(solution)/shard_map/expert_grads/pallas_call | solution.py:827
  259.8 3.2 collective-permute-start.20
  264.7 12.4 %collective-permute-done.20 = bf16[272,1024]{1,0:T(8,128)(2,1)S(1)} collective-permute-done((bf16[272,1024]{1,0:T(8,128)(2,1)S(1)}, bf16[272,1024]{1,0:T(8,128)(2,1)S(1)}, u32[]{:S(2)}, u32[]{:S(2)}) %collective-permute-start.20) | collective-permute-done | bytes 557088 | tf_op jit(solution)/shard_map/ppermute | solution.py:616
  283.6 4.5 middle.1
  288.2 4.0 fusion.1
  293.8 6.0 %fusion.3 = (bf16[3,512,512]{2,1,0:T(8,128)(2,1)}, bf16[3,512,512]{2,1,0:T(8,128)(2,1)}, bf16[3,512,512]{2,1,0:T(8,128)(2,1)}) fusion(bf16[3,3,512,512]{3,2,1,0:T(8,128)(2,1)} %collective-permute-done.28, bf16[3,3,512,512]{3,2,1,0:T(8,128)(2,1)} %get-tuple-element.147), kind=kLoop, calls=%fused_computation.14 | loop fusion | flops 9437184 | bytes 14155776 | tf_op jit(solution)/shard_map/convert_element_type | solution.py:382
  300.3 23.3 %attention_back.1 = (bf16[256,1024]{1,0:T(8,128)(2,1)}, bf16[2,256,1024]{2,1,0:T(8,128)(2,1)}, bf16[3200,1024]{1,0:T(8,128)(2,1)}) custom-call(s32[2]{0:T(128)} %pad_add_fusion.2.me_ref, bf16[4,4,256,128]{3,2,1,0:T(8,128)(2,1)} %get-tuple-element.114.qz_ref, bf16[4,4,256,128]{3,2,1,0:T(8,128)(2,1)} %copy-done.37, bf16[512,512]{1,0:T(8,128)(2,1)} %get-tuple-element.121.k_ref, ...), custom_call_target="tpu_custom_call" | custom-call | flops 10750000128 | tf_op jit(solution)/shard_map/attention_back/pallas_call | solution.py:889
  323.6 3.6 all-to-all-start.2
  339.8 10.9 %all-to-all-done.2.dkv_ref = bf16[2,256,1024]{2,1,0:T(8,128)(2,1)S(1)} async-done(((bf16[2,256,1024]{2,1,0:T(8,128)(2,1)}), bf16[2,256,1024]{2,1,0:T(8,128)(2,1)S(1)}, u32[]{:S(2)}, u32[]{:S(2)}) %all-to-all-start.2) | async-done | bytes 1048608 | tf_op jit(solution)/shard_map/all_to_all | solution.py:907
  353.1 3.1 last.1
  357.7 4.1 all-to-all-start.3
  361.8 3.5 add_convert_fusion.mine_ref
  365.3 11.3 %collective-permute-done.29.refs_1_ = bf16[3,512,512]{2,1,0:T(8,128)(2,1)} collective-permute-done((bf16[3,512,512]{2,1,0:T(8,128)(2,1)}, bf16[3,512,512]{2,1,0:T(8,128)(2,1)}, u32[]{:S(2)}, u32[]{:S(2)}) %collective-permute-start.29) | collective-permute-done | bytes 1572896 | tf_op jit(solution)/shard_map/ppermute | solution.py:623
  376.9 2.4 add_convert_fusion.1.mine_ref
  381.4 29.0 %collective-permute-done.32.refs_1_ = bf16[3,512,512]{2,1,0:T(8,128)(2,1)} collective-permute-done((bf16[3,512,512]{2,1,0:T(8,128)(2,1)}, bf16[3,512,512]{2,1,0:T(8,128)(2,1)}, u32[]{:S(2)}, u32[]{:S(2)}) %collective-permute-start.32) | collective-permute-done | bytes 1572896 | tf_op jit(solution)/shard_map/ppermute | solution.py:623
  410.4 3.0 add_convert_fusion.2.mine_ref
  413.4 34.0 %collective-permute-done.38 = bf16[3,512,512]{2,1,0:T(8,128)(2,1)} collective-permute-done((bf16[3,512,512]{2,1,0:T(8,128)(2,1)}, bf16[3,512,512]{2,1,0:T(8,128)(2,1)}, u32[]{:S(2)}, u32[]{:S(2)}) %collective-permute-start.38) | collective-permute-done | bytes 1572896 | tf_op jit(solution)/shard_map/ppermute | solution.py:623
  449.8 2.6 add_convert_fusion.13.refs_0_
  452.4 4.3 all-to-all-start.1
  457.1 3.9 collective-permute-done.33
  463.7 4.7 collective-permute-done.34
  468.4 4.4 collective-permute-start.35
  472.8 3.8 collective-permute-done.35
  480.2 4.9 finish.4
  485.8 4.4 finish.5
  490.2 4.9 finish.6
  495.0 4.4 finish.7
  499.4 38.4 %all-reduce.2.cloned.1.call-done.refs_0_ = bf16[3200,1024]{1,0:T(8,128)(2,1)} async-done(((bf16[3200,1024]{1,0:T(8,128)(2,1)}), bf16[3200,1024]{1,0:T(8,128)(2,1)}) %all-reduce.2.cloned.1.call-update) | async-done | bytes 6553616 | tf_op jit(solution)/shard_map/psum | solution.py:936
  540.1 7.6 %slice_convert_fusion = (f32[1024,1024]{1,0:T(8,128)}, f32[1024,1024]{1,0:T(8,128)S(1)}, f32[1024,1024]{1,0:T(8,128)}) fusion(bf16[3200,1024]{1,0:T(8,128)(2,1)} %after.15), kind=kLoop, calls=%fused_computation.8 | loop fusion | flops 3145728 | bytes 18874368 | tf_op jit(solution)/shard_map/convert_element_type | solution.py:939
  547.8 2.4 fusion.5
  (259 shorter events, 89.3 us)
Async XLA Ops:
  7.2 101.1 %all-gather.3.cloned.1.call-start = ((), (), s32[]{:S(2)}) async-start(), calls=%async_computation.5 | async-start | bytes 4718592 | tf_op jit(solution)/shard_map/all_gather | solution.py:653
  9.2 28.0 %collective-permute-start.5 = (bf16[64,1024]{1,0:T(8,128)(2,1)S(1)}, bf16[64,1024]{1,0:T(8,128)(2,1)S(1)}, u32[]{:S(2)}, u32[]{:S(2)}) collective-permute-start(bf16[64,1024]{1,0:T(8,128)(2,1)S(1)} %get-tuple-element.178.refs_4_), channel_id=1, source_target_pairs={{0,6},{1,7},{2,0},{3,1},{4,2},{5,3},{6,4},{7,5},{8,14},{9,15},{10,... | collective-permute-start | bytes 393224 | tf_op jit(solution)/shard_map/ppermute | solution.py:616
  14.3 24.6 %collective-permute-start.1 = (bf16[64,1024]{1,0:T(8,128)(2,1)S(1)}, bf16[64,1024]{1,0:T(8,128)(2,1)S(1)}, u32[]{:S(2)}, u32[]{:S(2)}) collective-permute-start(bf16[64,1024]{1,0:T(8,128)(2,1)S(1)} %get-tuple-element.179.refs_2_), channel_id=1, source_target_pairs={{0,2},{1,3},{2,4},{3,5},{4,6},{5,7},{6,0},{7,1},{8,10},{9,11},{10,... | collective-permute-start | bytes 393224 | tf_op jit(solution)/shard_map/ppermute | solution.py:616
  14.3 25.0 %collective-permute-start.3 = (bf16[64,1024]{1,0:T(8,128)(2,1)S(1)}, bf16[64,1024]{1,0:T(8,128)(2,1)S(1)}, u32[]{:S(2)}, u32[]{:S(2)}) collective-permute-start(bf16[64,1024]{1,0:T(8,128)(2,1)S(1)} %get-tuple-element.181.refs_3_), channel_id=1, source_target_pairs={{0,4},{1,5},{2,6},{3,7},{4,0},{5,1},{6,2},{7,3},{8,12},{9,13},{10,... | collective-permute-start | bytes 393224 | tf_op jit(solution)/shard_map/ppermute | solution.py:616
  15.3 28.4 %collective-permute-start = (bf16[64,1024]{1,0:T(8,128)(2,1)S(1)}, bf16[64,1024]{1,0:T(8,128)(2,1)S(1)}, u32[]{:S(2)}, u32[]{:S(2)}) collective-permute-start(bf16[64,1024]{1,0:T(8,128)(2,1)S(1)} %get-tuple-element.180.refs_1_.refs_0_), channel_id=1, source_target_pairs={{0,1},{1,0},{2,3},{3,2},{4,5},{5,4},{6,7},{7,6},{8,9},{9,8},{10,11... | collective-permute-start | bytes 393224 | tf_op jit(solution)/shard_map/ppermute | solution.py:619
  19.1 16.7 %all-to-all-start = ((s32[8,9,256]{2,1,0:T(8,128)}), s32[8,9,256]{2,1,0:T(8,128)S(1)}, u32[]{:S(2)}, u32[]{:S(2)}) async-start(s32[8,9,256]{2,1,0:T(8,128)} %after.8), calls=%async_computation | async-start | bytes 262144 | tf_op jit(solution)/shard_map/all_to_all | solution.py:643
  23.8 514.1 %all-reduce.2.cloned.1.call-start = ((), (), s32[]{:S(2)}) async-start(), calls=%async_computation.4 | async-start | bytes 13107200 | tf_op jit(solution)/shard_map/psum | solution.py:936
  37.2 6.5 %collective-permute-start.6 = (bf16[64,1024]{1,0:T(8,128)(2,1)S(1)}, bf16[64,1024]{1,0:T(8,128)(2,1)S(1)}, u32[]{:S(2)}, u32[]{:S(2)}) collective-permute-start(bf16[64,1024]{1,0:T(8,128)(2,1)S(1)} %collective-permute-done.5.refs_6_), channel_id=1, source_target_pairs={{0,1},{1,0},{2,3},{3,2},{4,5},{5,4},{6,7},{7,6},{8,9},{9,8},{10,11... | collective-permute-start | bytes 393224 | tf_op jit(solution)/shard_map/ppermute | solution.py:619
  38.9 5.0 collective-permute-start.2
  39.3 5.9 %collective-permute-start.4 = (bf16[64,1024]{1,0:T(8,128)(2,1)S(1)}, bf16[64,1024]{1,0:T(8,128)(2,1)S(1)}, u32[]{:S(2)}, u32[]{:S(2)}) collective-permute-start(bf16[64,1024]{1,0:T(8,128)(2,1)S(1)} %collective-permute-done.3.refs_4_), channel_id=1, source_target_pairs={{0,1},{1,0},{2,3},{3,2},{4,5},{5,4},{6,7},{7,6},{8,9},{9,8},{10,11... | collective-permute-start | bytes 393224 | tf_op jit(solution)/shard_map/ppermute | solution.py:619
  65.4 24.4 %collective-permute-start.8 = (bf16[272,1024]{1,0:T(8,128)(2,1)}, bf16[272,1024]{1,0:T(8,128)(2,1)S(1)}, u32[]{:S(2)}, u32[]{:S(2)}) collective-permute-start(bf16[272,1024]{1,0:T(8,128)(2,1)} %get-tuple-element.91.xa_ref.xg_ref), channel_id=1, source_target_pairs={{0,2},{1,3},{2,4},{3,5},{4,6},{5,7},{6,0},{7,1},{8,10},{9,11},{10,... | collective-permute-start | bytes 1671176 | tf_op jit(solution)/shard_map/ppermute | solution.py:616
  65.6 24.2 %collective-permute-start.7 = (bf16[272,1024]{1,0:T(8,128)(2,1)}, bf16[272,1024]{1,0:T(8,128)(2,1)S(1)}, u32[]{:S(2)}, u32[]{:S(2)}) collective-permute-start(bf16[272,1024]{1,0:T(8,128)(2,1)} %get-tuple-element.91.xa_ref.xg_ref), channel_id=1, source_target_pairs={{0,1},{1,0},{2,3},{3,2},{4,5},{5,4},{6,7},{7,6},{8,9},{9,8},{10,11... | collective-permute-start | bytes 1671176 | tf_op jit(solution)/shard_map/ppermute | solution.py:619
  91.4 36.3 %collective-permute-start.10 = (bf16[272,1024]{1,0:T(8,128)(2,1)}, bf16[272,1024]{1,0:T(8,128)(2,1)S(1)}, u32[]{:S(2)}, u32[]{:S(2)}) collective-permute-start(bf16[272,1024]{1,0:T(8,128)(2,1)} %after.9.tied_ref.xa_ref), channel_id=1, source_target_pairs={{0,2},{1,3},{2,4},{3,5},{4,6},{5,7},{6,0},{7,1},{8,10},{9,11},{10,... | collective-permute-start | bytes 1671176 | tf_op jit(solution)/shard_map/ppermute | solution.py:616
  91.4 38.0 %collective-permute-start.9 = (bf16[272,1024]{1,0:T(8,128)(2,1)}, bf16[272,1024]{1,0:T(8,128)(2,1)S(1)}, u32[]{:S(2)}, u32[]{:S(2)}) collective-permute-start(bf16[272,1024]{1,0:T(8,128)(2,1)} %after.9.tied_ref.xa_ref), channel_id=1, source_target_pairs={{0,1},{1,0},{2,3},{3,2},{4,5},{5,4},{6,7},{7,6},{8,9},{9,8},{10,11... | collective-permute-start | bytes 1671176 | tf_op jit(solution)/shard_map/ppermute | solution.py:619
  128.5 19.3 %collective-permute-start.12 = (bf16[272,1024]{1,0:T(8,128)(2,1)}, bf16[272,1024]{1,0:T(8,128)(2,1)S(1)}, u32[]{:S(2)}, u32[]{:S(2)}) collective-permute-start(bf16[272,1024]{1,0:T(8,128)(2,1)} %after.10.rest_1_.xa_ref), channel_id=1, source_target_pairs={{0,2},{1,3},{2,4},{3,5},{4,6},{5,7},{6,0},{7,1},{8,10},{9,11},{10,... | collective-permute-start | bytes 1671176 | tf_op jit(solution)/shard_map/ppermute | solution.py:616
  129.4 18.5 %collective-permute-start.11 = (bf16[272,1024]{1,0:T(8,128)(2,1)}, bf16[272,1024]{1,0:T(8,128)(2,1)S(1)}, u32[]{:S(2)}, u32[]{:S(2)}) collective-permute-start(bf16[272,1024]{1,0:T(8,128)(2,1)} %after.10.rest_1_.xa_ref), channel_id=1, source_target_pairs={{0,1},{1,0},{2,3},{3,2},{4,5},{5,4},{6,7},{7,6},{8,9},{9,8},{10,11... | collective-permute-start | bytes 1671176 | tf_op jit(solution)/shard_map/ppermute | solution.py:619
  145.9 17.3 %collective-permute-start.14 = (bf16[272,1024]{1,0:T(8,128)(2,1)S(1)}, bf16[272,1024]{1,0:T(8,128)(2,1)S(1)}, u32[]{:S(2)}, u32[]{:S(2)}) collective-permute-start(bf16[272,1024]{1,0:T(8,128)(2,1)S(1)} %get-tuple-element.105), channel_id=1, source_target_pairs={{0,1},{1,0},{2,3},{3,2},{4,5},{5,4},{6,7},{7,6},{8,9},{9,8},{10,11... | collective-permute-start | bytes 1671176 | tf_op jit(solution)/shard_map/ppermute | solution.py:619
  147.9 25.5 %collective-permute-start.13 = (bf16[272,1024]{1,0:T(8,128)(2,1)S(1)}, bf16[272,1024]{1,0:T(8,128)(2,1)S(1)}, u32[]{:S(2)}, u32[]{:S(2)}) collective-permute-start(bf16[272,1024]{1,0:T(8,128)(2,1)S(1)} %collective-permute-done.12.rest_5_.xa_ref), channel_id=1, source_target_pairs={{0,1},{1,0},{2,3},{3,2},{4,5},{5,4},{6,7},{7,6},{8,9},{9,8},{10,11... | collective-permute-start | bytes 1671176 | tf_op jit(solution)/shard_map/ppermute | solution.py:619
  161.1 28.2 %collective-permute-start.15 = (bf16[272,1024]{1,0:T(8,128)(2,1)S(1)}, bf16[272,1024]{1,0:T(8,128)(2,1)S(1)}, u32[]{:S(2)}, u32[]{:S(2)}) collective-permute-start(bf16[272,1024]{1,0:T(8,128)(2,1)S(1)} %get-tuple-element.112), channel_id=1, source_target_pairs={{0,1},{1,0},{2,3},{3,2},{4,5},{5,4},{6,7},{7,6},{8,9},{9,8},{10,11... | collective-permute-start | bytes 1671176 | tf_op jit(solution)/shard_map/ppermute | solution.py:619
  187.4 23.5 %collective-permute-start.17 = (bf16[272,1024]{1,0:T(8,128)(2,1)S(1)}, bf16[272,1024]{1,0:T(8,128)(2,1)S(1)}, u32[]{:S(2)}, u32[]{:S(2)}) collective-permute-start(bf16[272,1024]{1,0:T(8,128)(2,1)S(1)} %get-tuple-element.116), channel_id=1, source_target_pairs={{0,1},{1,0},{2,3},{3,2},{4,5},{5,4},{6,7},{7,6},{8,9},{9,8},{10,11... | collective-permute-start | bytes 1671176 | tf_op jit(solution)/shard_map/ppermute | solution.py:619
  207.4 10.0 %collective-permute-start.19 = (bf16[272,1024]{1,0:T(8,128)(2,1)S(1)}, bf16[272,1024]{1,0:T(8,128)(2,1)S(1)}, u32[]{:S(2)}, u32[]{:S(2)}) collective-permute-start(bf16[272,1024]{1,0:T(8,128)(2,1)S(1)} %get-tuple-element.118), channel_id=1, source_target_pairs={{0,1},{1,0},{2,3},{3,2},{4,5},{5,4},{6,7},{7,6},{8,9},{9,8},{10,11... | collective-permute-start | bytes 1671176 | tf_op jit(solution)/shard_map/ppermute | solution.py:619
  208.0 16.0 %collective-permute-start.16 = (bf16[272,1024]{1,0:T(8,128)(2,1)S(1)}, bf16[272,1024]{1,0:T(8,128)(2,1)S(1)}, u32[]{:S(2)}, u32[]{:S(2)}) collective-permute-start(bf16[272,1024]{1,0:T(8,128)(2,1)S(1)} %add_convert_fusion.11.rest_4_), channel_id=1, source_target_pairs={{0,6},{1,7},{2,0},{3,1},{4,2},{5,3},{6,4},{7,5},{8,14},{9,15},{10,... | collective-permute-start | bytes 1671176 | tf_op jit(solution)/shard_map/ppermute | solution.py:616
  211.1 31.7 %collective-permute-start.18 = (bf16[272,1024]{1,0:T(8,128)(2,1)S(1)}, bf16[272,1024]{1,0:T(8,128)(2,1)S(1)}, u32[]{:S(2)}, u32[]{:S(2)}) collective-permute-start(bf16[272,1024]{1,0:T(8,128)(2,1)S(1)} %add_convert_fusion.10.tied_ref), channel_id=1, source_target_pairs={{0,4},{1,5},{2,6},{3,7},{4,0},{5,1},{6,2},{7,3},{8,12},{9,13},{10,... | collective-permute-start | bytes 1671176 | tf_op jit(solution)/shard_map/ppermute | solution.py:616
  259.3 34.5 %collective-permute-start.28 = (bf16[3,3,512,512]{3,2,1,0:T(8,128)(2,1)}, bf16[3,3,512,512]{3,2,1,0:T(8,128)(2,1)}, u32[]{:S(2)}, u32[]{:S(2)}) collective-permute-start(bf16[3,3,512,512]{3,2,1,0:T(8,128)(2,1)} %get-tuple-element.148), channel_id=1, source_target_pairs={{0,8},{8,0},{16,24},{24,16},{1,9},{9,1},{17,25},{25,17},{2,10},{10... | collective-permute-start | bytes 14155784 | tf_op jit(solution)/shard_map/ppermute | solution.py:623
  259.3 28.8 %collective-permute-start.30 = (bf16[1,3,512,512]{3,2,1,0:T(8,128)(2,1)}, bf16[1,3,512,512]{3,2,1,0:T(8,128)(2,1)}, u32[]{:S(2)}, u32[]{:S(2)}) collective-permute-start(bf16[1,3,512,512]{3,2,1,0:T(8,128)(2,1)} %get-tuple-element.152), channel_id=1, source_target_pairs={{0,8},{8,0},{16,24},{24,16},{1,9},{9,1},{17,25},{25,17},{2,10},{10... | collective-permute-start | bytes 4718600 | tf_op jit(solution)/shard_map/ppermute | solution.py:623
  259.8 17.3 %collective-permute-start.20 = (bf16[272,1024]{1,0:T(8,128)(2,1)S(1)}, bf16[272,1024]{1,0:T(8,128)(2,1)S(1)}, u32[]{:S(2)}, u32[]{:S(2)}) collective-permute-start(bf16[272,1024]{1,0:T(8,128)(2,1)S(1)} %copy-done.48), channel_id=1, source_target_pairs={{0,2},{1,3},{2,4},{3,5},{4,6},{5,7},{6,0},{7,1},{8,10},{9,11},{10,... | collective-permute-start | bytes 1671176 | tf_op jit(solution)/shard_map/ppermute | solution.py:616
  279.3 55.5 %collective-permute-start.22 = (bf16[256,1024]{1,0:T(8,128)(2,1)}, bf16[256,1024]{1,0:T(8,128)(2,1)}, u32[]{:S(2)}, u32[]{:S(2)}) collective-permute-start(bf16[256,1024]{1,0:T(8,128)(2,1)} %get-tuple-element.136), channel_id=1, source_target_pairs={{0,1},{1,0},{2,3},{3,2},{4,5},{5,4},{6,7},{7,6},{8,9},{9,8},{10,11... | collective-permute-start | bytes 1572872 | tf_op jit(solution)/shard_map/ppermute | solution.py:619
  280.5 50.6 %collective-permute-start.24 = (bf16[256,1024]{1,0:T(8,128)(2,1)}, bf16[256,1024]{1,0:T(8,128)(2,1)}, u32[]{:S(2)}, u32[]{:S(2)}) collective-permute-start(bf16[256,1024]{1,0:T(8,128)(2,1)} %get-tuple-element.138), channel_id=1, source_target_pairs={{0,1},{1,0},{2,3},{3,2},{4,5},{5,4},{6,7},{7,6},{8,9},{9,8},{10,11... | collective-permute-start | bytes 1572872 | tf_op jit(solution)/shard_map/ppermute | solution.py:619
  281.4 45.9 %collective-permute-start.26 = (bf16[256,1024]{1,0:T(8,128)(2,1)}, bf16[256,1024]{1,0:T(8,128)(2,1)}, u32[]{:S(2)}, u32[]{:S(2)}) collective-permute-start(bf16[256,1024]{1,0:T(8,128)(2,1)} %get-tuple-element.140), channel_id=1, source_target_pairs={{0,1},{1,0},{2,3},{3,2},{4,5},{5,4},{6,7},{7,6},{8,9},{9,8},{10,11... | collective-permute-start | bytes 1572872 | tf_op jit(solution)/shard_map/ppermute | solution.py:619
  292.2 46.4 %collective-permute-start.31 = (bf16[3,512,512]{2,1,0:T(8,128)(2,1)}, bf16[3,512,512]{2,1,0:T(8,128)(2,1)}, u32[]{:S(2)}, u32[]{:S(2)}) collective-permute-start(bf16[3,512,512]{2,1,0:T(8,128)(2,1)} %fusion.1), channel_id=1, source_target_pairs={{0,16},{8,24},{16,0},{24,8},{1,17},{9,25},{17,1},{25,9},{2,18},{10... | collective-permute-start | bytes 4718600 | tf_op jit(solution)/shard_map/ppermute | solution.py:623
  299.8 76.9 %collective-permute-start.29 = (bf16[3,512,512]{2,1,0:T(8,128)(2,1)}, bf16[3,512,512]{2,1,0:T(8,128)(2,1)}, u32[]{:S(2)}, u32[]{:S(2)}) collective-permute-start(bf16[3,512,512]{2,1,0:T(8,128)(2,1)} %get-tuple-element.172), channel_id=1, source_target_pairs={{0,16},{8,24},{16,0},{24,8},{1,17},{9,25},{17,1},{25,9},{2,18},{10... | collective-permute-start | bytes 4718600 | tf_op jit(solution)/shard_map/ppermute | solution.py:623
  323.6 27.0 %all-to-all-start.2 = ((bf16[2,256,1024]{2,1,0:T(8,128)(2,1)}), bf16[2,256,1024]{2,1,0:T(8,128)(2,1)S(1)}, u32[]{:S(2)}, u32[]{:S(2)}) async-start(bf16[2,256,1024]{2,1,0:T(8,128)(2,1)} %get-tuple-element.149), calls=%async_computation.2 | async-start | bytes 2097152 | tf_op jit(solution)/shard_map/all_to_all | solution.py:907
  327.3 83.1 %collective-permute-start.32 = (bf16[3,512,512]{2,1,0:T(8,128)(2,1)}, bf16[3,512,512]{2,1,0:T(8,128)(2,1)}, u32[]{:S(2)}, u32[]{:S(2)}) collective-permute-start(bf16[3,512,512]{2,1,0:T(8,128)(2,1)} %get-tuple-element.171), channel_id=1, source_target_pairs={{0,16},{8,24},{16,0},{24,8},{1,17},{9,25},{17,1},{25,9},{2,18},{10... | collective-permute-start | bytes 4718600 | tf_op jit(solution)/shard_map/ppermute | solution.py:623
  331.1 116.2 %collective-permute-start.38 = (bf16[3,512,512]{2,1,0:T(8,128)(2,1)}, bf16[3,512,512]{2,1,0:T(8,128)(2,1)}, u32[]{:S(2)}, u32[]{:S(2)}) collective-permute-start(bf16[3,512,512]{2,1,0:T(8,128)(2,1)} %get-tuple-element.170), channel_id=1, source_target_pairs={{0,16},{8,24},{16,0},{24,8},{1,17},{9,25},{17,1},{25,9},{2,18},{10... | collective-permute-start | bytes 4718600 | tf_op jit(solution)/shard_map/ppermute | solution.py:623
  334.9 44.4 %collective-permute-start.21 = (bf16[256,1024]{1,0:T(8,128)(2,1)}, bf16[256,1024]{1,0:T(8,128)(2,1)}, u32[]{:S(2)}, u32[]{:S(2)}) collective-permute-start(bf16[256,1024]{1,0:T(8,128)(2,1)} %get-tuple-element.134), channel_id=1, source_target_pairs={{0,1},{1,0},{2,3},{3,2},{4,5},{5,4},{6,7},{7,6},{8,9},{9,8},{10,11... | collective-permute-start | bytes 1572872 | tf_op jit(solution)/shard_map/ppermute | solution.py:619
  338.5 42.9 %collective-permute-start.23 = (bf16[256,1024]{1,0:T(8,128)(2,1)}, bf16[256,1024]{1,0:T(8,128)(2,1)}, u32[]{:S(2)}, u32[]{:S(2)}) collective-permute-start(bf16[256,1024]{1,0:T(8,128)(2,1)} %add_convert_fusion.17), channel_id=1, source_target_pairs={{0,6},{1,7},{2,0},{3,1},{4,2},{5,3},{6,4},{7,5},{8,14},{9,15},{10,... | collective-permute-start | bytes 1572872 | tf_op jit(solution)/shard_map/ppermute | solution.py:616
  357.7 94.8 %all-to-all-start.3 = ((bf16[4,64,1024]{2,1,0:T(8,128)(2,1)}), bf16[4,64,1024]{2,1,0:T(8,128)(2,1)}, u32[]{:S(2)}, u32[]{:S(2)}) async-start(bf16[4,64,1024]{2,1,0:T(8,128)(2,1)} %bitcast.61), calls=%async_computation.3 | async-start | bytes 1048576 | tf_op jit(solution)/shard_map/all_to_all | solution.py:932
  376.7 72.6 %collective-permute-start.25 = (bf16[256,1024]{1,0:T(8,128)(2,1)}, bf16[256,1024]{1,0:T(8,128)(2,1)S(1)}, u32[]{:S(2)}, u32[]{:S(2)}) collective-permute-start(bf16[256,1024]{1,0:T(8,128)(2,1)} %add_convert_fusion.16), channel_id=1, source_target_pairs={{0,4},{1,5},{2,6},{3,7},{4,0},{5,1},{6,2},{7,3},{8,12},{9,13},{10,... | collective-permute-start | bytes 1572872 | tf_op jit(solution)/shard_map/ppermute | solution.py:616
  379.3 70.5 %collective-permute-start.27 = (bf16[256,1024]{1,0:T(8,128)(2,1)S(1)}, bf16[256,1024]{1,0:T(8,128)(2,1)S(1)}, u32[]{:S(2)}, u32[]{:S(2)}) collective-permute-start(bf16[256,1024]{1,0:T(8,128)(2,1)S(1)} %copy-done.50), channel_id=1, source_target_pairs={{0,2},{1,3},{2,4},{3,5},{4,6},{5,7},{6,0},{7,1},{8,10},{9,11},{10,... | collective-permute-start | bytes 1572872 | tf_op jit(solution)/shard_map/ppermute | solution.py:616
  381.4 98.8 %collective-permute-start.42 = (bf16[3,512,512]{2,1,0:T(8,128)(2,1)}, bf16[3,512,512]{2,1,0:T(8,128)(2,1)}, u32[]{:S(2)}, u32[]{:S(2)}) collective-permute-start(bf16[3,512,512]{2,1,0:T(8,128)(2,1)} %add_convert_fusion.mine_ref), channel_id=1, source_target_pairs={{0,8},{8,0},{16,24},{24,16},{1,9},{9,1},{17,25},{25,17},{2,10},{10... | collective-permute-start | bytes 4718600 | tf_op jit(solution)/shard_map/ppermute | solution.py:623
  410.4 75.4 %collective-permute-start.41 = (bf16[3,512,512]{2,1,0:T(8,128)(2,1)S(1)}, bf16[3,512,512]{2,1,0:T(8,128)(2,1)}, u32[]{:S(2)}, u32[]{:S(2)}) collective-permute-start(bf16[3,512,512]{2,1,0:T(8,128)(2,1)S(1)} %add_convert_fusion.1.mine_ref), channel_id=1, source_target_pairs={{0,8},{8,0},{16,24},{24,16},{1,9},{9,1},{17,25},{25,17},{2,10},{10... | collective-permute-start | bytes 4718600 | tf_op jit(solution)/shard_map/ppermute | solution.py:623
  447.4 42.8 %collective-permute-start.40 = (bf16[3,512,512]{2,1,0:T(8,128)(2,1)}, bf16[3,512,512]{2,1,0:T(8,128)(2,1)}, u32[]{:S(2)}, u32[]{:S(2)}) collective-permute-start(bf16[3,512,512]{2,1,0:T(8,128)(2,1)} %add_convert_fusion.2.mine_ref), channel_id=1, source_target_pairs={{0,8},{8,0},{16,24},{24,16},{1,9},{9,1},{17,25},{25,17},{2,10},{10... | collective-permute-start | bytes 4718600 | tf_op jit(solution)/shard_map/ppermute | solution.py:623
  449.3 45.8 %collective-permute-start.39 = (bf16[3,512,512]{2,1,0:T(8,128)(2,1)S(1)}, bf16[3,512,512]{2,1,0:T(8,128)(2,1)}, u32[]{:S(2)}, u32[]{:S(2)}) collective-permute-start(bf16[3,512,512]{2,1,0:T(8,128)(2,1)S(1)} %add_convert_fusion.3.mine_ref), channel_id=1, source_target_pairs={{0,8},{8,0},{16,24},{24,16},{1,9},{9,1},{17,25},{25,17},{2,10},{10... | collective-permute-start | bytes 4718600 | tf_op jit(solution)/shard_map/ppermute | solution.py:623
  452.4 33.4 %all-to-all-start.1 = ((bf16[4,64,1024]{2,1,0:T(8,128)(2,1)}), bf16[4,64,1024]{2,1,0:T(8,128)(2,1)}, u32[]{:S(2)}, u32[]{:S(2)}) async-start(bf16[4,64,1024]{2,1,0:T(8,128)(2,1)} %bitcast.70), calls=%async_computation.1 | async-start | bytes 1048576 | tf_op jit(solution)/shard_map/all_to_all | solution.py:932
  456.8 4.2 collective-permute-start.33
  461.7 6.7 %collective-permute-start.34 = (f32[8,1024]{1,0:T(8,128)S(1)}, f32[8,1024]{1,0:T(8,128)S(1)}, u32[]{:S(2)}, u32[]{:S(2)}) collective-permute-start(f32[8,1024]{1,0:T(8,128)S(1)} %add.280), channel_id=1, source_target_pairs={{0,2},{1,3},{2,0},{3,1},{4,6},{5,7},{6,4},{7,5},{8,10},{9,11},{10,... | collective-permute-start | bytes 98312 | tf_op jit(solution)/shard_map/ppermute | solution.py:619
  468.4 8.2 %collective-permute-start.35 = (f32[8,1024]{1,0:T(8,128)S(1)}, f32[8,1024]{1,0:T(8,128)S(1)}, u32[]{:S(2)}, u32[]{:S(2)}) collective-permute-start(f32[8,1024]{1,0:T(8,128)S(1)} %add.281), channel_id=1, source_target_pairs={{0,4},{1,5},{2,6},{3,7},{4,0},{5,1},{6,2},{7,3},{8,12},{9,13},{10,... | collective-permute-start | bytes 98312 | tf_op jit(solution)/shard_map/ppermute | solution.py:619
  478.8 6.4 %collective-permute-start.37 = (f32[8,1024]{1,0:T(8,128)S(1)}, f32[8,1024]{1,0:T(8,128)S(1)}, u32[]{:S(2)}, u32[]{:S(2)}) collective-permute-start(f32[8,1024]{1,0:T(8,128)S(1)} %add.283), channel_id=1, source_target_pairs={{0,16},{8,24},{16,0},{24,8},{1,17},{9,25},{17,1},{25,9},{2,18},{10... | collective-permute-start | bytes 98312 | tf_op jit(solution)/shard_map/ppermute | solution.py:623
  (64 other events, 762.0 us)
Sparse Core Ops, SparseCore 0:
  10.1 98.0 all-gather.2
  323.7 214.0 all-reduce.1

commit v3 on v2

--- a/solution.py
+++ b/solution.py
@@ -236,52 +236,25 @@
     return slot == slot_row
 
 
-def upstream_kernel(named_ref, u_ref, wd_ref, tied_ref, slot_ref, ug_ref, v_ref):
-    experts = wd_ref.shape[0]
-    tokens = named_ref.shape[2]
-    width = wd_ref.shape[2]
-    rows = tokens * MOST // BLOCK
-    earlier = lax.broadcasted_iota(jnp.int32, (tokens, tokens), 0)
-    later = lax.broadcasted_iota(jnp.int32, (tokens, tokens), 1)
-    before = (earlier < later).astype(F32).astype(BF16)
-    for c in range(PAIR):
-        named = named_ref[c]
-        rank = mul(named.astype(BF16), before)
-        slot_ref[c] = jnp.where(named > 0, rank, -1.0)
-
-    def expert_step(e, carry):
-        at = pl.ds(pl.multiple_of(e * rows, rows), rows)
-        both = []
-        for c in range(PAIR):
-            pick = one_hot(slot_ref[c, pl.ds(e, 1), :], rows).astype(F32).astype(BF16)
-            picked = mul(pick, u_ref[:, c, 0].reshape(tokens, width)).astype(BF16)
-            ug_ref[c, at, :] = picked
-            both.append(picked)
-        product = mul(jnp.concatenate(both, axis=0), wd_ref[e], NT)
-        for c in range(PAIR):
-            v_ref[c, at, :] = product[c * rows : (c + 1) * rows]
-        return carry
-
-    lax.fori_loop(0, experts, expert_step, 0)
-
-
 def expert_kernel(
     kept,
     info_ref,
     xa_ref,
     xb_ref,
-    slot_ref,
-    v_ref,
+    named_ref,
+    u_ref,
     wg_ref,
     wu_ref,
     wd_ref,
     *rest,
 ):
-    (dxa_ref, dxb_ref, ya_ref, yb_ref, xs_ref, hs_ref, dg_ref, du_ref) = rest[kept : kept + 8]
-    (dxs_ref, ys_ref, pick_ref, gates_ref, back_ref) = rest[kept + 8 :]
+    (dxa_ref, dxb_ref) = rest[kept : kept + 2]
+    (y_ref, xs_ref, us_ref, hs_ref, dg_ref, du_ref) = rest[kept + 2 : kept + 8]
+    (dxs_ref, ys_ref, pick_ref, slot_ref, gates_ref, back_ref) = rest[kept + 8 :]
     e = pl.program_id(0)
     experts = pl.num_programs(0)
-    tokens = slot_ref.shape[2]
+    tokens = named_ref.shape[2]
+    width = xa_ref.shape[1]
     rows = tokens * MOST // BLOCK
     places = [(info_ref[0] + c) % PAIR for c in range(PAIR)]
     sources = (xa_ref, xb_ref)
@@ -289,19 +262,28 @@
     @pl.when(e == 0)
     def _():
         back_ref[...] = jnp.zeros_like(back_ref)
+        earlier = lax.broadcasted_iota(jnp.int32, (tokens, tokens), 0)
+        later = lax.broadcasted_iota(jnp.int32, (tokens, tokens), 1)
+        before = (earlier < later).astype(F32).astype(BF16)
+        for c in range(PAIR):
+            named = named_ref[places[c]]
+            slot_ref[c] = jnp.where(named > 0, mul(named.astype(BF16), before), -1.0)
 
     at = pl.ds(pl.multiple_of(e * rows, rows), rows)
     number = info_ref[1] * experts + e
     row = lax.rem(number, 8)
     lanes = pl.ds(pl.multiple_of(lax.div(number, 8) * tokens, tokens), tokens)
-    entering, gate = [], []
+    entering, leaving, gate = [], [], []
     for c in range(PAIR):
-        hot = one_hot(slot_ref[places[c], pl.ds(e, 1), :], rows)
+        hot = one_hot(slot_ref[c, pl.ds(e, 1), :], rows)
         pick = hot.astype(F32).astype(BF16)
         pick_ref[c, at, :] = pick
         picked = mul(pick, sources[c][:tokens, :]).astype(BF16)
         xs_ref[places[c]] = picked
         entering.append(picked)
+        picked = mul(pick, u_ref[:, places[c], 0].reshape(tokens, width)).astype(BF16)
+        us_ref[places[c]] = picked
+        leaving.append(picked)
         sent = sources[c][tokens:, lanes].astype(F32)
         gates_ref[...] = sent[:8] + sent[8:]
         gate.append(jnp.sum(jnp.where(hot, gates_ref[pl.ds(row, 1), :], 0.0), axis=1, keepdims=True))
@@ -309,10 +291,10 @@
     gate = jnp.concatenate(gate, axis=0)
     gate_pre = mul(entering, wg_ref[0])
     up_pre = mul(entering, wu_ref[0])
+    product = mul(jnp.concatenate(leaving, axis=0), wd_ref[0], NT)
     share = 1.0 / (1.0 + jnp.exp(-gate_pre))
     silu = gate_pre * share
     hidden = silu * up_pre
-    product = jnp.concatenate([v_ref[places[c]] for c in range(PAIR)], axis=0)
     grad_gate = jnp.sum(hidden * product, axis=1, keepdims=True)
     grad_act = gate * product
     grad_gate_pre = (grad_act * up_pre * share * (1.0 + gate_pre * (1.0 - share))).astype(BF16)
@@ -327,7 +309,7 @@
         du_ref[places[c]] = grad_up_pre[part]
         dxs_ref[c, at, :] = grad_rows[part]
         ys_ref[c, at, :] = out_rows[part]
-        hot = one_hot(slot_ref[places[c], pl.ds(e, 1), :], rows)
+        hot = one_hot(slot_ref[c, pl.ds(e, 1), :], rows)
         returned = jnp.sum(jnp.where(hot, grad_gate[part], 0.0), axis=0, keepdims=True)
         high = returned.astype(BF16).astype(F32)
         back_ref[c, pl.ds(row, 1), lanes] = high
@@ -335,15 +317,14 @@
 
     @pl.when(e == experts - 1)
     def _():
-        for c, (dx_ref, y_ref) in enumerate(((dxa_ref, ya_ref), (dxb_ref, yb_ref))):
+        for c, dx_ref in enumerate((dxa_ref, dxb_ref)):
             dx_ref[:tokens, :] = mul(pick_ref[c], dxs_ref[c], TN).astype(BF16)
             dx_ref[tokens:, :] = back_ref[c].astype(BF16)
-            y_ref[...] = mul(pick_ref[c], ys_ref[c], TN).astype(BF16)
-
-
-def expert_grads_kernel(
-    info_ref, xs_ref, us_ref, hs_ref, dg_ref, du_ref, earlier_ref, tied_ref, sent_ref, keep_ref, send_ref
-):
+            y_ref[places[c]] = mul(pick_ref[c], ys_ref[c], TN).astype(BF16)
+
+
+def expert_grads_kernel(info_ref, xs_ref, us_ref, hs_ref, dg_ref, du_ref, *rest):
+    keep_ref, send_ref = rest[-2:]
     core = info_ref[3]
     group, rows, width = xs_ref.shape
     inner = hs_ref.shape[2]
@@ -604,7 +585,6 @@
     same_member = [[r * members + m for r in range(rows_here)] for m in range(members)]
     same_row = [[r * members + m for m in range(members)] for r in range(rows_here)]
     slots = tokens * MOST // BLOCK
-    groups = shards // PAIR
 
     meta = jnp.concatenate(
         [positions.reshape(1, tokens), expert_ids.reshape(tokens, TOPK).T], axis=0
@@ -652,6 +632,10 @@
     me_row = jnp.stack([member, me] + places).astype(jnp.int32)
     upstream = lax.all_gather(out_grad, "seq", axis=0, tiled=False)
     upstream = upstream.reshape(rows_here, members, rows_here, block, width)
+    stored = [
+        pltpu.with_memory_space_constraint(v, pltpu.HBM)
+        for v in (upstream, gate_weight, up_weight, down_weight)
+    ]
 
     meta = meta.reshape(rows_here, members, TOPK + 1, rows_here, block)
     row_meta = lax.dynamic_index_in_dim(meta, row, 3, keepdims=False)
@@ -704,60 +688,28 @@
         router,
     )
 
-    constant = lambda shape: pl.BlockSpec(
-        shape, lambda i: (0,) * len(shape), pipeline_mode=pl.Buffered(1)
-    )
-    grouped = lambda *shape: pl.BlockSpec((PAIR,) + shape, lambda i: (i,) + (0,) * len(shape))
     per_row = members // PAIR
     one_on = onward(xg, 1)
     beside = [across(xg, other) for other in range(1, members)]
     one_on = after([one_on], *beside)[0]
     sets = [[xg] + beside, [one_on] + [across(one_on, other) for other in range(1, members)]]
     two_on = onward(one_on, 1)
-    slot, us, product = pl.pallas_call(
-        upstream_kernel,
-        grid=(groups,),
-        out_shape=[
-            struct((shards, 8, tokens), F32),
-            struct((shards, experts * slots, width), BF16),
-            struct((shards, experts * slots, hidden), F32),
-        ],
-        in_specs=[
-            grouped(8, tokens),
-            pl.BlockSpec(
-                (rows_here, PAIR, 1, block, width),
-                lambda i: (0, i % per_row, i // per_row, 0, 0),
-            ),
-            constant((experts, hidden, width)),
-        ]
-        + [pl.BlockSpec(memory_space=pl.ANY)],
-        out_specs=[
-            grouped(8, tokens),
-            grouped(experts * slots, width),
-            grouped(experts * slots, hidden),
-        ],
-        compiler_params=params(48),
-        cost_estimate=took(15.5),
-        name="upstream",
-    )(named, upstream, down_weight, one_on)
-
     wide, narrow = experts * slots, hidden
     kept = []
-    values = after([two_on], slot)[0]
-    for k in range(2, rows_here):
-        values = onward(values, 1) if k > 2 else values
-        sets.append([values] + [across(values, other) for other in range(1, members)])
     order = list(range(rows_here))
-    dx_parts, y_parts, dx_sums = [[] for _ in sets], [[] for _ in sets], []
+    dx_parts, dx_sums = [[] for _ in order], []
     for k in order:
+        if k == 1:
+            values = after([two_on], dx_parts[0][0])[0]
+            for i in range(2, rows_here):
+                values = onward(values, 1) if i > 2 else values
+                sets.append([values] + [across(values, other) for other in range(1, members)])
         group = sets[k]
-        tied = []
-        for later, member_of in ((k + 1, -1), (k + 2, 0)):
-            tied += [sets[later][member_of]] if later < rows_here else []
-        tied += dx_sums[k - 2 : k - 1] if k > 1 else []
+        tied = dx_sums[k - 2 : k - 1] if k > 1 else []
         for q in range(members // PAIR):
             pair = (row - k) % rows_here * per_row + ((member // PAIR) ^ q)
-            info = jnp.stack([member % PAIR, me, pair, core]).astype(jnp.int32)
+            info = [member % PAIR, me, pair, (row - k) % rows_here, (member // PAIR) ^ q]
+            info = jnp.stack(info).astype(jnp.int32)
             flat = lambda *shape: pl.BlockSpec(shape, lambda e, info: (0,) * len(shape))
             of_pair = lambda w: pl.BlockSpec((PAIR, slots, w), lambda e, info: (info[2], e, 0))
             of_expert = lambda a, b: pl.BlockSpec((1, a, b), lambda e, info: (e, 0, 0))
@@ -770,7 +722,10 @@
                         flat(tokens + PAD, width),
                         flat(tokens + PAD, width),
                         pl.BlockSpec((PAIR, 8, tokens), lambda e, info: (info[2], 0, 0)),
-                        of_pair(hidden),
+                        pl.BlockSpec(
+                            (rows_here, PAIR, 1, block, width),
+                            lambda e, info: (0, info[4], info[3], 0, 0),
+                        ),
                         of_expert(width, hidden),
                         of_expert(width, hidden),
                         of_expert(hidden, width),
@@ -779,8 +734,8 @@
                     out_specs=[
                         flat(tokens + PAD, width),
                         flat(tokens + PAD, width),
-                        flat(tokens, width),
-                        flat(tokens, width),
+                        pl.BlockSpec((PAIR, tokens, width), lambda e, info: (info[2], 0, 0)),
+                        of_pair(width),
                         of_pair(width),
                         of_pair(hidden),
                         of_pair(hidden),
@@ -790,6 +745,7 @@
                         pltpu.VMEM((PAIR, wide, width), BF16),
                         pltpu.VMEM((PAIR, wide, width), BF16),
                         pltpu.VMEM((PAIR, wide, tokens), BF16),
+                        pltpu.VMEM((PAIR, 8, tokens), F32),
                         pltpu.VMEM((8, tokens), F32),
                         pltpu.VMEM((PAIR, PAD, width), F32),
                     ],
@@ -797,48 +753,90 @@
                 out_shape=[
                     struct((tokens + PAD, width), BF16),
                     struct((tokens + PAD, width), BF16),
-                    struct((tokens, width), BF16),
-                    struct((tokens, width), BF16),
-                    struct((shards, wide, width), BF16),
-                    struct((shards, wide, hidden), BF16),
-                    struct((shards, wide, hidden), BF16),
-                    struct((shards, wide, hidden), BF16),
+                    pltpu.HBM((shards, tokens, width), BF16),
+                    pltpu.HBM((shards, wide, width), BF16),
+                    pltpu.HBM((shards, wide, width), BF16),
+                    pltpu.HBM((shards, wide, hidden), BF16),
+                    pltpu.HBM((shards, wide, hidden), BF16),
+                    pltpu.HBM((shards, wide, hidden), BF16),
                 ],
-                input_output_aliases={8 + i: 4 + i for i in range(len(kept))},
+                input_output_aliases={8 + i: 2 + i for i in range(len(kept))},
                 compiler_params=params(40),
-                cost_estimate=took(13.3),
+                cost_estimate=took(16),
                 name="experts",
-            )(info, group[2 * q], group[2 * q + 1], slot, product, gate_weight, up_weight, down_weight, *kept, *tied)
+            )(
+                info,
+                group[2 * q],
+                group[2 * q + 1],
+                named,
+                *stored,
+                *kept,
+                *tied,
+            )
             dx_parts[k] += outcome[:2]
-            y_parts[k] += outcome[2:4]
-            kept = outcome[4:]
+            kept = outcome[2:]
         dx_sums.append(joined(dx_parts[k]))
     sent = [dx_sums[0]] + [onward(dx_sums[k], rows_here - k) for k in range(1, rows_here)]
     dx_sum = add(*sent)
 
     info = jnp.stack([member % PAIR, me, me, core]).astype(jnp.int32)
     halves = (3, width // 2, hidden)
-    mine, keep = [], us
-    for first, count in ((0, 1), (1, experts - 1)):
-        if not count:
-            continue
-        one_expert = lambda w: pl.BlockSpec((shards, slots, w), lambda i, at=first: (0, at + i, 0))
-        half = pl.BlockSpec((1,) + halves, lambda i: (i, 0, 0, 0))
-        keep, send = pl.pallas_call(
-            expert_grads_kernel,
-            grid=(count,),
-            out_shape=[struct((count,) + halves, BF16)] * 2,
-            in_specs=[scalars(), one_expert(width), one_expert(width)]
-            + [one_expert(hidden)] * 3
-            + [pl.BlockSpec(memory_space=pl.ANY)] * 3,
-            out_specs=[half] * 2,
-            compiler_params=params(60),
-            cost_estimate=took(4.6 * count + 1.5),
-            name="expert_grads",
-        )(info, kept[0], us, *kept[1:], keep, dx_sums[2 if first == 0 else 3], sent[1 if first == 0 else 2])
-        received = row_swap(send, 1)
-        mine += [add(keep[i], received[i]) for i in range(count)]
-    queued = mine[-1]
+    one_expert = lambda w: pl.BlockSpec((shards, slots, w), lambda i: (0, i, 0))
+    half = pl.BlockSpec((1,) + halves, lambda i: (i, 0, 0, 0))
+    keep, send = pl.pallas_call(
+        expert_grads_kernel,
+        grid=(experts,),
+        out_shape=[struct((experts,) + halves, BF16)] * 2,
+        in_specs=[scalars(), one_expert(width), one_expert(width)]
+        + [one_expert(hidden)] * 3
+        + [pl.BlockSpec(memory_space=pl.ANY)] * 2,
+        out_specs=[half] * 2,
+        compiler_params=params(60),
+        cost_estimate=took(60),
+        name="expert_grads",
+    )(info, *kept[1:], dx_sums[2], dx_sums[3])
+    received = row_swap(after([send], dx_sum)[0], 1)
+    y_sum = lax.psum_scatter(
+        after([kept[0]], dx_sums[3])[0], "seq", scatter_dimension=0, tiled=False
+    )
+    own_upstream = lax.dynamic_index_in_dim(upstream, row, 2, keepdims=False)
+    own_upstream = lax.dynamic_index_in_dim(own_upstream, member, 1, keepdims=False)
+    own_upstream = own_upstream.reshape(tokens, width)
+    vectors, grad_mixed, grad_residual, gaz = pl.pallas_call(
+        middle_kernel,
+        out_shape=[
+            struct((EXTRA, width), BF16),
+            struct((tokens, width), BF16),
+            struct((tokens, width), F32),
+            struct((rows_here, TILES, 4 * BLOCK, LANES), BF16),
+        ],
+        in_specs=[whole()] * 8 + [pl.BlockSpec(memory_space=pl.ANY)],
+        out_specs=[whole()] * 4,
+        compiler_params=params(48),
+        cost_estimate=took(6),
+        name="middle",
+    )(dx_sum, own_upstream, xg, residual, gates, gain_two, router, output_weight, keep)
+
+    dq, dkv, weights = pl.pallas_call(
+        functools.partial(attention_back_kernel, members),
+        out_shape=[
+            struct((tokens, width), BF16),
+            struct((members, tokens, width), BF16),
+            struct((3 * width + EXTRA, width), BF16),
+        ],
+        in_specs=[scalars()] + [whole()] * 12 + [pl.BlockSpec(memory_space=pl.ANY)],
+        out_specs=[whole()] * 3,
+        scratch_shapes=[
+            pltpu.VMEM((length, inner), F32),
+            pltpu.VMEM((length, inner), F32),
+            pltpu.VMEM((length, width), BF16),
+        ],
+        compiler_params=params(58),
+        cost_estimate=took(21.5),
+        name="attention_back",
+    )(me_pair, qz, gaz, k_row, v_row, own_pos, cosine, sine, mix, own_mix, att, grad_mixed, vectors, vectors)
+    kept_half = after([keep], dq)[0]
+    mine = [add(kept_half[i], received[i]) for i in range(experts)]
     crossed = []
     for e in range(experts):
         bit = 2
@@ -863,47 +861,9 @@
             out_specs=[grad_spec(width, hidden), grad_spec(width, hidden), grad_spec(hidden, width)],
             input_output_aliases={3 + i: i for i in range(len(finished))},
             compiler_params=params(32),
-            cost_estimate=took(4.6),
+            cost_estimate=took(0.1),
             name="finish",
         )(info, mine[e], row_swap(mine[e], 1), *finished)
-    later = after([y for part in y_parts for y in part[1:]], dx_sum)
-    later = [later[k * (members - 1) : (k + 1) * (members - 1)] for k in range(rows_here)]
-    own_upstream = lax.dynamic_index_in_dim(upstream, row, 2, keepdims=False)
-    own_upstream = lax.dynamic_index_in_dim(own_upstream, member, 1, keepdims=False)
-    own_upstream = own_upstream.reshape(tokens, width)
-    vectors, grad_mixed, grad_residual, gaz = pl.pallas_call(
-        middle_kernel,
-        out_shape=[
-            struct((EXTRA, width), BF16),
-            struct((tokens, width), BF16),
-            struct((tokens, width), F32),
-            struct((rows_here, TILES, 4 * BLOCK, LANES), BF16),
-        ],
-        in_specs=[whole()] * 8 + [pl.BlockSpec(memory_space=pl.ANY)],
-        out_specs=[whole()] * 4,
-        compiler_params=params(48),
-        cost_estimate=took(6),
-        name="middle",
-    )(dx_sum, own_upstream, xg, residual, gates, gain_two, router, output_weight, dx_sums[0])
-
-    dq, dkv, weights = pl.pallas_call(
-        functools.partial(attention_back_kernel, members),
-        out_shape=[
-            struct((tokens, width), BF16),
-            struct((members, tokens, width), BF16),
-            struct((3 * width + EXTRA, width), BF16),
-        ],
-        in_specs=[scalars()] + [whole()] * 12 + [pl.BlockSpec(memory_space=pl.ANY)],
-        out_specs=[whole()] * 3,
-        scratch_shapes=[
-            pltpu.VMEM((length, inner), F32),
-            pltpu.VMEM((length, inner), F32),
-            pltpu.VMEM((length, width), BF16),
-        ],
-        compiler_params=params(58),
-        cost_estimate=took(21.5),
-        name="attention_back",
-    )(me_pair, qz, gaz, k_row, v_row, own_pos, cosine, sine, mix, own_mix, att, grad_mixed, vectors, vectors)
     dkv = lax.all_to_all(dkv, "seq", 0, 0, tiled=True, axis_index_groups=same_row)
     grad_in, first_part = pl.pallas_call(
         functools.partial(last_kernel, members),
@@ -911,7 +871,7 @@
         in_specs=[whole()] * 8 + [pl.BlockSpec(memory_space=pl.ANY)],
         out_specs=[whole()] * 2,
         compiler_params=params(48),
-        cost_estimate=took(3.1),
+        cost_estimate=took(0.1),
         name="last",
     )(dq, dkv, query_weight, key_weight, value_weight, own_in, grad_residual, gain_one, crossed[0])
 
@@ -924,9 +884,6 @@
     while bit < lax.axis_size("rows"):
         first_sum = first_sum + row_swap(first_sum, bit)
         bit *= 2
-    y_sum = scatter(
-        [joined([y, *rest]) for y, rest in zip(after([p[0] for p in y_parts], dq), later)]
-    )
     steps = [crossed[min(i, experts - 1)] for i in range(4)]
     hidden_out = after([(residual + y_sum.astype(F32)).astype(BF16)], steps[1])[0]
     back = lambda values: lax.all_to_all(

time: 567 us -> 591 us (1.042)
  starting transfers between devices: 70.1 us -> 112 us
  Pallas kernels: 162 us -> 151 us
  other arithmetic: 49.1 us -> 42.1 us
    ppermute x12 -> x11, waiting for transfers between devices: 74.3 us -> 120 us  [row_swap(): return lax.ppermute(values, 'rows', [(j, j ^ other) for j in range(count)])]
    psum x1, waiting for transfers between devices: 38.4 us -> 0.01 us  [local(): shared = lax.psum(weights, ('rows', 'seq'))]
    all_to_all x2, starting transfers between devices: 8.48 us -> 43.3 us  [local(): lax.all_to_all(values.reshape(rows_here, block, width), 'seq', 0, 0, tile...]
    pallas_call x3 -> x1, Pallas kernels: 39 us -> 19.2 us  [local(): pl.pallas_call(expert_grads_kernel, grid=(experts,), out_shape=[struct((e...]
    ppermute x19 -> x15, waiting for transfers between devices: 29.2 us -> 46.6 us  [across(): return lax.ppermute(values, 'seq', [(j, j ^ other) for j in range(shards)])]
    all_gather x1, waiting for transfers between devices: 14 us -> 1 us  [local(): upstream = lax.all_gather(out_grad, 'seq', axis=0, tiled=False)]
    all_to_all x1, waiting for transfers between devices: 10.9 us -> 0.01 us  [local(): lax.all_to_all(dkv, 'seq', 0, 0, tiled=True, axis_index_groups=same_row)]
    pallas_call x4, Pallas kernels: 53.8 us -> 62.9 us  [local(): pl.pallas_call(functools.partial(expert_kernel, len(kept) + len(tied)), g...]
  transfers between devices with their start and end apart: 49 -> 42, of which waited for: 18 -> 21; matrix products, arithmetic and copies ran while one was open for 9% -> 7% of each run, Pallas kernels for 26% -> 26%
where the time goes in v3:
time: 591 us; the launch traced here: 582 us
  waiting for transfers between devices  231 us (39%)
  Pallas kernels  151 us (26%)
  starting transfers between devices  112 us (19%)
  other arithmetic  42.1 us (7%)
  local copies, waits for them, and re-layouts  31 us (5%)
  between operations  14.8 us (3%)
    ppermute x11, waiting for transfers between devices, row_swap(): return lax.ppermute(values, 'rows', [(j, j ^ other) for j in range(count)])  120 us
    pallas_call x4, Pallas kernels, local(): pl.pallas_call(functools.partial(expert_kernel, len(kept) + len(tied)), g...  62.9 us
    ppermute x15, waiting for transfers between devices, across(): return lax.ppermute(values, 'seq', [(j, j ^ other) for j in range(shards)])  46.6 us
    ppermute x9, waiting for transfers between devices, onward(): return lax.ppermute(values, 'seq', [(j, to(j)) for j in range(shards)])  46.3 us
    all_to_all x2, starting transfers between devices, local(): lax.all_to_all(values.reshape(rows_here, block, width), 'seq', 0, 0, tile...  43.3 us
    ppermute x15, starting transfers between devices, across(): return lax.ppermute(values, 'seq', [(j, j ^ other) for j in range(shards)])  34.2 us
    convert_element_type x10, other arithmetic, add(): return sum((term.astype(F32) for term in terms)).astype(terms[0].dtype)  24.5 us
    pallas_call x1, Pallas kernels, local(): pl.pallas_call(functools.partial(attention_back_kernel, members), out_sha...  23.2 us
  transfers between devices with their start and end apart: 42, of which 21 were waited for; matrix products, arithmetic and copies ran while one was open for 7% of the time, Pallas kernels for 26%

profile of v3, /device:TPU:0, one launch (start us, length us, event | category | flops | bytes accessed | tf_op | source)
XLA Modules:
  0.0 581.6 jit_solution(4424424266387828908)
XLA Ops:
  12.1 7.3 %all-to-all-start = ((s32[8,9,256]{2,1,0:T(8,128)}), s32[8,9,256]{2,1,0:T(8,128)S(1)}, u32[]{:S(2)}, u32[]{:S(2)}) async-start(s32[8,9,256]{2,1,0:T(8,128)} %after.9), calls=%async_computation | async-start | bytes 262144 | tf_op jit(solution)/shard_map/all_to_all | solution.py:623
  21.4 2.4 collective-permute-start.3
  27.4 6.9 %all-to-all-done = s32[8,9,256]{2,1,0:T(8,128)S(1)} async-done(((s32[8,9,256]{2,1,0:T(8,128)}), s32[8,9,256]{2,1,0:T(8,128)S(1)}, u32[]{:S(2)}, u32[]{:S(2)}) %all-to-all-start) | async-done | bytes 73760 | tf_op jit(solution)/shard_map/all_to_all | solution.py:623
  36.9 7.9 %collective-permute-done.3.refs_4_ = bf16[64,1024]{1,0:T(8,128)(2,1)S(1)} collective-permute-done((bf16[64,1024]{1,0:T(8,128)(2,1)}, bf16[64,1024]{1,0:T(8,128)(2,1)S(1)}, u32[]{:S(2)}, u32[]{:S(2)}) %collective-permute-start.3) | collective-permute-done | bytes 131104 | tf_op jit(solution)/shard_map/ppermute | solution.py:596
  51.8 19.5 %front.1 = (bf16[512,1024]{1,0:T(8,128)(2,1)}, bf16[256,1024]{1,0:T(8,128)(2,1)}, bf16[4,4,256,128]{3,2,1,0:T(8,128)(2,1)}, bf16[512,512]{1,0:T(8,128)(2,1)}, bf...) custom-call(s32[10]{0:T(128)} %stack.109.me_ref, ...), custom_call_target="tpu_custom_call" | custom-call | flops 9749999616 | tf_op jit(solution)/shard_map/front/pallas_call | solution.py:655
  72.0 8.1 %collective-permute-start.7 = (bf16[272,1024]{1,0:T(8,128)(2,1)}, bf16[272,1024]{1,0:T(8,128)(2,1)S(1)}, u32[]{:S(2)}, u32[]{:S(2)}) collective-permute-start(bf16[272,1024]{1,0:T(8,128)(2,1)} %get-tuple-element.78.xa_ref.xg_ref), channel_id=1, source_target_pairs={{0,2},{1,3},{2,4},{3,5},{4,6},{5,7},{6,0},{7,1},{8,10},{9,11},{10,... | collective-permute-start | bytes 1671176 | tf_op jit(solution)/shard_map/ppermute | solution.py:596
  80.9 14.1 %collective-permute-done.8.refs_1_.xb_ref = bf16[272,1024]{1,0:T(8,128)(2,1)S(1)} collective-permute-done((bf16[272,1024]{1,0:T(8,128)(2,1)}, bf16[272,1024]{1,0:T(8,128)(2,1)S(1)}, u32[]{:S(2)}, u32[]{:S(2)}) %collective-permute-start.8) | collective-permute-done | bytes 557088 | tf_op jit(solution)/shard_map/ppermute | solution.py:599
  95.0 6.8 %collective-permute-done.7.refs_0_ = bf16[272,1024]{1,0:T(8,128)(2,1)S(1)} collective-permute-done((bf16[272,1024]{1,0:T(8,128)(2,1)}, bf16[272,1024]{1,0:T(8,128)(2,1)S(1)}, u32[]{:S(2)}, u32[]{:S(2)}) %collective-permute-start.7) | collective-permute-done | bytes 557088 | tf_op jit(solution)/shard_map/ppermute | solution.py:596
  102.6 2.8 collective-permute-start.13
  105.4 2.9 collective-permute-start.9
  111.4 15.7 %experts.4 = (bf16[272,1024]{1,0:T(8,128)(2,1)S(1)}, bf16[272,1024]{1,0:T(8,128)(2,1)S(1)}, bf16[8,256,1024]{2,1,0:T(8,128)(2,1)}, bf16[8,512,1024]{2,1,0:T(8,12...) custom-call(s32[5]{0:T(128)S(1)} %stack.117.info_ref, ...), custom_call_target="tpu_custom_call" | custom-call | flops 8000000000 | tf_op jit(solution)/shard_map/experts/pallas_call | solution.py:716
  128.7 12.7 %collective-permute-start.12 = (bf16[272,1024]{1,0:T(8,128)(2,1)}, bf16[272,1024]{1,0:T(8,128)(2,1)S(1)}, u32[]{:S(2)}, u32[]{:S(2)}) collective-permute-start(bf16[272,1024]{1,0:T(8,128)(2,1)} %after.11.xa_ref), channel_id=1, source_target_pairs={{0,1},{1,0},{2,3},{3,2},{4,5},{5,4},{6,7},{7,6},{8,9},{9,8},{10,11... | collective-permute-start | bytes 1671176 | tf_op jit(solution)/shard_map/ppermute | solution.py:599
  141.7 15.7 %experts.5 = (bf16[272,1024]{1,0:T(8,128)(2,1)S(1)}, bf16[272,1024]{1,0:T(8,128)(2,1)S(1)}, bf16[8,256,1024]{2,1,0:T(8,128)(2,1)}, bf16[8,512,1024]{2,1,0:T(8,12...) custom-call(s32[5]{0:T(128)S(1)} %stack.123.info_ref, ...), custom_call_target="tpu_custom_call", output_to_operand_aliasing={{2}: (8, {}), {3}: (9, {}), {4}: (10, {}), {5}: (11, {}), {... | custom-call | flops 8000000000 | tf_op jit(solution)/shard_map/experts/pallas_call | solution.py:716
  159.5 7.5 %collective-permute-done.14 = bf16[272,1024]{1,0:T(8,128)(2,1)S(1)} collective-permute-done((bf16[272,1024]{1,0:T(8,128)(2,1)S(1)}, bf16[272,1024]{1,0:T(8,128)(2,1)S(1)}, u32[]{:S(2)}, u32[]{:S(2)}) %collective-permute-start.14) | collective-permute-done | bytes 557088 | tf_op jit(solution)/shard_map/ppermute | solution.py:599
  167.2 15.8 %experts.6 = (bf16[272,1024]{1,0:T(8,128)(2,1)S(1)}, bf16[272,1024]{1,0:T(8,128)(2,1)S(1)}, bf16[8,256,1024]{2,1,0:T(8,128)(2,1)}, bf16[8,512,1024]{2,1,0:T(8,12...) custom-call(s32[5]{0:T(128)S(1)} %stack.120.info_ref, ...), custom_call_target="tpu_custom_call", output_to_operand_aliasing={{2}: (8, {}), {3}: (9, {}), {4}: (10, {}), {5}: (11, {}), {... | custom-call | flops 8000000000 | tf_op jit(solution)/shard_map/experts/pallas_call | solution.py:716
  185.2 5.6 collective-permute-done.11.xb_ref
  190.9 15.7 %experts.7 = (bf16[272,1024]{1,0:T(8,128)(2,1)S(1)}, bf16[272,1024]{1,0:T(8,128)(2,1)S(1)}, bf16[8,256,1024]{2,1,0:T(8,128)(2,1)}, bf16[8,512,1024]{2,1,0:T(8,12...) custom-call(s32[5]{0:T(128)S(1)} %stack.114.info_ref, ...), custom_call_target="tpu_custom_call", output_to_operand_aliasing={{2}: (8, {}), {3}: (9, {}), {4}: (10, {}), {5}: (11, {}), {... | custom-call | flops 8000000000 | tf_op jit(solution)/shard_map/experts/pallas_call | solution.py:716
  211.4 8.8 %collective-permute-done.16 = bf16[272,1024]{1,0:T(8,128)(2,1)} collective-permute-done((bf16[272,1024]{1,0:T(8,128)(2,1)S(1)}, bf16[272,1024]{1,0:T(8,128)(2,1)}, u32[]{:S(2)}, u32[]{:S(2)}) %collective-permute-start.16) | collective-permute-done | bytes 557088 | tf_op jit(solution)/shard_map/ppermute | solution.py:599
  222.5 19.2 %expert_grads.1 = (bf16[4,3,512,512]{3,2,1,0:T(8,128)(2,1)}, bf16[4,3,512,512]{3,2,1,0:T(8,128)(2,1)}) custom-call(s32[4]{0:T(128)} %pad_add_fusion.1.info_ref, bf16[8,512,1024]{2,1,0:T(8,128)(2,1)} %get-tuple-element.104.xs_ref, bf16[8,512,1024]{2,1,0:T(8,128)(2,1)} %get-tuple-element.105.us_ref, bf16[8,512,512]{2,1,0:T(8,128)(2,1)} %get-tuple-element.106.hs_ref, ...), custom_call_target="tpu_custom_call" | custom-call | flops 30000001024 | tf_op jit(solution)/shard_map/expert_grads/pallas_call | solution.py:786
  241.7 31.6 %collective-permute-done.19 = bf16[272,1024]{1,0:T(8,128)(2,1)S(1)} collective-permute-done((bf16[272,1024]{1,0:T(8,128)(2,1)}, bf16[272,1024]{1,0:T(8,128)(2,1)S(1)}, u32[]{:S(2)}, u32[]{:S(2)}) %collective-permute-start.19) | collective-permute-done | bytes 557088 | tf_op jit(solution)/shard_map/ppermute | solution.py:596
  277.4 4.1 middle.1
  285.0 23.2 %attention_back.1 = (bf16[256,1024]{1,0:T(8,128)(2,1)}, bf16[2,256,1024]{2,1,0:T(8,128)(2,1)}, bf16[3200,1024]{1,0:T(8,128)(2,1)}) custom-call(s32[2]{0:T(128)} %pad_add_fusion.2.me_ref, bf16[4,4,256,128]{3,2,1,0:T(8,128)(2,1)} %get-tuple-element.112.qz_ref, bf16[4,4,256,128]{3,2,1,0:T(8,128)(2,1)} %copy-done.25, bf16[512,512]{1,0:T(8,128)(2,1)} %get-tuple-element.115.k_ref, ...), custom_call_target="tpu_custom_call" | custom-call | flops 10750000128 | tf_op jit(solution)/shard_map/attention_back/pallas_call | solution.py:820
  308.2 7.2 %fusion.3 = (bf16[3,512,512]{2,1,0:T(8,128)(2,1)}, bf16[3,512,512]{2,1,0:T(8,128)(2,1)S(1)}, bf16[3,512,512]{2,1,0:T(8,128)(2,1)S(1)}, bf16[3,512,512]{2,1,0:T(8,128)(2,1)}) fusion(bf16[4,3,512,512]{3,2,1,0:T(8,128)(2,1)} %collective-permute-done.21, bf16[4,3,512,512]{3,2,1,0:T(8,128)(2,1)} %after.13), kind=kLoop, calls=%fused_computation.14 | loop fusion | flops 12582912 | bytes 18874368 | tf_op jit(solution)/shard_map/convert_element_type | solution.py:363
  315.4 2.6 collective-permute-start.23
  320.1 4.7 all-to-all-start.2
  324.8 36.0 %collective-permute-done.23.tied_ref = bf16[3,512,512]{2,1,0:T(8,128)(2,1)} collective-permute-done((bf16[3,512,512]{2,1,0:T(8,128)(2,1)S(1)}, bf16[3,512,512]{2,1,0:T(8,128)(2,1)}, u32[]{:S(2)}, u32[]{:S(2)}) %collective-permute-start.23) | collective-permute-done | bytes 1572896 | tf_op jit(solution)/shard_map/ppermute | solution.py:603
  360.8 2.4 add_convert_fusion.mine_ref
  363.3 41.3 %collective-permute-done.22.refs_1_ = bf16[3,512,512]{2,1,0:T(8,128)(2,1)} collective-permute-done((bf16[3,512,512]{2,1,0:T(8,128)(2,1)}, bf16[3,512,512]{2,1,0:T(8,128)(2,1)}, u32[]{:S(2)}, u32[]{:S(2)}) %collective-permute-start.22) | collective-permute-done | bytes 1572896 | tf_op jit(solution)/shard_map/ppermute | solution.py:603
  404.6 3.5 add_convert_fusion.1.mine_ref
  408.1 32.5 %collective-permute-done.24.refs_1_ = bf16[3,512,512]{2,1,0:T(8,128)(2,1)} collective-permute-done((bf16[3,512,512]{2,1,0:T(8,128)(2,1)S(1)}, bf16[3,512,512]{2,1,0:T(8,128)(2,1)}, u32[]{:S(2)}, u32[]{:S(2)}) %collective-permute-start.24) | collective-permute-done | bytes 1572896 | tf_op jit(solution)/shard_map/ppermute | solution.py:603
  448.3 3.5 last.1
  453.2 22.6 %all-to-all-start.3 = ((bf16[4,64,1024]{2,1,0:T(8,128)(2,1)}), bf16[4,64,1024]{2,1,0:T(8,128)(2,1)}, u32[]{:S(2)}, u32[]{:S(2)}) async-start(bf16[4,64,1024]{2,1,0:T(8,128)(2,1)} %bitcast.69), calls=%async_computation.4 | async-start | bytes 1048576 | tf_op jit(solution)/shard_map/all_to_all | solution.py:889
  475.8 5.6 collective-permute-done.30
  481.4 3.6 add_convert_fusion.3.mine_ref
  484.9 2.3 fusion.4.refs_0_
  487.2 9.0 %all-to-all-done.3.refs_2_ = bf16[4,64,1024]{2,1,0:T(8,128)(2,1)} async-done(((bf16[4,64,1024]{2,1,0:T(8,128)(2,1)}), bf16[4,64,1024]{2,1,0:T(8,128)(2,1)}, u32[]{:S(2)}, u32[]{:S(2)}) %all-to-all-start.3) | async-done | bytes 524320 | tf_op jit(solution)/shard_map/all_to_all | solution.py:889
  496.2 20.7 %all-to-all-start.1 = ((bf16[4,64,1024]{2,1,0:T(8,128)(2,1)}), bf16[4,64,1024]{2,1,0:T(8,128)(2,1)}, u32[]{:S(2)}, u32[]{:S(2)}) async-start(bf16[4,64,1024]{2,1,0:T(8,128)(2,1)} %bitcast.81), calls=%async_computation.2 | async-start | bytes 1048576 | tf_op jit(solution)/shard_map/all_to_all | solution.py:889
  517.5 3.6 collective-permute-done.25
  523.8 3.1 collective-permute-done.26
  526.9 4.6 collective-permute-start.27
  531.6 2.5 collective-permute-done.27
  535.3 3.9 collective-permute-done.29
  541.9 4.4 finish.4
  546.3 4.9 finish.5
  551.2 4.4 finish.6
  555.6 4.9 finish.7
  560.4 7.6 %slice_convert_fusion = (f32[1024,1024]{1,0:T(8,128)}, f32[1024,1024]{1,0:T(8,128)S(1)}, f32[1024,1024]{1,0:T(8,128)}) fusion(bf16[3200,1024]{1,0:T(8,128)(2,1)} %after.17), kind=kLoop, calls=%fused_computation.8 | loop fusion | flops 3145728 | bytes 18874368 | tf_op jit(solution)/shard_map/convert_element_type | solution.py:896
  570.3 2.4 fusion.6
  (198 shorter events, 69.0 us)
Async XLA Ops:
  7.2 102.1 %all-gather.3.cloned.1.call-start = ((), (), s32[]{:S(2)}) async-start(), calls=%async_computation.7 | async-start | bytes 4718592 | tf_op jit(solution)/shard_map/all_gather | solution.py:633
  12.1 22.2 %all-to-all-start = ((s32[8,9,256]{2,1,0:T(8,128)}), s32[8,9,256]{2,1,0:T(8,128)S(1)}, u32[]{:S(2)}, u32[]{:S(2)}) async-start(s32[8,9,256]{2,1,0:T(8,128)} %after.9), calls=%async_computation | async-start | bytes 262144 | tf_op jit(solution)/shard_map/all_to_all | solution.py:623
  19.4 465.5 %reduce-scatter.2.cloned.1.call-start = ((), (), s32[]{:S(2)}) async-start(), calls=%async_computation.5 | async-start | bytes 4718592 | tf_op jit(solution)/shard_map/reduce_scatter | solution.py:799
  19.5 16.3 %collective-permute-start.1 = (bf16[64,1024]{1,0:T(8,128)(2,1)}, bf16[64,1024]{1,0:T(8,128)(2,1)S(1)}, u32[]{:S(2)}, u32[]{:S(2)}) collective-permute-start(bf16[64,1024]{1,0:T(8,128)(2,1)} %get-tuple-element.152.refs_2_), channel_id=1, source_target_pairs={{0,2},{1,3},{2,4},{3,5},{4,6},{5,7},{6,0},{7,1},{8,10},{9,11},{10,... | collective-permute-start | bytes 393224 | tf_op jit(solution)/shard_map/ppermute | solution.py:596
  21.4 23.3 %collective-permute-start.3 = (bf16[64,1024]{1,0:T(8,128)(2,1)}, bf16[64,1024]{1,0:T(8,128)(2,1)S(1)}, u32[]{:S(2)}, u32[]{:S(2)}) collective-permute-start(bf16[64,1024]{1,0:T(8,128)(2,1)} %get-tuple-element.154.refs_3_), channel_id=1, source_target_pairs={{0,4},{1,5},{2,6},{3,7},{4,0},{5,1},{6,2},{7,3},{8,12},{9,13},{10,... | collective-permute-start | bytes 393224 | tf_op jit(solution)/shard_map/ppermute | solution.py:596
  23.8 21.5 %collective-permute-start.5 = (bf16[64,1024]{1,0:T(8,128)(2,1)}, bf16[64,1024]{1,0:T(8,128)(2,1)S(1)}, u32[]{:S(2)}, u32[]{:S(2)}) collective-permute-start(bf16[64,1024]{1,0:T(8,128)(2,1)} %get-tuple-element.151.refs_4_), channel_id=1, source_target_pairs={{0,6},{1,7},{2,0},{3,1},{4,2},{5,3},{6,4},{7,5},{8,14},{9,15},{10,... | collective-permute-start | bytes 393224 | tf_op jit(solution)/shard_map/ppermute | solution.py:596
  25.3 24.3 %collective-permute-start = (bf16[64,1024]{1,0:T(8,128)(2,1)}, bf16[64,1024]{1,0:T(8,128)(2,1)S(1)}, u32[]{:S(2)}, u32[]{:S(2)}) collective-permute-start(bf16[64,1024]{1,0:T(8,128)(2,1)} %get-tuple-element.153.refs_1_.refs_0_), channel_id=1, source_target_pairs={{0,1},{1,0},{2,3},{3,2},{4,5},{5,4},{6,7},{7,6},{8,9},{9,8},{10,11... | collective-permute-start | bytes 393224 | tf_op jit(solution)/shard_map/ppermute | solution.py:599
  35.7 13.8 %collective-permute-start.2 = (bf16[64,1024]{1,0:T(8,128)(2,1)S(1)}, bf16[64,1024]{1,0:T(8,128)(2,1)S(1)}, u32[]{:S(2)}, u32[]{:S(2)}) collective-permute-start(bf16[64,1024]{1,0:T(8,128)(2,1)S(1)} %collective-permute-done.1.refs_2_), channel_id=1, source_target_pairs={{0,1},{1,0},{2,3},{3,2},{4,5},{5,4},{6,7},{7,6},{8,9},{9,8},{10,11... | collective-permute-start | bytes 393224 | tf_op jit(solution)/shard_map/ppermute | solution.py:599
  44.8 5.0 collective-permute-start.4
  45.3 5.8 %collective-permute-start.6 = (bf16[64,1024]{1,0:T(8,128)(2,1)S(1)}, bf16[64,1024]{1,0:T(8,128)(2,1)S(1)}, u32[]{:S(2)}, u32[]{:S(2)}) collective-permute-start(bf16[64,1024]{1,0:T(8,128)(2,1)S(1)} %collective-permute-done.5.refs_6_), channel_id=1, source_target_pairs={{0,1},{1,0},{2,3},{3,2},{4,5},{5,4},{6,7},{7,6},{8,9},{9,8},{10,11... | collective-permute-start | bytes 393224 | tf_op jit(solution)/shard_map/ppermute | solution.py:599
  71.3 23.7 %collective-permute-start.8 = (bf16[272,1024]{1,0:T(8,128)(2,1)}, bf16[272,1024]{1,0:T(8,128)(2,1)S(1)}, u32[]{:S(2)}, u32[]{:S(2)}) collective-permute-start(bf16[272,1024]{1,0:T(8,128)(2,1)} %get-tuple-element.78.xa_ref.xg_ref), channel_id=1, source_target_pairs={{0,1},{1,0},{2,3},{3,2},{4,5},{5,4},{6,7},{7,6},{8,9},{9,8},{10,11... | collective-permute-start | bytes 1671176 | tf_op jit(solution)/shard_map/ppermute | solution.py:599
  72.0 29.8 %collective-permute-start.7 = (bf16[272,1024]{1,0:T(8,128)(2,1)}, bf16[272,1024]{1,0:T(8,128)(2,1)S(1)}, u32[]{:S(2)}, u32[]{:S(2)}) collective-permute-start(bf16[272,1024]{1,0:T(8,128)(2,1)} %get-tuple-element.78.xa_ref.xg_ref), channel_id=1, source_target_pairs={{0,2},{1,3},{2,4},{3,5},{4,6},{5,7},{6,0},{7,1},{8,10},{9,11},{10,... | collective-permute-start | bytes 1671176 | tf_op jit(solution)/shard_map/ppermute | solution.py:596
  102.6 39.1 %collective-permute-start.13 = (bf16[272,1024]{1,0:T(8,128)(2,1)}, bf16[272,1024]{1,0:T(8,128)(2,1)S(1)}, u32[]{:S(2)}, u32[]{:S(2)}) collective-permute-start(bf16[272,1024]{1,0:T(8,128)(2,1)} %after.10.xa_ref), channel_id=1, source_target_pairs={{0,1},{1,0},{2,3},{3,2},{4,5},{5,4},{6,7},{7,6},{8,9},{9,8},{10,11... | collective-permute-start | bytes 1671176 | tf_op jit(solution)/shard_map/ppermute | solution.py:599
  105.4 22.6 %collective-permute-start.9 = (bf16[272,1024]{1,0:T(8,128)(2,1)}, bf16[272,1024]{1,0:T(8,128)(2,1)S(1)}, u32[]{:S(2)}, u32[]{:S(2)}) collective-permute-start(bf16[272,1024]{1,0:T(8,128)(2,1)} %after.10.xa_ref), channel_id=1, source_target_pairs={{0,2},{1,3},{2,4},{3,5},{4,6},{5,7},{6,0},{7,1},{8,10},{9,11},{10,... | collective-permute-start | bytes 1671176 | tf_op jit(solution)/shard_map/ppermute | solution.py:596
  111.4 30.2 %copy-start.7 = (bf16[272,1024]{1,0:T(8,128)(2,1)S(1)}, bf16[272,1024]{1,0:T(8,128)(2,1)}, u32[]{:S(2)}) copy-start(bf16[272,1024]{1,0:T(8,128)(2,1)} %after.10.xa_ref) | copy-start | bytes 1671172
  128.7 38.5 %collective-permute-start.12 = (bf16[272,1024]{1,0:T(8,128)(2,1)}, bf16[272,1024]{1,0:T(8,128)(2,1)S(1)}, u32[]{:S(2)}, u32[]{:S(2)}) collective-permute-start(bf16[272,1024]{1,0:T(8,128)(2,1)} %after.11.xa_ref), channel_id=1, source_target_pairs={{0,1},{1,0},{2,3},{3,2},{4,5},{5,4},{6,7},{7,6},{8,9},{9,8},{10,11... | collective-permute-start | bytes 1671176 | tf_op jit(solution)/shard_map/ppermute | solution.py:599
  141.4 18.0 %collective-permute-start.10 = (bf16[272,1024]{1,0:T(8,128)(2,1)}, bf16[272,1024]{1,0:T(8,128)(2,1)S(1)}, u32[]{:S(2)}, u32[]{:S(2)}) collective-permute-start(bf16[272,1024]{1,0:T(8,128)(2,1)} %after.11.xa_ref), channel_id=1, source_target_pairs={{0,2},{1,3},{2,4},{3,5},{4,6},{5,7},{6,0},{7,1},{8,10},{9,11},{10,... | collective-permute-start | bytes 1671176 | tf_op jit(solution)/shard_map/ppermute | solution.py:596
  141.6 25.4 %collective-permute-start.14 = (bf16[272,1024]{1,0:T(8,128)(2,1)S(1)}, bf16[272,1024]{1,0:T(8,128)(2,1)S(1)}, u32[]{:S(2)}, u32[]{:S(2)}) collective-permute-start(bf16[272,1024]{1,0:T(8,128)(2,1)S(1)} %get-tuple-element.92), channel_id=1, source_target_pairs={{0,1},{1,0},{2,3},{3,2},{4,5},{5,4},{6,7},{7,6},{8,9},{9,8},{10,11... | collective-permute-start | bytes 1671176 | tf_op jit(solution)/shard_map/ppermute | solution.py:599
  141.7 25.3 %copy-start.5 = (bf16[272,1024]{1,0:T(8,128)(2,1)S(1)}, bf16[272,1024]{1,0:T(8,128)(2,1)}, u32[]{:S(2)}) copy-start(bf16[272,1024]{1,0:T(8,128)(2,1)} %copy-done.4) | copy-start | bytes 1671172
  141.7 25.5 %copy-start.3 = (bf16[272,1024]{1,0:T(8,128)(2,1)S(1)}, bf16[272,1024]{1,0:T(8,128)(2,1)}, u32[]{:S(2)}) copy-start(bf16[272,1024]{1,0:T(8,128)(2,1)} %after.11.xa_ref) | copy-start | bytes 1671172
  157.4 27.6 %collective-permute-start.15 = (bf16[272,1024]{1,0:T(8,128)(2,1)S(1)}, bf16[272,1024]{1,0:T(8,128)(2,1)S(1)}, u32[]{:S(2)}, u32[]{:S(2)}) collective-permute-start(bf16[272,1024]{1,0:T(8,128)(2,1)S(1)} %get-tuple-element.100), channel_id=1, source_target_pairs={{0,1},{1,0},{2,3},{3,2},{4,5},{5,4},{6,7},{7,6},{8,9},{9,8},{10,11... | collective-permute-start | bytes 1671176 | tf_op jit(solution)/shard_map/ppermute | solution.py:599
  159.4 31.4 %collective-permute-start.11 = (bf16[272,1024]{1,0:T(8,128)(2,1)S(1)}, bf16[272,1024]{1,0:T(8,128)(2,1)S(1)}, u32[]{:S(2)}, u32[]{:S(2)}) collective-permute-start(bf16[272,1024]{1,0:T(8,128)(2,1)S(1)} %collective-permute-done.10.xa_ref), channel_id=1, source_target_pairs={{0,1},{1,0},{2,3},{3,2},{4,5},{5,4},{6,7},{7,6},{8,9},{9,8},{10,11... | collective-permute-start | bytes 1671176 | tf_op jit(solution)/shard_map/ppermute | solution.py:599
  183.0 26.3 %collective-permute-start.17 = (bf16[272,1024]{1,0:T(8,128)(2,1)S(1)}, bf16[272,1024]{1,0:T(8,128)(2,1)}, u32[]{:S(2)}, u32[]{:S(2)}) collective-permute-start(bf16[272,1024]{1,0:T(8,128)(2,1)S(1)} %get-tuple-element.110), channel_id=1, source_target_pairs={{0,1},{1,0},{2,3},{3,2},{4,5},{5,4},{6,7},{7,6},{8,9},{9,8},{10,11... | collective-permute-start | bytes 1671176 | tf_op jit(solution)/shard_map/ppermute | solution.py:599
  206.6 13.6 %collective-permute-start.16 = (bf16[272,1024]{1,0:T(8,128)(2,1)S(1)}, bf16[272,1024]{1,0:T(8,128)(2,1)}, u32[]{:S(2)}, u32[]{:S(2)}) collective-permute-start(bf16[272,1024]{1,0:T(8,128)(2,1)S(1)} %get-tuple-element.103), channel_id=1, source_target_pairs={{0,1},{1,0},{2,3},{3,2},{4,5},{5,4},{6,7},{7,6},{8,9},{9,8},{10,11... | collective-permute-start | bytes 1671176 | tf_op jit(solution)/shard_map/ppermute | solution.py:599
  209.3 32.4 %collective-permute-start.18 = (bf16[272,1024]{1,0:T(8,128)(2,1)S(1)}, bf16[272,1024]{1,0:T(8,128)(2,1)}, u32[]{:S(2)}, u32[]{:S(2)}) collective-permute-start(bf16[272,1024]{1,0:T(8,128)(2,1)S(1)} %add_convert_fusion.11.rest_6_), channel_id=1, source_target_pairs={{0,6},{1,7},{2,0},{3,1},{4,2},{5,3},{6,4},{7,5},{8,14},{9,15},{10,... | collective-permute-start | bytes 1671176 | tf_op jit(solution)/shard_map/ppermute | solution.py:596
  211.4 62.0 %collective-permute-start.19 = (bf16[272,1024]{1,0:T(8,128)(2,1)}, bf16[272,1024]{1,0:T(8,128)(2,1)S(1)}, u32[]{:S(2)}, u32[]{:S(2)}) collective-permute-start(bf16[272,1024]{1,0:T(8,128)(2,1)} %add_convert_fusion.9.rest_0_), channel_id=1, source_target_pairs={{0,4},{1,5},{2,6},{3,7},{4,0},{5,1},{6,2},{7,3},{8,12},{9,13},{10,... | collective-permute-start | bytes 1671176 | tf_op jit(solution)/shard_map/ppermute | solution.py:596
  221.4 51.9 %collective-permute-start.20 = (bf16[272,1024]{1,0:T(8,128)(2,1)S(1)}, bf16[272,1024]{1,0:T(8,128)(2,1)S(1)}, u32[]{:S(2)}, u32[]{:S(2)}) collective-permute-start(bf16[272,1024]{1,0:T(8,128)(2,1)S(1)} %add_convert_fusion.10.refs_1_.rest_1_), channel_id=1, source_target_pairs={{0,2},{1,3},{2,4},{3,5},{4,6},{5,7},{6,0},{7,1},{8,10},{9,11},{10,... | collective-permute-start | bytes 1671176 | tf_op jit(solution)/shard_map/ppermute | solution.py:596
  222.3 338.2 %all-reduce.2.cloned.1.call-start = ((), (), s32[]{:S(2)}) async-start(), calls=%async_computation.6 | async-start | bytes 13107200 | tf_op jit(solution)/shard_map/psum | solution.py:893
  275.6 32.6 %collective-permute-start.21 = (bf16[4,3,512,512]{3,2,1,0:T(8,128)(2,1)}, bf16[4,3,512,512]{3,2,1,0:T(8,128)(2,1)}, u32[]{:S(2)}, u32[]{:S(2)}) collective-permute-start(bf16[4,3,512,512]{3,2,1,0:T(8,128)(2,1)} %after.14), channel_id=1, source_target_pairs={{0,8},{8,0},{16,24},{24,16},{1,9},{9,1},{17,25},{25,17},{2,10},{10... | collective-permute-start | bytes 18874376 | tf_op jit(solution)/shard_map/ppermute | solution.py:603
  315.4 45.4 %collective-permute-start.23 = (bf16[3,512,512]{2,1,0:T(8,128)(2,1)S(1)}, bf16[3,512,512]{2,1,0:T(8,128)(2,1)}, u32[]{:S(2)}, u32[]{:S(2)}) collective-permute-start(bf16[3,512,512]{2,1,0:T(8,128)(2,1)S(1)} %get-tuple-element.144), channel_id=1, source_target_pairs={{0,16},{8,24},{16,0},{24,8},{1,17},{9,25},{17,1},{25,9},{2,18},{10... | collective-permute-start | bytes 4718600 | tf_op jit(solution)/shard_map/ppermute | solution.py:603
  318.0 86.6 %collective-permute-start.22 = (bf16[3,512,512]{2,1,0:T(8,128)(2,1)}, bf16[3,512,512]{2,1,0:T(8,128)(2,1)}, u32[]{:S(2)}, u32[]{:S(2)}) collective-permute-start(bf16[3,512,512]{2,1,0:T(8,128)(2,1)} %get-tuple-element.145), channel_id=1, source_target_pairs={{0,16},{8,24},{16,0},{24,8},{1,17},{9,25},{17,1},{25,9},{2,18},{10... | collective-permute-start | bytes 4718600 | tf_op jit(solution)/shard_map/ppermute | solution.py:603
  318.1 122.5 %collective-permute-start.24 = (bf16[3,512,512]{2,1,0:T(8,128)(2,1)S(1)}, bf16[3,512,512]{2,1,0:T(8,128)(2,1)}, u32[]{:S(2)}, u32[]{:S(2)}) collective-permute-start(bf16[3,512,512]{2,1,0:T(8,128)(2,1)S(1)} %get-tuple-element.143), channel_id=1, source_target_pairs={{0,16},{8,24},{16,0},{24,8},{1,17},{9,25},{17,1},{25,9},{2,18},{10... | collective-permute-start | bytes 4718600 | tf_op jit(solution)/shard_map/ppermute | solution.py:603
  320.0 161.3 %collective-permute-start.30 = (bf16[3,512,512]{2,1,0:T(8,128)(2,1)}, bf16[3,512,512]{2,1,0:T(8,128)(2,1)}, u32[]{:S(2)}, u32[]{:S(2)}) collective-permute-start(bf16[3,512,512]{2,1,0:T(8,128)(2,1)} %get-tuple-element.142), channel_id=1, source_target_pairs={{0,16},{8,24},{16,0},{24,8},{1,17},{9,25},{17,1},{25,9},{2,18},{10... | collective-permute-start | bytes 4718600 | tf_op jit(solution)/shard_map/ppermute | solution.py:603
  320.1 122.4 %all-to-all-start.2 = ((bf16[2,256,1024]{2,1,0:T(8,128)(2,1)}), bf16[2,256,1024]{2,1,0:T(8,128)(2,1)}, u32[]{:S(2)}, u32[]{:S(2)}) async-start(bf16[2,256,1024]{2,1,0:T(8,128)(2,1)} %get-tuple-element.124), calls=%async_computation.3 | async-start | bytes 2097152 | tf_op jit(solution)/shard_map/all_to_all | solution.py:867
  363.2 77.4 %copy-start.29 = (bf16[3,512,512]{2,1,0:T(8,128)(2,1)S(1)}, bf16[3,512,512]{2,1,0:T(8,128)(2,1)}, u32[]{:S(2)}) copy-start(bf16[3,512,512]{2,1,0:T(8,128)(2,1)} %copy-done.28) | copy-start | bytes 4718596
  363.2 178.7 %collective-permute-start.34 = (bf16[3,512,512]{2,1,0:T(8,128)(2,1)S(1)}, bf16[3,512,512]{2,1,0:T(8,128)(2,1)}, u32[]{:S(2)}, u32[]{:S(2)}) collective-permute-start(bf16[3,512,512]{2,1,0:T(8,128)(2,1)S(1)} %add_convert_fusion.mine_ref), channel_id=1, source_target_pairs={{0,8},{8,0},{16,24},{24,16},{1,9},{9,1},{17,25},{25,17},{2,10},{10... | collective-permute-start | bytes 4718600 | tf_op jit(solution)/shard_map/ppermute | solution.py:603
  408.1 34.4 %copy-start.24 = (f32[1024]{0:T(1024)S(1)}, f32[1024]{0:T(1024)}, u32[]{:S(2)}) copy-start(f32[1024]{0:T(1024)} %param.18) | copy-start | bytes 12292
  408.1 138.2 %collective-permute-start.33 = (bf16[3,512,512]{2,1,0:T(8,128)(2,1)}, bf16[3,512,512]{2,1,0:T(8,128)(2,1)}, u32[]{:S(2)}, u32[]{:S(2)}) collective-permute-start(bf16[3,512,512]{2,1,0:T(8,128)(2,1)} %add_convert_fusion.1.mine_ref), channel_id=1, source_target_pairs={{0,8},{8,0},{16,24},{24,16},{1,9},{9,1},{17,25},{25,17},{2,10},{10... | collective-permute-start | bytes 4718600 | tf_op jit(solution)/shard_map/ppermute | solution.py:603
  442.5 108.7 %collective-permute-start.32 = (bf16[3,512,512]{2,1,0:T(8,128)(2,1)S(1)}, bf16[3,512,512]{2,1,0:T(8,128)(2,1)}, u32[]{:S(2)}, u32[]{:S(2)}) collective-permute-start(bf16[3,512,512]{2,1,0:T(8,128)(2,1)S(1)} %add_convert_fusion.2.mine_ref), channel_id=1, source_target_pairs={{0,8},{8,0},{16,24},{24,16},{1,9},{9,1},{17,25},{25,17},{2,10},{10... | collective-permute-start | bytes 4718600 | tf_op jit(solution)/shard_map/ppermute | solution.py:603
  453.2 43.0 %all-to-all-start.3 = ((bf16[4,64,1024]{2,1,0:T(8,128)(2,1)}), bf16[4,64,1024]{2,1,0:T(8,128)(2,1)}, u32[]{:S(2)}, u32[]{:S(2)}) async-start(bf16[4,64,1024]{2,1,0:T(8,128)(2,1)} %bitcast.69), calls=%async_computation.4 | async-start | bytes 1048576 | tf_op jit(solution)/shard_map/all_to_all | solution.py:889
  484.9 70.7 %collective-permute-start.31 = (bf16[3,512,512]{2,1,0:T(8,128)(2,1)}, bf16[3,512,512]{2,1,0:T(8,128)(2,1)}, u32[]{:S(2)}, u32[]{:S(2)}) collective-permute-start(bf16[3,512,512]{2,1,0:T(8,128)(2,1)} %add_convert_fusion.3.mine_ref), channel_id=1, source_target_pairs={{0,8},{8,0},{16,24},{24,16},{1,9},{9,1},{17,25},{25,17},{2,10},{10... | collective-permute-start | bytes 4718600 | tf_op jit(solution)/shard_map/ppermute | solution.py:603
  487.2 54.7 %copy-start.22 = (s32[4]{0:T(128)S(1)}, s32[4]{0:T(128)}, u32[]{:S(2)}) copy-start(s32[4]{0:T(128)} %pad_add_fusion.1.info_ref) | copy-start | bytes 52
  496.2 45.7 %all-to-all-start.1 = ((bf16[4,64,1024]{2,1,0:T(8,128)(2,1)}), bf16[4,64,1024]{2,1,0:T(8,128)(2,1)}, u32[]{:S(2)}, u32[]{:S(2)}) async-start(bf16[4,64,1024]{2,1,0:T(8,128)(2,1)} %bitcast.81), calls=%async_computation.2 | async-start | bytes 1048576 | tf_op jit(solution)/shard_map/all_to_all | solution.py:889
  516.9 4.1 collective-permute-start.25
  521.8 5.1 collective-permute-start.26
  526.9 7.1 %collective-permute-start.27 = (f32[8,1024]{1,0:T(8,128)S(1)}, f32[8,1024]{1,0:T(8,128)S(1)}, u32[]{:S(2)}, u32[]{:S(2)}) collective-permute-start(f32[8,1024]{1,0:T(8,128)S(1)} %add.259), channel_id=1, source_target_pairs={{0,4},{1,5},{2,6},{3,7},{4,0},{5,1},{6,2},{7,3},{8,12},{9,13},{10,... | collective-permute-start | bytes 98312 | tf_op jit(solution)/shard_map/ppermute | solution.py:599
  534.0 1.2 collective-permute-start.28
  535.2 3.9 collective-permute-start.29
  (34 other events, 88.2 us)
Sparse Core Ops, SparseCore 0:
  10.1 99.1 all-gather.2
  222.4 109.4 reduce-scatter.1
  338.6 180.6 all-reduce.1

commit v4 on v3

--- a/solution.py
+++ b/solution.py
@@ -320,7 +320,7 @@
         for c, dx_ref in enumerate((dxa_ref, dxb_ref)):
             dx_ref[:tokens, :] = mul(pick_ref[c], dxs_ref[c], TN).astype(BF16)
             dx_ref[tokens:, :] = back_ref[c].astype(BF16)
-            y_ref[places[c]] = mul(pick_ref[c], ys_ref[c], TN).astype(BF16)
+            y_ref[places[c], 0] = mul(pick_ref[c], ys_ref[c], TN).astype(BF16)
 
 
 def expert_grads_kernel(info_ref, xs_ref, us_ref, hs_ref, dg_ref, du_ref, *rest):
@@ -359,8 +359,42 @@
         down_ref[0, rows, inner:] = source[2, half // 2 :].astype(F32)
 
 
+def spread_kernel(query_ref, keyval_ref, output_ref, vectors_ref, *rest):
+    sums = rest[-5:]
+    inner = sums[1].shape[1]
+    sums[0][...] = query_ref[...].astype(F32)
+    sums[1][...] = keyval_ref[:, :inner].astype(F32)
+    sums[2][...] = keyval_ref[:, inner:].astype(F32)
+    sums[3][...] = output_ref[...].astype(F32)
+
+    @pl.when(pl.program_id(0) == 0)
+    def _():
+        sums[4][...] = vectors_ref[...].astype(F32)
+
+
 def add(*terms):
     return sum(term.astype(F32) for term in terms).astype(terms[0].dtype)
+
+
+def plus_kernel(left_ref, right_ref, out_ref):
+    total = left_ref[...].astype(F32) + right_ref[...].astype(F32)
+    out_ref[...] = total.reshape(out_ref.shape).astype(out_ref.dtype)
+
+
+def plus(left, right, at=None):
+    parts, rows, columns = left.shape[-3:]
+    entry = pl.BlockSpec((1, rows, columns), lambda i: (i, 0, 0))
+    source = entry if at is None else pl.BlockSpec((1, 1, rows, columns), lambda i: (at, i, 0, 0))
+    return pl.pallas_call(
+        plus_kernel,
+        grid=(parts,),
+        out_shape=struct((parts, rows, columns), left.dtype),
+        in_specs=[source, source],
+        out_specs=entry,
+        compiler_params=params(16),
+        cost_estimate=took(0.1),
+        name="plus",
+    )(left, right)
 
 
 def after(values, *others):
@@ -392,12 +426,9 @@
     gain_two_ref,
     router_ref,
     wo_ref,
-    queued_ref,
-    vectors_ref,
-    mixed_ref,
-    gres_ref,
-    gaz_ref,
+    *rest,
 ):
+    vectors_ref, mixed_ref, gres_ref, gaz_ref = rest[-4:]
     tokens, width = u_ref.shape
     experts = gates_ref.shape[0]
     pieces = tokens // BLOCK
@@ -436,6 +467,7 @@
 
 def attention_back_kernel(
     members,
+    experts,
     me_ref,
     qz_ref,
     gaz_ref,
@@ -449,14 +481,13 @@
     att_ref,
     mixed_ref,
     vectors_ref,
-    queued_ref,
-    dq_ref,
-    dkv_ref,
-    weights_ref,
-    dk_acc,
-    dv_acc,
-    row_ref,
+    wq_ref,
+    wk_ref,
+    wv_ref,
+    gain_one_ref,
+    *rest,
 ):
+    dq_ref, dkv_ref, weights_ref, dk_acc, dv_acc, row_ref = rest[-6:]
     member = me_ref[0]
     tokens = own_ref.shape[0]
     pieces = tokens // BLOCK
@@ -503,28 +534,40 @@
     ):
         product = mul(left_ref[...], right_ref[...], TN)
         weights_ref[i * width : (i + 1) * width, :] = product.astype(BF16)
-    weights_ref[3 * width :, :] = vectors_ref[...]
+    first = jnp.sum(mul(dq_ref[...], wq_ref[...], NT) * own_ref[...].astype(F32), axis=0, keepdims=True)
+    for at in range(0, length, tokens):
+        rows = slice(at, at + tokens)
+        grad_mixer = mul(row_ref[rows, :inner], wk_ref[...], NT)
+        grad_mixer += mul(row_ref[rows, inner:], wv_ref[...], NT)
+        first += jnp.sum(grad_mixer * mix_ref[rows, :].astype(F32), axis=0, keepdims=True)
+    first = first / gain_one_ref[...]
+    vectors = vectors_ref[...].astype(F32)
+    place = lax.broadcasted_iota(jnp.int32, vectors.shape, 0)
+    weights_ref[3 * width :, :] = jnp.where(place == experts + 1, first, vectors).astype(BF16)
 
 
 def last_kernel(
     members,
     dq_ref,
-    dkv_ref,
+    *refs,
+):
+    last_body(dq_ref, refs[:members], *refs[members:])
+
+
+def last_body(
+    dq_ref,
+    dkv_refs,
     wq_ref,
     wk_ref,
     wv_ref,
     input_ref,
     gres_ref,
     gain_one_ref,
-    tied_ref,
-    gh_ref,
-    first_ref,
+    *rest,
 ):
+    gh_ref = rest[-1]
     inner = wk_ref.shape[1]
-    grad_kv = dkv_ref[0].astype(F32)
-    for other in range(1, members):
-        grad_kv = grad_kv + dkv_ref[other].astype(F32)
-    grad_kv = grad_kv.astype(BF16)
+    grad_kv = sum(dkv_ref[...].astype(F32) for dkv_ref in dkv_refs).astype(BF16)
     grad_mixer = (
         mul(dq_ref[...], wq_ref[...], NT)
         + mul(grad_kv[:, :inner], wk_ref[...], NT)
@@ -533,9 +576,6 @@
     x = input_ref[...].astype(F32)
     scale = lax.rsqrt(jnp.mean(x * x, axis=-1, keepdims=True) + EPS)
     normed = x * scale
-    first_ref[...] = jnp.broadcast_to(
-        jnp.sum(grad_mixer * normed, axis=0, keepdims=True), first_ref.shape
-    ).astype(first_ref.dtype)
     scaled = grad_mixer * gain_one_ref[...]
     gh_ref[...] = (
         gres_ref[...]
@@ -699,13 +739,8 @@
     order = list(range(rows_here))
     dx_parts, dx_sums = [[] for _ in order], []
     for k in order:
-        if k == 1:
-            values = after([two_on], dx_parts[0][0])[0]
-            for i in range(2, rows_here):
-                values = onward(values, 1) if i > 2 else values
-                sets.append([values] + [across(values, other) for other in range(1, members)])
         group = sets[k]
-        tied = dx_sums[k - 2 : k - 1] if k > 1 else []
+        tied = []
         for q in range(members // PAIR):
             pair = (row - k) % rows_here * per_row + ((member // PAIR) ^ q)
             info = [member % PAIR, me, pair, (row - k) % rows_here, (member // PAIR) ^ q]
@@ -734,7 +769,9 @@
                     out_specs=[
                         flat(tokens + PAD, width),
                         flat(tokens + PAD, width),
-                        pl.BlockSpec((PAIR, tokens, width), lambda e, info: (info[2], 0, 0)),
+                        pl.BlockSpec(
+                            (PAIR, 1, tokens, width), lambda e, info: (info[4], info[3], 0, 0)
+                        ),
                         of_pair(width),
                         of_pair(width),
                         of_pair(hidden),
@@ -753,7 +790,7 @@
                 out_shape=[
                     struct((tokens + PAD, width), BF16),
                     struct((tokens + PAD, width), BF16),
-                    pltpu.HBM((shards, tokens, width), BF16),
+                    pltpu.HBM((members, rows_here, tokens, width), BF16),
                     pltpu.HBM((shards, wide, width), BF16),
                     pltpu.HBM((shards, wide, width), BF16),
                     pltpu.HBM((shards, wide, hidden), BF16),
@@ -775,7 +812,15 @@
             )
             dx_parts[k] += outcome[:2]
             kept = outcome[2:]
-        dx_sums.append(joined(dx_parts[k]))
+        part = dx_parts[k]
+        if k == 0:
+            values = after([two_on], part[0])[0]
+            for i in range(2, rows_here):
+                values = onward(values, 1) if i > 2 else values
+                sets.append([values] + [across(values, other) for other in range(1, members)])
+        if k < 2:
+            part = part[:1] + list(after(part[1:], *sets[rows_here - 1][1:]))
+        dx_sums.append(joined(part))
     sent = [dx_sums[0]] + [onward(dx_sums[k], rows_here - k) for k in range(1, rows_here)]
     dx_sum = add(*sent)
 
@@ -795,10 +840,14 @@
         cost_estimate=took(60),
         name="expert_grads",
     )(info, *kept[1:], dx_sums[2], dx_sums[3])
-    received = row_swap(after([send], dx_sum)[0], 1)
-    y_sum = lax.psum_scatter(
-        after([kept[0]], dx_sums[3])[0], "seq", scatter_dimension=0, tiled=False
-    )
+    part_of = lambda values, m: lax.dynamic_index_in_dim(values, m, 0, keepdims=False)
+    y_all = after([kept[0]], dx_sums[3])[0]
+    middle_row = rows_here // 2
+    y_near = [
+        [across(part_of(y_all, member ^ o)[:middle_row], o) for o in range(1, members)],
+        [across(part_of(y_all, member ^ o)[middle_row:], o) for o in range(1, members)],
+    ]
+    soon = y_near[0]
     own_upstream = lax.dynamic_index_in_dim(upstream, row, 2, keepdims=False)
     own_upstream = lax.dynamic_index_in_dim(own_upstream, member, 1, keepdims=False)
     own_upstream = own_upstream.reshape(tokens, width)
@@ -810,21 +859,23 @@
             struct((tokens, width), F32),
             struct((rows_here, TILES, 4 * BLOCK, LANES), BF16),
         ],
-        in_specs=[whole()] * 8 + [pl.BlockSpec(memory_space=pl.ANY)],
+        in_specs=[whole()] * 8 + [pl.BlockSpec(memory_space=pl.ANY)] * (1 + len(soon)),
         out_specs=[whole()] * 4,
         compiler_params=params(48),
         cost_estimate=took(6),
         name="middle",
-    )(dx_sum, own_upstream, xg, residual, gates, gain_two, router, output_weight, keep)
+    )(dx_sum, own_upstream, xg, residual, gates, gain_two, router, output_weight, keep, *soon)
 
     dq, dkv, weights = pl.pallas_call(
-        functools.partial(attention_back_kernel, members),
+        functools.partial(attention_back_kernel, members, expert_count),
         out_shape=[
             struct((tokens, width), BF16),
             struct((members, tokens, width), BF16),
             struct((3 * width + EXTRA, width), BF16),
         ],
-        in_specs=[scalars()] + [whole()] * 12 + [pl.BlockSpec(memory_space=pl.ANY)],
+        in_specs=[scalars()]
+        + [whole()] * 16
+        + [pl.BlockSpec(memory_space=pl.ANY)],
         out_specs=[whole()] * 3,
         scratch_shapes=[
             pltpu.VMEM((length, inner), F32),
@@ -832,29 +883,67 @@
             pltpu.VMEM((length, width), BF16),
         ],
         compiler_params=params(58),
-        cost_estimate=took(21.5),
+        cost_estimate=took(0.1),
         name="attention_back",
-    )(me_pair, qz, gaz, k_row, v_row, own_pos, cosine, sine, mix, own_mix, att, grad_mixed, vectors, vectors)
+    )(
+        me_pair,
+        qz,
+        gaz,
+        k_row,
+        v_row,
+        own_pos,
+        cosine,
+        sine,
+        mix,
+        own_mix,
+        att,
+        grad_mixed,
+        vectors,
+        query_weight,
+        key_weight,
+        value_weight,
+        gain_one,
+        gain_one,
+    )
+    received = row_swap(after([send], gaz)[0], 1)
     kept_half = after([keep], dq)[0]
-    mine = [add(kept_half[i], received[i]) for i in range(experts)]
-    crossed = []
-    for e in range(experts):
-        bit = 2
-        while bit < lax.axis_size("rows"):
-            crossed.append(row_swap(mine[e], bit))
-            mine[e] = add(mine[e], crossed[-1])
-            bit *= 2
+    mine = [plus(kept_half, received, i) for i in range(experts)]
+    crossed = [row_swap(m, 2) for m in mine]
+    dkv = [part_of(dkv, member)] + [across(part_of(dkv, member ^ o), o) for o in range(1, members)]
+    grad_in = pl.pallas_call(
+        functools.partial(last_kernel, members),
+        out_shape=struct((tokens, width), BF16),
+        in_specs=[whole()] * (7 + members) + [pl.BlockSpec(memory_space=pl.ANY)] * len(y_near[1]),
+        out_specs=whole(),
+        compiler_params=params(48),
+        cost_estimate=took(0.1),
+        name="last",
+    )(dq, *dkv, query_weight, key_weight, value_weight, own_in, grad_residual, gain_one, *y_near[1])
+
+    y_near = [jnp.concatenate(halves, axis=0) for halves in zip(*y_near)]
+    y_far = lax.all_to_all(
+        add(after([part_of(y_all, member)], dq)[0], *y_near), "seq", 0, 0, tiled=True, axis_index_groups=same_member
+    )
+    y_sum = jnp.sum(y_far.astype(F32), axis=0)
+    hidden_out = (residual + y_sum).astype(BF16)
+    back = lambda values: lax.all_to_all(
+        values.reshape(rows_here, block, width), "seq", 0, 0, tiled=True, axis_index_groups=same_member
+    )
+    hidden_out, grad_in = back(hidden_out), back(grad_in)
     finished = []
     for e in range(experts):
+        served = {1: y_far, 2: grad_in, 3: hidden_out}.get(e)
+        crossed[e] = after([crossed[e]], served)[0] if e in (1, 2, 3) else crossed[e]
+        mine[e] = plus(mine[e], crossed[e])
         grad_spec = lambda a, b: pl.BlockSpec((1, a, b), lambda i, e=e: (e, 0, 0))
         half = pl.BlockSpec(halves, lambda i: (0, 0, 0))
         finished = pl.pallas_call(
             functools.partial(finish_kernel, len(finished)),
             grid=(1,),
             out_shape=[
-                struct((experts, width, hidden), F32),
-                struct((experts, width, hidden), F32),
-                struct((experts, hidden, width), F32),
+                pltpu.HBM((experts, width, hidden), F32),
+                pltpu.HBM((experts, width, hidden), F32),
+                pltpu.HBM((experts, hidden, width), F32),
             ],
             in_specs=[scalars(), half, half]
             + [pl.BlockSpec(memory_space=pl.ANY)] * len(finished),
@@ -864,44 +953,40 @@
             cost_estimate=took(0.1),
             name="finish",
         )(info, mine[e], row_swap(mine[e], 1), *finished)
-    dkv = lax.all_to_all(dkv, "seq", 0, 0, tiled=True, axis_index_groups=same_row)
-    grad_in, first_part = pl.pallas_call(
-        functools.partial(last_kernel, members),
-        out_shape=[struct((tokens, width), BF16), struct((8, width), F32)],
-        in_specs=[whole()] * 8 + [pl.BlockSpec(memory_space=pl.ANY)],
-        out_specs=[whole()] * 2,
-        compiler_params=params(48),
+    shared = lax.psum(weights, ("rows", "seq"))
+    step = 128
+    part = lambda i: pl.BlockSpec((step, width), lambda r, i=i: (i * (width // step) + r, 0))
+    rows_of = lambda w: pl.BlockSpec((step, w), lambda r: (r, 0))
+    query_sum, key_sum, value_sum, output_sum, vector_sum = pl.pallas_call(
+        spread_kernel,
+        grid=(width // step,),
+        out_shape=[
+            pltpu.HBM((width, width), F32),
+            pltpu.HBM((width, inner), F32),
+            pltpu.HBM((width, inner), F32),
+            pltpu.HBM((width, width), F32),
+            struct((EXTRA, width), F32),
+        ],
+        in_specs=[part(0), part(1), part(2), pl.BlockSpec((EXTRA, width), lambda r: (3 * width // EXTRA, 0))]
+        + [pl.BlockSpec(memory_space=pl.ANY)] * 3,
+        out_specs=[
+            rows_of(width),
+            rows_of(inner),
+            rows_of(inner),
+            rows_of(width),
+            pl.BlockSpec((EXTRA, width), lambda r: (0, 0)),
+        ],
+        compiler_params=params(24),
         cost_estimate=took(0.1),
-        name="last",
-    )(dq, dkv, query_weight, key_weight, value_weight, own_in, grad_residual, gain_one, crossed[0])
-
-    steps = [crossed[min(i, experts - 1)] for i in range(4)]
-    first_sum, bit = after([first_part], steps[2])[0], 1
-    while bit < shards:
-        first_sum = first_sum + across(first_sum, bit)
-        bit *= 2
-    bit = 1
-    while bit < lax.axis_size("rows"):
-        first_sum = first_sum + row_swap(first_sum, bit)
-        bit *= 2
-    steps = [crossed[min(i, experts - 1)] for i in range(4)]
-    hidden_out = after([(residual + y_sum.astype(F32)).astype(BF16)], steps[1])[0]
-    back = lambda values: lax.all_to_all(
-        values.reshape(rows_here, block, width), "seq", 0, 0, tiled=True, axis_index_groups=same_member
-    )
-    hidden_out, grad_in = back(hidden_out), back(grad_in)
-    shared = lax.psum(weights, ("rows", "seq"))
-    shared = after([shared], hidden_out, grad_in, first_sum, finished[0])[0]
-    query_sum, keyval_sum, output_sum, vector_sum = (
-        shared[i * width : (i + 1) * width].astype(F32) for i in range(4)
-    )
+        name="spread",
+    )(*[pltpu.with_memory_space_constraint(shared, pltpu.HBM)] * 4, hidden_out, grad_in, finished[0])
     return (
         hidden_out,
         grad_in.astype(F32),
-        first_sum[0],
+        vector_sum[expert_count + 1],
         query_sum,
-        keyval_sum[:, :inner],
-        keyval_sum[:, inner:],
+        key_sum,
+        value_sum,
         output_sum,
         vector_sum[expert_count],
         vector_sum[:expert_count].T,

time: 591 us -> 536 us (0.907)
  starting transfers between devices: 112 us -> 65.5 us
  Pallas kernels: 151 us -> 190 us
  waiting for transfers between devices: 231 us -> 195 us
  other arithmetic: 42.1 us -> 19.6 us
  local copies, waits for them, and re-layouts: 31 us -> 41.5 us
    ppermute x11 -> x9, waiting for transfers between devices: 120 us -> 68.8 us  [row_swap(): return lax.ppermute(values, 'rows', [(j, j ^ other) for j in range(count)])]
    all_to_all x1, waiting for transfers between devices: 0.01 us -> 40.8 us  [local(): lax.all_to_all(add(after([part_of(y_all, member)], dq)[0], *y_near), 'seq...]
    pallas_call x2 -> x11, Pallas kernels: 26.7 us -> 65.6 us  [the longest x8 26.4 us: plus(): pl.pallas_call(plus_kernel, grid=(parts,), out_shape=struct((parts, rows,...]
    all_to_all x2, starting transfers between devices: 43.3 us -> 6.95 us  [local(): lax.all_to_all(values.reshape(rows_here, block, width), 'seq', 0, 0, tile...]
    ppermute x9, waiting for transfers between devices: 46.3 us -> 14.3 us  [onward(): return lax.ppermute(values, 'seq', [(j, to(j)) for j in range(shards)])]
    psum x1, waiting for transfers between devices: 0.01 us -> 23.6 us  [local(): shared = lax.psum(weights, ('rows', 'seq'))]
    ppermute x15, waiting for transfers between devices: 46.6 us -> 30.1 us  [across(): return lax.ppermute(values, 'seq', [(j, j ^ other) for j in range(shards)])]
    ppermute x15, starting transfers between devices: 34.2 us -> 20.3 us  [across(): return lax.ppermute(values, 'seq', [(j, j ^ other) for j in range(shards)])]
  transfers between devices with their start and end apart: 42 -> 39, of which waited for: 21 -> 16; matrix products, arithmetic and copies ran while one was open for 7% -> 7% of each run, Pallas kernels for 26% -> 34%
where the time goes in v4:
time: 536 us; the launch traced here: 526 us
  waiting for transfers between devices  195 us (36%)
  Pallas kernels  190 us (35%)
  starting transfers between devices  65.5 us (12%)
  local copies, waits for them, and re-layouts  41.5 us (8%)
  other arithmetic  19.6 us (4%)
  between operations  15.1 us (3%)
    ppermute x9, waiting for transfers between devices, row_swap(): return lax.ppermute(values, 'rows', [(j, j ^ other) for j in range(count)])  68.8 us
    pallas_call x4, Pallas kernels, local(): pl.pallas_call(functools.partial(expert_kernel, len(kept) + len(tied)), g...  63.4 us
    all_to_all x1, waiting for transfers between devices, local(): lax.all_to_all(add(after([part_of(y_all, member)], dq)[0], *y_near), 'seq...  40.8 us
    ppermute x15, waiting for transfers between devices, across(): return lax.ppermute(values, 'seq', [(j, j ^ other) for j in range(shards)])  30.1 us
    pallas_call x8, Pallas kernels, plus(): pl.pallas_call(plus_kernel, grid=(parts,), out_shape=struct((parts, rows,...  26.4 us
    pallas_call x1, Pallas kernels, local(): pl.pallas_call(functools.partial(attention_back_kernel, members, expert_c...  26.4 us
    unnamed x102, local copies, waits for them, and re-layouts  25.7 us
    psum x1, waiting for transfers between devices, local(): shared = lax.psum(weights, ('rows', 'seq'))  23.6 us
  transfers between devices with their start and end apart: 39, of which 16 were waited for; matrix products, arithmetic and copies ran while one was open for 7% of the time, Pallas kernels for 34%

profile of v4, /device:TPU:0, one launch (start us, length us, event | category | flops | bytes accessed | tf_op | source)
XLA Modules:
  0.0 526.1 jit_solution(4487006445543957318)
XLA Ops:
  12.1 7.3 %all-to-all-start = ((s32[8,9,256]{2,1,0:T(8,128)}), s32[8,9,256]{2,1,0:T(8,128)S(1)}, u32[]{:S(2)}, u32[]{:S(2)}) async-start(s32[8,9,256]{2,1,0:T(8,128)} %after.12), calls=%async_computation | async-start | bytes 262144 | tf_op jit(solution)/shard_map/all_to_all | solution.py:663
  21.4 2.4 collective-permute-start.3
  27.7 6.7 %all-to-all-done = s32[8,9,256]{2,1,0:T(8,128)S(1)} async-done(((s32[8,9,256]{2,1,0:T(8,128)}), s32[8,9,256]{2,1,0:T(8,128)S(1)}, u32[]{:S(2)}, u32[]{:S(2)}) %all-to-all-start) | async-done | bytes 73760 | tf_op jit(solution)/shard_map/all_to_all | solution.py:663
  36.9 8.0 %collective-permute-done.3.refs_4_ = bf16[64,1024]{1,0:T(8,128)(2,1)S(1)} collective-permute-done((bf16[64,1024]{1,0:T(8,128)(2,1)}, bf16[64,1024]{1,0:T(8,128)(2,1)S(1)}, u32[]{:S(2)}, u32[]{:S(2)}) %collective-permute-start.3) | collective-permute-done | bytes 131104 | tf_op jit(solution)/shard_map/ppermute | solution.py:636
  51.9 19.5 %front.1 = (bf16[512,1024]{1,0:T(8,128)(2,1)}, bf16[256,1024]{1,0:T(8,128)(2,1)}, bf16[4,4,256,128]{3,2,1,0:T(8,128)(2,1)}, bf16[512,512]{1,0:T(8,128)(2,1)}, bf...) custom-call(s32[10]{0:T(128)} %stack.109.me_ref, ...), custom_call_target="tpu_custom_call" | custom-call | flops 9749999616 | tf_op jit(solution)/shard_map/front/pallas_call | solution.py:695
  72.1 8.0 %collective-permute-start.7 = (bf16[272,1024]{1,0:T(8,128)(2,1)}, bf16[272,1024]{1,0:T(8,128)(2,1)S(1)}, u32[]{:S(2)}, u32[]{:S(2)}) collective-permute-start(bf16[272,1024]{1,0:T(8,128)(2,1)} %get-tuple-element.81.xa_ref.xg_ref), channel_id=1, source_target_pairs={{0,2},{1,3},{2,4},{3,5},{4,6},{5,7},{6,0},{7,1},{8,10},{9,11},{10,... | collective-permute-start | bytes 1671176 | tf_op jit(solution)/shard_map/ppermute | solution.py:636
  81.1 13.8 %collective-permute-done.8.refs_1_.xb_ref = bf16[272,1024]{1,0:T(8,128)(2,1)S(1)} collective-permute-done((bf16[272,1024]{1,0:T(8,128)(2,1)}, bf16[272,1024]{1,0:T(8,128)(2,1)S(1)}, u32[]{:S(2)}, u32[]{:S(2)}) %collective-permute-start.8) | collective-permute-done | bytes 557088 | tf_op jit(solution)/shard_map/ppermute | solution.py:639
  94.9 6.3 %collective-permute-done.7.refs_0_ = bf16[272,1024]{1,0:T(8,128)(2,1)S(1)} collective-permute-done((bf16[272,1024]{1,0:T(8,128)(2,1)}, bf16[272,1024]{1,0:T(8,128)(2,1)S(1)}, u32[]{:S(2)}, u32[]{:S(2)}) %collective-permute-start.7) | collective-permute-done | bytes 557088 | tf_op jit(solution)/shard_map/ppermute | solution.py:636
  102.0 3.4 collective-permute-start.13
  105.5 2.8 collective-permute-start.9
  110.9 15.8 %experts.4 = (bf16[272,1024]{1,0:T(8,128)(2,1)S(1)}, bf16[272,1024]{1,0:T(8,128)(2,1)S(1)}, bf16[2,4,256,1024]{3,2,1,0:T(8,128)(2,1)}, bf16[8,512,1024]{2,1,0:T(...) custom-call(s32[5]{0:T(128)S(1)} %stack.117.info_ref, ...), custom_call_target="tpu_custom_call" | custom-call | flops 8000000000 | tf_op jit(solution)/shard_map/experts/pallas_call | solution.py:751
  131.4 15.7 %experts.5 = (bf16[272,1024]{1,0:T(8,128)(2,1)S(1)}, bf16[272,1024]{1,0:T(8,128)(2,1)S(1)}, bf16[2,4,256,1024]{3,2,1,0:T(8,128)(2,1)}, bf16[8,512,1024]{2,1,0:T(...) custom-call(s32[5]{0:T(128)S(1)} %stack.123.info_ref, ...), custom_call_target="tpu_custom_call", output_to_operand_aliasing={{2}: (8, {}), {3}: (9, {}), {4}: (10, {}), {5}: (11, {}), {... | custom-call | flops 8000000000 | tf_op jit(solution)/shard_map/experts/pallas_call | solution.py:751
  149.7 15.9 %experts.6 = (bf16[272,1024]{1,0:T(8,128)(2,1)S(1)}, bf16[272,1024]{1,0:T(8,128)(2,1)}, bf16[2,4,256,1024]{3,2,1,0:T(8,128)(2,1)}, bf16[8,512,1024]{2,1,0:T(8,12...) custom-call(s32[5]{0:T(128)S(1)} %stack.120.info_ref, ...), custom_call_target="tpu_custom_call", output_to_operand_aliasing={{2}: (8, {}), {3}: (9, {}), {4}: (10, {}), {5}: (11, {}), {... | custom-call | flops 8000000000 | tf_op jit(solution)/shard_map/experts/pallas_call | solution.py:751
  169.5 15.9 %experts.7 = (bf16[272,1024]{1,0:T(8,128)(2,1)S(1)}, bf16[272,1024]{1,0:T(8,128)(2,1)}, bf16[2,4,256,1024]{3,2,1,0:T(8,128)(2,1)}, bf16[8,512,1024]{2,1,0:T(8,12...) custom-call(s32[5]{0:T(128)S(1)} %stack.114.info_ref, ...), custom_call_target="tpu_custom_call", output_to_operand_aliasing={{2}: (8, {}), {3}: (9, {}), {4}: (10, {}), {5}: (11, {}), {... | custom-call | flops 8000000000 | tf_op jit(solution)/shard_map/experts/pallas_call | solution.py:751
  191.3 2.1 collective-permute-done.16
  197.5 7.7 %collective-permute-done.14 = bf16[272,1024]{1,0:T(8,128)(2,1)S(1)} collective-permute-done((bf16[272,1024]{1,0:T(8,128)(2,1)}, bf16[272,1024]{1,0:T(8,128)(2,1)S(1)}, u32[]{:S(2)}, u32[]{:S(2)}) %collective-permute-start.14) | collective-permute-done | bytes 557088 | tf_op jit(solution)/shard_map/ppermute | solution.py:639
  208.8 3.0 dynamic-slice_bitcast_fusion.1
  212.0 19.3 %expert_grads.1 = (bf16[4,3,512,512]{3,2,1,0:T(8,128)(2,1)}, bf16[4,3,512,512]{3,2,1,0:T(8,128)(2,1)}) custom-call(s32[4]{0:T(128)} %pad_add_fusion.2.info_ref, bf16[8,512,1024]{2,1,0:T(8,128)(2,1)} %get-tuple-element.111.xs_ref, bf16[8,512,1024]{2,1,0:T(8,128)(2,1)} %get-tuple-element.112.us_ref, bf16[8,512,512]{2,1,0:T(8,128)(2,1)} %get-tuple-element.113.hs_ref, ...), custom_call_target="tpu_custom_call" | custom-call | flops 30000001024 | tf_op jit(solution)/shard_map/expert_grads/pallas_call | solution.py:831
  233.4 3.3 collective-permute-done.21.rest_1_
  238.7 4.0 middle.1
  247.5 3.1 dynamic-slice_bitcast_fusion.refs_0_
  250.6 26.4 %attention_back.1 = (bf16[256,1024]{1,0:T(8,128)(2,1)}, bf16[2,256,1024]{2,1,0:T(8,128)(2,1)}, bf16[3200,1024]{1,0:T(8,128)(2,1)}) custom-call(s32[2]{0:T(128)} %pad_add_fusion.1.me_ref, bf16[4,4,256,128]{3,2,1,0:T(8,128)(2,1)} %get-tuple-element.104.qz_ref, bf16[4,4,256,128]{3,2,1,0:T(8,128)(2,1)} %copy-done.12, bf16[512,512]{1,0:T(8,128)(2,1)} %get-tuple-element.118.k_ref, ...), custom_call_target="tpu_custom_call" | custom-call | flops 50000000 | tf_op jit(solution)/shard_map/attention_back/pallas_call | solution.py:869
  278.2 4.2 add_convert_fusion
  282.4 5.7 %all-to-all-start.1 = ((bf16[4,256,1024]{2,1,0:T(8,128)(2,1)}), bf16[4,256,1024]{2,1,0:T(8,128)(2,1)}, u32[]{:S(2)}, u32[]{:S(2)}) async-start(bf16[4,256,1024]{2,1,0:T(8,128)(2,1)} %add_convert_fusion), calls=%async_computation.1 | async-start | bytes 4194304 | tf_op jit(solution)/shard_map/all_to_all | solution.py:924
  290.8 2.8 copy-done
  293.5 3.9 plus.14.left_ref
  298.7 2.5 plus.12.left_ref
  303.9 4.1 last.1
  307.9 3.5 plus.10.left_ref
  311.9 40.8 %all-to-all-done.1.refs_1_ = bf16[4,256,1024]{2,1,0:T(8,128)(2,1)} async-done(((bf16[4,256,1024]{2,1,0:T(8,128)(2,1)}), bf16[4,256,1024]{2,1,0:T(8,128)(2,1)}, u32[]{:S(2)}, u32[]{:S(2)}) %all-to-all-start.1) | async-done | bytes 2097184 | tf_op jit(solution)/shard_map/all_to_all | solution.py:924
  352.7 3.5 all-to-all-start.3
  356.2 2.8 copy-done.1
  359.0 3.6 plus.8.left_ref
  366.8 9.3 %all-to-all-done.3.refs_1_.rest_1_ = bf16[4,64,1024]{2,1,0:T(8,128)(2,1)S(1)} async-done(((bf16[4,64,1024]{2,1,0:T(8,128)(2,1)}), bf16[4,64,1024]{2,1,0:T(8,128)(2,1)S(1)}, u32[]{:S(2)}, u32[]{:S(2)}) %all-to-all-start.3) | async-done | bytes 524320 | tf_op jit(solution)/shard_map/all_to_all | solution.py:929
  376.1 3.5 all-to-all-start.2
  379.6 3.9 plus.15.mine_ref
  383.5 3.5 plus.13.mine_ref
  387.6 33.8 %collective-permute-done.27.refs_0_ = bf16[3,512,512]{2,1,0:T(8,128)(2,1)} collective-permute-done((bf16[3,512,512]{2,1,0:T(8,128)(2,1)}, bf16[3,512,512]{2,1,0:T(8,128)(2,1)}, u32[]{:S(2)}, u32[]{:S(2)}) %collective-permute-start.27) | collective-permute-done | bytes 1572896 | tf_op jit(solution)/shard_map/ppermute | solution.py:643
  421.4 2.7 plus.11.mine_ref
  424.2 35.0 %collective-permute-done.25.refs_0_ = bf16[3,512,512]{2,1,0:T(8,128)(2,1)} collective-permute-done((bf16[3,512,512]{2,1,0:T(8,128)(2,1)}, bf16[3,512,512]{2,1,0:T(8,128)(2,1)}, u32[]{:S(2)}, u32[]{:S(2)}) %collective-permute-start.25) | collective-permute-done | bytes 1572896 | tf_op jit(solution)/shard_map/ppermute | solution.py:643
  459.2 2.7 plus.9.mine_ref
  463.1 4.9 finish.4
  468.0 5.0 finish.5
  473.0 4.4 finish.6
  477.4 3.5 finish.7
  480.9 23.6 %all-reduce.2.cloned.1.call-done.query_ref.keyval_ref.output_ref.vectors_ref = bf16[3200,1024]{1,0:T(8,128)(2,1)} async-done(((bf16[3200,1024]{1,0:T(8,128)(2,1)}), bf16[3200,1024]{1,0:T(8,128)(2,1)}) %all-reduce.2.cloned.1.call-update) | async-done | bytes 6553616 | tf_op jit(solution)/shard_map/psum | solution.py:956
  504.5 3.4 copy-done.2
  507.9 8.8 %spread.1 = (f32[1024,1024]{1,0:T(8,128)}, f32[1024,512]{1,0:T(8,128)}, f32[1024,512]{1,0:T(8,128)}, f32[1024,1024]{1,0:T(8,128)}, f32[128,1024]{1,0:T(8,128)S(1)}) custom-call(bf16[3200,1024]{1,0:T(8,128)(2,1)} %all-reduce.2.cloned.1.call-done.query_ref.keyval_ref.output_ref.vectors_ref, ...), custom_call_target="tpu_custom_call" | custom-call | flops 50000000 | tf_op jit(solution)/shard_map/spread/pallas_call | solution.py:960
  (214 shorter events, 75.3 us)
Async XLA Ops:
  7.2 101.6 %all-gather.3.cloned.1.call-start = ((), (), s32[]{:S(2)}) async-start(), calls=%async_computation.5 | async-start | bytes 4718592 | tf_op jit(solution)/shard_map/all_gather | solution.py:673
  12.1 22.3 %all-to-all-start = ((s32[8,9,256]{2,1,0:T(8,128)}), s32[8,9,256]{2,1,0:T(8,128)S(1)}, u32[]{:S(2)}, u32[]{:S(2)}) async-start(s32[8,9,256]{2,1,0:T(8,128)} %after.12), calls=%async_computation | async-start | bytes 262144 | tf_op jit(solution)/shard_map/all_to_all | solution.py:663
  19.4 16.4 %collective-permute-start.1 = (bf16[64,1024]{1,0:T(8,128)(2,1)}, bf16[64,1024]{1,0:T(8,128)(2,1)S(1)}, u32[]{:S(2)}, u32[]{:S(2)}) collective-permute-start(bf16[64,1024]{1,0:T(8,128)(2,1)} %get-tuple-element.155.refs_2_), channel_id=1, source_target_pairs={{0,2},{1,3},{2,4},{3,5},{4,6},{5,7},{6,0},{7,1},{8,10},{9,11},{10,... | collective-permute-start | bytes 393224 | tf_op jit(solution)/shard_map/ppermute | solution.py:636
  21.4 23.4 %collective-permute-start.3 = (bf16[64,1024]{1,0:T(8,128)(2,1)}, bf16[64,1024]{1,0:T(8,128)(2,1)S(1)}, u32[]{:S(2)}, u32[]{:S(2)}) collective-permute-start(bf16[64,1024]{1,0:T(8,128)(2,1)} %get-tuple-element.157.refs_3_), channel_id=1, source_target_pairs={{0,4},{1,5},{2,6},{3,7},{4,0},{5,1},{6,2},{7,3},{8,12},{9,13},{10,... | collective-permute-start | bytes 393224 | tf_op jit(solution)/shard_map/ppermute | solution.py:636
  23.8 21.5 %collective-permute-start.5 = (bf16[64,1024]{1,0:T(8,128)(2,1)}, bf16[64,1024]{1,0:T(8,128)(2,1)S(1)}, u32[]{:S(2)}, u32[]{:S(2)}) collective-permute-start(bf16[64,1024]{1,0:T(8,128)(2,1)} %get-tuple-element.154.refs_4_), channel_id=1, source_target_pairs={{0,6},{1,7},{2,0},{3,1},{4,2},{5,3},{6,4},{7,5},{8,14},{9,15},{10,... | collective-permute-start | bytes 393224 | tf_op jit(solution)/shard_map/ppermute | solution.py:636
  25.3 24.4 %collective-permute-start = (bf16[64,1024]{1,0:T(8,128)(2,1)}, bf16[64,1024]{1,0:T(8,128)(2,1)S(1)}, u32[]{:S(2)}, u32[]{:S(2)}) collective-permute-start(bf16[64,1024]{1,0:T(8,128)(2,1)} %get-tuple-element.156.refs_1_.refs_0_), channel_id=1, source_target_pairs={{0,1},{1,0},{2,3},{3,2},{4,5},{5,4},{6,7},{7,6},{8,9},{9,8},{10,11... | collective-permute-start | bytes 393224 | tf_op jit(solution)/shard_map/ppermute | solution.py:639
  35.8 13.9 %collective-permute-start.2 = (bf16[64,1024]{1,0:T(8,128)(2,1)S(1)}, bf16[64,1024]{1,0:T(8,128)(2,1)S(1)}, u32[]{:S(2)}, u32[]{:S(2)}) collective-permute-start(bf16[64,1024]{1,0:T(8,128)(2,1)S(1)} %collective-permute-done.1.refs_2_), channel_id=1, source_target_pairs={{0,1},{1,0},{2,3},{3,2},{4,5},{5,4},{6,7},{7,6},{8,9},{9,8},{10,11... | collective-permute-start | bytes 393224 | tf_op jit(solution)/shard_map/ppermute | solution.py:639
  44.9 5.0 collective-permute-start.4
  45.3 5.9 %collective-permute-start.6 = (bf16[64,1024]{1,0:T(8,128)(2,1)S(1)}, bf16[64,1024]{1,0:T(8,128)(2,1)S(1)}, u32[]{:S(2)}, u32[]{:S(2)}) collective-permute-start(bf16[64,1024]{1,0:T(8,128)(2,1)S(1)} %collective-permute-done.5.refs_6_), channel_id=1, source_target_pairs={{0,1},{1,0},{2,3},{3,2},{4,5},{5,4},{6,7},{7,6},{8,9},{9,8},{10,11... | collective-permute-start | bytes 393224 | tf_op jit(solution)/shard_map/ppermute | solution.py:639
  71.4 23.5 %collective-permute-start.8 = (bf16[272,1024]{1,0:T(8,128)(2,1)}, bf16[272,1024]{1,0:T(8,128)(2,1)S(1)}, u32[]{:S(2)}, u32[]{:S(2)}) collective-permute-start(bf16[272,1024]{1,0:T(8,128)(2,1)} %get-tuple-element.81.xa_ref.xg_ref), channel_id=1, source_target_pairs={{0,1},{1,0},{2,3},{3,2},{4,5},{5,4},{6,7},{7,6},{8,9},{9,8},{10,11... | collective-permute-start | bytes 1671176 | tf_op jit(solution)/shard_map/ppermute | solution.py:639
  72.1 29.1 %collective-permute-start.7 = (bf16[272,1024]{1,0:T(8,128)(2,1)}, bf16[272,1024]{1,0:T(8,128)(2,1)S(1)}, u32[]{:S(2)}, u32[]{:S(2)}) collective-permute-start(bf16[272,1024]{1,0:T(8,128)(2,1)} %get-tuple-element.81.xa_ref.xg_ref), channel_id=1, source_target_pairs={{0,2},{1,3},{2,4},{3,5},{4,6},{5,7},{6,0},{7,1},{8,10},{9,11},{10,... | collective-permute-start | bytes 1671176 | tf_op jit(solution)/shard_map/ppermute | solution.py:636
  102.0 29.3 %collective-permute-start.13 = (bf16[272,1024]{1,0:T(8,128)(2,1)}, bf16[272,1024]{1,0:T(8,128)(2,1)S(1)}, u32[]{:S(2)}, u32[]{:S(2)}) collective-permute-start(bf16[272,1024]{1,0:T(8,128)(2,1)} %after.13.xa_ref), channel_id=1, source_target_pairs={{0,1},{1,0},{2,3},{3,2},{4,5},{5,4},{6,7},{7,6},{8,9},{9,8},{10,11... | collective-permute-start | bytes 1671176 | tf_op jit(solution)/shard_map/ppermute | solution.py:639
  105.5 22.8 %collective-permute-start.9 = (bf16[272,1024]{1,0:T(8,128)(2,1)}, bf16[272,1024]{1,0:T(8,128)(2,1)S(1)}, u32[]{:S(2)}, u32[]{:S(2)}) collective-permute-start(bf16[272,1024]{1,0:T(8,128)(2,1)} %after.13.xa_ref), channel_id=1, source_target_pairs={{0,2},{1,3},{2,4},{3,5},{4,6},{5,7},{6,0},{7,1},{8,10},{9,11},{10,... | collective-permute-start | bytes 1671176 | tf_op jit(solution)/shard_map/ppermute | solution.py:636
  110.9 20.4 %copy-start.18 = (bf16[272,1024]{1,0:T(8,128)(2,1)S(1)}, bf16[272,1024]{1,0:T(8,128)(2,1)}, u32[]{:S(2)}) copy-start(bf16[272,1024]{1,0:T(8,128)(2,1)} %after.13.xa_ref) | copy-start | bytes 1671172
  129.1 20.6 %collective-permute-start.12 = (bf16[272,1024]{1,0:T(8,128)(2,1)}, bf16[272,1024]{1,0:T(8,128)(2,1)S(1)}, u32[]{:S(2)}, u32[]{:S(2)}) collective-permute-start(bf16[272,1024]{1,0:T(8,128)(2,1)} %after.14.xa_ref), channel_id=1, source_target_pairs={{0,1},{1,0},{2,3},{3,2},{4,5},{5,4},{6,7},{7,6},{8,9},{9,8},{10,11... | collective-permute-start | bytes 1671176 | tf_op jit(solution)/shard_map/ppermute | solution.py:639
  131.2 16.7 %collective-permute-start.10 = (bf16[272,1024]{1,0:T(8,128)(2,1)}, bf16[272,1024]{1,0:T(8,128)(2,1)S(1)}, u32[]{:S(2)}, u32[]{:S(2)}) collective-permute-start(bf16[272,1024]{1,0:T(8,128)(2,1)} %after.14.xa_ref), channel_id=1, source_target_pairs={{0,2},{1,3},{2,4},{3,5},{4,6},{5,7},{6,0},{7,1},{8,10},{9,11},{10,... | collective-permute-start | bytes 1671176 | tf_op jit(solution)/shard_map/ppermute | solution.py:636
  147.9 18.0 %collective-permute-start.11 = (bf16[272,1024]{1,0:T(8,128)(2,1)S(1)}, bf16[272,1024]{1,0:T(8,128)(2,1)S(1)}, u32[]{:S(2)}, u32[]{:S(2)}) collective-permute-start(bf16[272,1024]{1,0:T(8,128)(2,1)S(1)} %collective-permute-done.10.xa_ref), channel_id=1, source_target_pairs={{0,1},{1,0},{2,3},{3,2},{4,5},{5,4},{6,7},{7,6},{8,9},{9,8},{10,11... | collective-permute-start | bytes 1671176 | tf_op jit(solution)/shard_map/ppermute | solution.py:639
  165.6 21.2 %collective-permute-start.18 = (bf16[272,1024]{1,0:T(8,128)(2,1)}, bf16[272,1024]{1,0:T(8,128)(2,1)}, u32[]{:S(2)}, u32[]{:S(2)}) collective-permute-start(bf16[272,1024]{1,0:T(8,128)(2,1)} %get-tuple-element.109), channel_id=1, source_target_pairs={{0,1},{1,0},{2,3},{3,2},{4,5},{5,4},{6,7},{7,6},{8,9},{9,8},{10,11... | collective-permute-start | bytes 1671176 | tf_op jit(solution)/shard_map/ppermute | solution.py:639
  166.7 26.7 %collective-permute-start.16 = (bf16[272,1024]{1,0:T(8,128)(2,1)}, bf16[272,1024]{1,0:T(8,128)(2,1)}, u32[]{:S(2)}, u32[]{:S(2)}) collective-permute-start(bf16[272,1024]{1,0:T(8,128)(2,1)} %after.17), channel_id=1, source_target_pairs={{0,1},{1,0},{2,3},{3,2},{4,5},{5,4},{6,7},{7,6},{8,9},{9,8},{10,11... | collective-permute-start | bytes 1671176 | tf_op jit(solution)/shard_map/ppermute | solution.py:639
  185.4 19.8 %collective-permute-start.14 = (bf16[272,1024]{1,0:T(8,128)(2,1)}, bf16[272,1024]{1,0:T(8,128)(2,1)S(1)}, u32[]{:S(2)}, u32[]{:S(2)}) collective-permute-start(bf16[272,1024]{1,0:T(8,128)(2,1)} %get-tuple-element.103), channel_id=1, source_target_pairs={{0,1},{1,0},{2,3},{3,2},{4,5},{5,4},{6,7},{7,6},{8,9},{9,8},{10,11... | collective-permute-start | bytes 1671176 | tf_op jit(solution)/shard_map/ppermute | solution.py:639
  188.9 42.4 %collective-permute-start.19 = (bf16[272,1024]{1,0:T(8,128)(2,1)}, bf16[272,1024]{1,0:T(8,128)(2,1)}, u32[]{:S(2)}, u32[]{:S(2)}) collective-permute-start(bf16[272,1024]{1,0:T(8,128)(2,1)} %add_convert_fusion.2.rest_0_), channel_id=1, source_target_pairs={{0,4},{1,5},{2,6},{3,7},{4,0},{5,1},{6,2},{7,3},{8,12},{9,13},{10,... | collective-permute-start | bytes 1671176 | tf_op jit(solution)/shard_map/ppermute | solution.py:636
  189.4 41.9 %collective-permute-start.15 = (bf16[272,1024]{1,0:T(8,128)(2,1)}, bf16[272,1024]{1,0:T(8,128)(2,1)}, u32[]{:S(2)}, u32[]{:S(2)}) collective-permute-start(bf16[272,1024]{1,0:T(8,128)(2,1)} %after.16), channel_id=1, source_target_pairs={{0,1},{1,0},{2,3},{3,2},{4,5},{5,4},{6,7},{7,6},{8,9},{9,8},{10,11... | collective-permute-start | bytes 1671176 | tf_op jit(solution)/shard_map/ppermute | solution.py:639
  195.5 35.8 %collective-permute-start.17 = (bf16[272,1024]{1,0:T(8,128)(2,1)}, bf16[272,1024]{1,0:T(8,128)(2,1)}, u32[]{:S(2)}, u32[]{:S(2)}) collective-permute-start(bf16[272,1024]{1,0:T(8,128)(2,1)} %add_convert_fusion.3), channel_id=1, source_target_pairs={{0,6},{1,7},{2,0},{3,1},{4,2},{5,3},{6,4},{7,5},{8,14},{9,15},{10,... | collective-permute-start | bytes 1671176 | tf_op jit(solution)/shard_map/ppermute | solution.py:636
  207.3 24.0 %collective-permute-start.20 = (bf16[272,1024]{1,0:T(8,128)(2,1)S(1)}, bf16[272,1024]{1,0:T(8,128)(2,1)}, u32[]{:S(2)}, u32[]{:S(2)}) collective-permute-start(bf16[272,1024]{1,0:T(8,128)(2,1)S(1)} %add_convert_fusion.5.refs_1_.rest_1_), channel_id=1, source_target_pairs={{0,2},{1,3},{2,4},{3,5},{4,6},{5,7},{6,0},{7,1},{8,10},{9,11},{10,... | collective-permute-start | bytes 1671176 | tf_op jit(solution)/shard_map/ppermute | solution.py:636
  211.8 24.9 %collective-permute-start.21 = (bf16[2,256,1024]{2,1,0:T(8,128)(2,1)}, bf16[2,256,1024]{2,1,0:T(8,128)(2,1)S(1)}, u32[]{:S(2)}, u32[]{:S(2)}) collective-permute-start(bf16[2,256,1024]{2,1,0:T(8,128)(2,1)} %get-tuple-element.149), channel_id=1, source_target_pairs={{0,1},{1,0},{2,3},{3,2},{4,5},{5,4},{6,7},{7,6},{8,9},{9,8},{10,11... | collective-permute-start | bytes 3145736 | tf_op jit(solution)/shard_map/ppermute | solution.py:639
  212.0 25.7 %copy-start.13 = (f32[256,1024]{1,0:T(8,128)S(1)}, f32[256,1024]{1,0:T(8,128)}, u32[]{:S(2)}) copy-start(f32[256,1024]{1,0:T(8,128)} %get-tuple-element.80.res_ref) | copy-start | bytes 3145732
  212.0 25.7 %copy-start.30 = (bf16[1024,32]{0,1:T(8,128)(2,1)S(1)}, bf16[1024,32]{0,1:T(8,128)(2,1)}, u32[]{:S(2)}) copy-start(bf16[1024,32]{0,1:T(8,128)(2,1)} %param.24) | copy-start | bytes 196612
  212.0 25.7 %copy-start.32 = (f32[32,256]{1,0:T(8,128)S(1)}, f32[32,256]{1,0:T(8,128)}, u32[]{:S(2)}) copy-start(f32[32,256]{1,0:T(8,128)} %get-tuple-element.110.gates_ref) | copy-start | bytes 98308
  212.0 25.7 %copy-start.34 = (f32[1024]{0:T(1024)S(1)}, f32[1024]{0:T(1024)}, u32[]{:S(2)}) copy-start(f32[1024]{0:T(1024)} %param.23) | copy-start | bytes 12292
  245.2 45.5 %collective-permute-start.24 = (bf16[4,3,512,512]{3,2,1,0:T(8,128)(2,1)}, bf16[4,3,512,512]{3,2,1,0:T(8,128)(2,1)}, u32[]{:S(2)}, u32[]{:S(2)}) collective-permute-start(bf16[4,3,512,512]{3,2,1,0:T(8,128)(2,1)} %after.20), channel_id=1, source_target_pairs={{0,8},{8,0},{16,24},{24,16},{1,9},{9,1},{17,25},{25,17},{2,10},{10... | collective-permute-start | bytes 18874376 | tf_op jit(solution)/shard_map/ppermute | solution.py:643
  245.2 31.8 %collective-permute-start.22 = (bf16[2,256,1024]{2,1,0:T(8,128)(2,1)}, bf16[2,256,1024]{2,1,0:T(8,128)(2,1)S(1)}, u32[]{:S(2)}, u32[]{:S(2)}) collective-permute-start(bf16[2,256,1024]{2,1,0:T(8,128)(2,1)} %get-tuple-element.148), channel_id=1, source_target_pairs={{0,1},{1,0},{2,3},{3,2},{4,5},{5,4},{6,7},{7,6},{8,9},{9,8},{10,11... | collective-permute-start | bytes 3145736 | tf_op jit(solution)/shard_map/ppermute | solution.py:639
  282.4 70.2 %all-to-all-start.1 = ((bf16[4,256,1024]{2,1,0:T(8,128)(2,1)}), bf16[4,256,1024]{2,1,0:T(8,128)(2,1)}, u32[]{:S(2)}, u32[]{:S(2)}) async-start(bf16[4,256,1024]{2,1,0:T(8,128)(2,1)} %add_convert_fusion), calls=%async_computation.1 | async-start | bytes 4194304 | tf_op jit(solution)/shard_map/all_to_all | solution.py:924
  288.1 216.4 %all-reduce.2.cloned.1.call-start = ((), (), s32[]{:S(2)}) async-start(), calls=%async_computation.4 | async-start | bytes 13107200 | tf_op jit(solution)/shard_map/psum | solution.py:956
  289.0 14.9 %collective-permute-start.23 = (bf16[256,1024]{1,0:T(8,128)(2,1)}, bf16[256,1024]{1,0:T(8,128)(2,1)}, u32[]{:S(2)}, u32[]{:S(2)}) collective-permute-start(bf16[256,1024]{1,0:T(8,128)(2,1)} %get-tuple-element.150), channel_id=1, source_target_pairs={{0,1},{1,0},{2,3},{3,2},{4,5},{5,4},{6,7},{7,6},{8,9},{9,8},{10,11... | collective-permute-start | bytes 1572872 | tf_op jit(solution)/shard_map/ppermute | solution.py:639
  297.5 82.1 %collective-permute-start.31 = (bf16[3,512,512]{2,1,0:T(8,128)(2,1)}, bf16[3,512,512]{2,1,0:T(8,128)(2,1)}, u32[]{:S(2)}, u32[]{:S(2)}) collective-permute-start(bf16[3,512,512]{2,1,0:T(8,128)(2,1)} %plus.14.left_ref), channel_id=1, source_target_pairs={{0,16},{8,24},{16,0},{24,8},{1,17},{9,25},{17,1},{25,9},{2,18},{10... | collective-permute-start | bytes 4718600 | tf_op jit(solution)/shard_map/ppermute | solution.py:643
  301.2 82.2 %collective-permute-start.29 = (bf16[3,512,512]{2,1,0:T(8,128)(2,1)S(1)}, bf16[3,512,512]{2,1,0:T(8,128)(2,1)}, u32[]{:S(2)}, u32[]{:S(2)}) collective-permute-start(bf16[3,512,512]{2,1,0:T(8,128)(2,1)S(1)} %plus.12.left_ref), channel_id=1, source_target_pairs={{0,16},{8,24},{16,0},{24,8},{1,17},{9,25},{17,1},{25,9},{2,18},{10... | collective-permute-start | bytes 4718600 | tf_op jit(solution)/shard_map/ppermute | solution.py:643
  311.5 109.9 %collective-permute-start.27 = (bf16[3,512,512]{2,1,0:T(8,128)(2,1)}, bf16[3,512,512]{2,1,0:T(8,128)(2,1)}, u32[]{:S(2)}, u32[]{:S(2)}) collective-permute-start(bf16[3,512,512]{2,1,0:T(8,128)(2,1)} %plus.10.left_ref), channel_id=1, source_target_pairs={{0,16},{8,24},{16,0},{24,8},{1,17},{9,25},{17,1},{25,9},{2,18},{10... | collective-permute-start | bytes 4718600 | tf_op jit(solution)/shard_map/ppermute | solution.py:643
  352.7 23.4 %all-to-all-start.3 = ((bf16[4,64,1024]{2,1,0:T(8,128)(2,1)}), bf16[4,64,1024]{2,1,0:T(8,128)(2,1)S(1)}, u32[]{:S(2)}, u32[]{:S(2)}) async-start(bf16[4,64,1024]{2,1,0:T(8,128)(2,1)} %bitcast.41), calls=%async_computation.3 | async-start | bytes 1048576 | tf_op jit(solution)/shard_map/all_to_all | solution.py:929
  362.6 96.6 %collective-permute-start.25 = (bf16[3,512,512]{2,1,0:T(8,128)(2,1)}, bf16[3,512,512]{2,1,0:T(8,128)(2,1)}, u32[]{:S(2)}, u32[]{:S(2)}) collective-permute-start(bf16[3,512,512]{2,1,0:T(8,128)(2,1)} %plus.8.left_ref), channel_id=1, source_target_pairs={{0,16},{8,24},{16,0},{24,8},{1,17},{9,25},{17,1},{25,9},{2,18},{10... | collective-permute-start | bytes 4718600 | tf_op jit(solution)/shard_map/ppermute | solution.py:643
  376.1 48.1 %all-to-all-start.2 = ((bf16[4,64,1024]{2,1,0:T(8,128)(2,1)}), bf16[4,64,1024]{2,1,0:T(8,128)(2,1)S(1)}, u32[]{:S(2)}, u32[]{:S(2)}) async-start(bf16[4,64,1024]{2,1,0:T(8,128)(2,1)} %bitcast.38), calls=%async_computation.2 | async-start | bytes 1048576 | tf_op jit(solution)/shard_map/all_to_all | solution.py:929
  383.5 79.6 %collective-permute-start.32 = (bf16[3,512,512]{2,1,0:T(8,128)(2,1)}, bf16[3,512,512]{2,1,0:T(8,128)(2,1)}, u32[]{:S(2)}, u32[]{:S(2)}) collective-permute-start(bf16[3,512,512]{2,1,0:T(8,128)(2,1)} %plus.15.mine_ref), channel_id=1, source_target_pairs={{0,8},{8,0},{16,24},{24,16},{1,9},{9,1},{17,25},{25,17},{2,10},{10... | collective-permute-start | bytes 4718600 | tf_op jit(solution)/shard_map/ppermute | solution.py:643
  387.0 80.9 %collective-permute-start.30 = (bf16[3,512,512]{2,1,0:T(8,128)(2,1)}, bf16[3,512,512]{2,1,0:T(8,128)(2,1)}, u32[]{:S(2)}, u32[]{:S(2)}) collective-permute-start(bf16[3,512,512]{2,1,0:T(8,128)(2,1)} %plus.13.mine_ref), channel_id=1, source_target_pairs={{0,8},{8,0},{16,24},{24,16},{1,9},{9,1},{17,25},{25,17},{2,10},{10... | collective-permute-start | bytes 4718600 | tf_op jit(solution)/shard_map/ppermute | solution.py:643
  424.1 37.9 %copy-start.4 = (bf16[4,64,1024]{2,1,0:T(8,128)(2,1)S(1)}, bf16[4,64,1024]{2,1,0:T(8,128)(2,1)}, u32[]{:S(2)}) copy-start(bf16[4,64,1024]{2,1,0:T(8,128)(2,1)} %copy-done.3) | copy-start | bytes 1572868
  424.1 39.0 %copy-start.33 = (s32[4]{0:T(128)S(1)}, s32[4]{0:T(128)}, u32[]{:S(2)}) copy-start(s32[4]{0:T(128)} %pad_add_fusion.2.info_ref) | copy-start | bytes 52
  424.1 48.9 %collective-permute-start.28 = (bf16[3,512,512]{2,1,0:T(8,128)(2,1)S(1)}, bf16[3,512,512]{2,1,0:T(8,128)(2,1)}, u32[]{:S(2)}, u32[]{:S(2)}) collective-permute-start(bf16[3,512,512]{2,1,0:T(8,128)(2,1)S(1)} %plus.11.mine_ref), channel_id=1, source_target_pairs={{0,8},{8,0},{16,24},{24,16},{1,9},{9,1},{17,25},{25,17},{2,10},{10... | collective-permute-start | bytes 4718600 | tf_op jit(solution)/shard_map/ppermute | solution.py:643
  424.2 35.0 %copy-start.5 = (bf16[4,64,1024]{2,1,0:T(8,128)(2,1)}, bf16[4,64,1024]{2,1,0:T(8,128)(2,1)S(1)}, u32[]{:S(2)}) copy-start(bf16[4,64,1024]{2,1,0:T(8,128)(2,1)S(1)} %all-to-all-done.2.refs_1_.rest_0_) | copy-start | bytes 1572868
  461.9 15.5 %collective-permute-start.26 = (bf16[3,512,512]{2,1,0:T(8,128)(2,1)S(1)}, bf16[3,512,512]{2,1,0:T(8,128)(2,1)S(1)}, u32[]{:S(2)}, u32[]{:S(2)}) collective-permute-start(bf16[3,512,512]{2,1,0:T(8,128)(2,1)S(1)} %plus.9.mine_ref), channel_id=1, source_target_pairs={{0,8},{8,0},{16,24},{24,16},{1,9},{9,1},{17,25},{25,17},{2,10},{10... | collective-permute-start | bytes 4718600 | tf_op jit(solution)/shard_map/ppermute | solution.py:643
  477.4 27.1 %copy-start.6 = (bf16[4,64,1024]{2,1,0:T(8,128)(2,1)S(1)}, bf16[4,64,1024]{2,1,0:T(8,128)(2,1)}, u32[]{:S(2)}) copy-start(bf16[4,64,1024]{2,1,0:T(8,128)(2,1)} %copy-done.5) | copy-start | bytes 1572868
  (41 other events, 183.1 us)
Sparse Core Ops, SparseCore 0:
  10.1 98.6 all-gather.2
  294.7 209.7 all-reduce.1

commit v5 on v4

--- a/solution.py
+++ b/solution.py
@@ -107,7 +107,7 @@
 
 def probabilities(stacked, key_tile, allowed):
     keys = key_tile.shape[0]
-    scores = mul(stacked, key_tile, NT) * HEAD_DIM**-0.5
+    scores = mul(stacked, key_tile, NT)
     scores = scores.reshape(4, BLOCK, keys)
     scores = jnp.where(allowed[None], scores, NEG)
     weights = jnp.exp(scores - jnp.max(scores, axis=-1, keepdims=True))
@@ -154,8 +154,9 @@
     xg_ref,
     gates_ref,
     input_ref,
-    h_ref,
+    *rest,
 ):
+    probs_refs, h_ref = rest[:-1], rest[-1]
     member = me_ref[0]
     length, width = h_ref.shape
     tokens = own_ref.shape[0]
@@ -192,7 +193,7 @@
             cosine, sine = cos_ref[own[piece], :], sin_ref[own[piece], :]
             first = rotate(pre[rows, :LANES], cosine, sine)
             second = rotate(pre[rows, LANES:], cosine, sine)
-            qz_ref[piece, tile] = spread_heads(first, second).astype(BF16)
+            qz_ref[piece, tile] = (spread_heads(first, second) * HEAD_DIM**-0.5).astype(BF16)
         return carry
 
     lax.fori_loop(0, TILES, query_step, 0)
@@ -204,7 +205,9 @@
         def attend(tile, carry):
             lanes = pl.ds(pl.multiple_of(tile * LANES, LANES), LANES)
             probs = probabilities(qz_ref[piece, tile], k_ref[:keys, lanes], allowed)
-            first, second = gather_heads(mul(probs.astype(BF16), v_ref[:keys, lanes]))
+            probs = probs.astype(BF16)
+            probs_refs[piece][tile] = probs
+            first, second = gather_heads(mul(probs, v_ref[:keys, lanes]))
             at = pl.multiple_of(tile * 256, 256)
             att_ref[rows, pl.ds(at, LANES)] = first.astype(BF16)
             att_ref[rows, pl.ds(at + LANES, LANES)] = second.astype(BF16)
@@ -292,7 +295,7 @@
     gate_pre = mul(entering, wg_ref[0])
     up_pre = mul(entering, wu_ref[0])
     product = mul(jnp.concatenate(leaving, axis=0), wd_ref[0], NT)
-    share = 1.0 / (1.0 + jnp.exp(-gate_pre))
+    share = 0.5 * jnp.tanh(0.5 * gate_pre) + 0.5
     silu = gate_pre * share
     hidden = silu * up_pre
     grad_gate = jnp.sum(hidden * product, axis=1, keepdims=True)
@@ -391,7 +394,7 @@
         out_shape=struct((parts, rows, columns), left.dtype),
         in_specs=[source, source],
         out_specs=entry,
-        compiler_params=params(16),
+        compiler_params=params(56),
         cost_estimate=took(0.1),
         name="plus",
     )(left, right)
@@ -473,7 +476,23 @@
     gaz_ref,
     k_ref,
     v_ref,
-    pos_ref,
+    *refs,
+):
+    pieces = gaz_ref.shape[0]
+    attention_back_body(
+        members, experts, me_ref, qz_ref, gaz_ref, k_ref, v_ref, refs[:pieces], *refs[pieces:]
+    )
+
+
+def attention_back_body(
+    members,
+    experts,
+    me_ref,
+    qz_ref,
+    gaz_ref,
+    k_ref,
+    v_ref,
+    probs_refs,
     cos_ref,
     sin_ref,
     mix_ref,
@@ -496,8 +515,7 @@
     dk_acc[...] = jnp.zeros_like(dk_acc)
     dv_acc[...] = jnp.zeros_like(dv_acc)
     for piece in range(pieces):
-        allowed = allowed_keys(piece, members, member, pos_ref)
-        keys = allowed.shape[1]
+        keys = (piece + 1) * members * BLOCK
         rows = slice(piece * BLOCK, (piece + 1) * BLOCK)
         at = pl.ds(pl.multiple_of((piece * members + member) * BLOCK, BLOCK), BLOCK)
 
@@ -505,13 +523,14 @@
             lanes = pl.ds(pl.multiple_of(tile * LANES, LANES), LANES)
             stacked, grads = qz_ref[piece, tile], gaz_ref[piece, tile]
             key_tile = k_ref[:keys, lanes]
-            probs = probabilities(stacked, key_tile, allowed)
-            grad_probs = mul(grads, v_ref[:keys, lanes], NT)
-            delta = jnp.sum(probs * grad_probs, axis=-1, keepdims=True)
-            grad_scores = (probs * (grad_probs - delta) * HEAD_DIM**-0.5).astype(BF16)
+            low_probs = probs_refs[piece][tile]
+            probs = low_probs.astype(F32)
+            weighted = probs * mul(grads, v_ref[:keys, lanes], NT)
+            delta = jnp.sum(weighted, axis=-1, keepdims=True)
+            grad_scores = (weighted - probs * delta).astype(BF16)
             dk_acc[:keys, lanes] += mul(grad_scores, stacked, TN)
-            dv_acc[:keys, lanes] += mul(probs.astype(BF16), grads, TN)
-            first, second = gather_heads(mul(grad_scores, key_tile))
+            dv_acc[:keys, lanes] += mul(low_probs, grads, TN)
+            first, second = gather_heads(mul(grad_scores, key_tile) * HEAD_DIM**-0.5)
             cosine, sine = cos_ref[at, :], sin_ref[at, :]
             out = pl.multiple_of(tile * 256, 256)
             dq_ref[rows, pl.ds(out, LANES)] = unrotate(first, cosine, sine).astype(BF16)
@@ -692,7 +711,7 @@
 
     gain_one, gain_two = first_gain.reshape(1, width), second_gain.reshape(1, width)
     router = router_weight.T
-    mix, own_mix, qz, k_row, v_row, att, residual, xg, gates, own_in = pl.pallas_call(
+    mix, own_mix, qz, k_row, v_row, att, residual, xg, gates, own_in, *probs = pl.pallas_call(
         functools.partial(front_kernel, members, shards),
         out_shape=[
             struct((length, width), BF16),
@@ -705,9 +724,13 @@
             struct((tokens + PAD, width), BF16),
             struct((expert_count, tokens), F32),
             struct((tokens, width), BF16),
+        ]
+        + [
+            struct((TILES, 4 * BLOCK, (piece + 1) * members * BLOCK), BF16)
+            for piece in range(rows_here)
         ],
         in_specs=[scalars()] + [whole()] * (shards + 11),
-        out_specs=[whole()] * 10,
+        out_specs=[whole()] * (10 + rows_here),
         scratch_shapes=[pltpu.VMEM((length, width), BF16)],
         compiler_params=params(56),
         cost_estimate=took(19.5),
@@ -874,7 +897,7 @@
             struct((3 * width + EXTRA, width), BF16),
         ],
         in_specs=[scalars()]
-        + [whole()] * 16
+        + [whole()] * (15 + rows_here)
         + [pl.BlockSpec(memory_space=pl.ANY)],
         out_specs=[whole()] * 3,
         scratch_shapes=[
@@ -891,7 +914,7 @@
         gaz,
         k_row,
         v_row,
-        own_pos,
+        *probs,
         cosine,
         sine,
         mix,
@@ -921,19 +944,17 @@
     )(dq, *dkv, query_weight, key_weight, value_weight, own_in, grad_residual, gain_one, *y_near[1])
 
     y_near = [jnp.concatenate(halves, axis=0) for halves in zip(*y_near)]
-    y_far = lax.all_to_all(
-        add(after([part_of(y_all, member)], dq)[0], *y_near), "seq", 0, 0, tiled=True, axis_index_groups=same_member
-    )
-    y_sum = jnp.sum(y_far.astype(F32), axis=0)
-    hidden_out = (residual + y_sum).astype(BF16)
+    y_total = add(after([part_of(y_all, member)], dq)[0], *y_near)
+    y_parts = [part_of(y_total, (row - k) % rows_here) for k in range(rows_here)]
+    y_sum = scatter(y_parts)
+    hidden_out = (residual + y_sum.astype(F32)).astype(BF16)
     back = lambda values: lax.all_to_all(
         values.reshape(rows_here, block, width), "seq", 0, 0, tiled=True, axis_index_groups=same_member
     )
     hidden_out, grad_in = back(hidden_out), back(grad_in)
     finished = []
     for e in range(experts):
-        served = {1: y_far, 2: grad_in, 3: hidden_out}.get(e)
-        crossed[e] = after([crossed[e]], served)[0] if e in (1, 2, 3) else crossed[e]
+        crossed[e] = after([crossed[e]], grad_in)[0] if e == 3 else crossed[e]
         mine[e] = plus(mine[e], crossed[e])
         grad_spec = lambda a, b: pl.BlockSpec((1, a, b), lambda i, e=e: (e, 0, 0))
         half = pl.BlockSpec(halves, lambda i: (0, 0, 0))
@@ -949,7 +970,7 @@
             + [pl.BlockSpec(memory_space=pl.ANY)] * len(finished),
             out_specs=[grad_spec(width, hidden), grad_spec(width, hidden), grad_spec(hidden, width)],
             input_output_aliases={3 + i: i for i in range(len(finished))},
-            compiler_params=params(32),
+            compiler_params=params(60),
             cost_estimate=took(0.1),
             name="finish",
         )(info, mine[e], row_swap(mine[e], 1), *finished)
@@ -968,7 +989,7 @@
             struct((EXTRA, width), F32),
         ],
         in_specs=[part(0), part(1), part(2), pl.BlockSpec((EXTRA, width), lambda r: (3 * width // EXTRA, 0))]
-        + [pl.BlockSpec(memory_space=pl.ANY)] * 3,
+        + [pl.BlockSpec(memory_space=pl.ANY)] * 2,
         out_specs=[
             rows_of(width),
             rows_of(inner),
@@ -979,7 +1000,8 @@
         compiler_params=params(24),
         cost_estimate=took(0.1),
         name="spread",
-    )(*[pltpu.with_memory_space_constraint(shared, pltpu.HBM)] * 4, hidden_out, grad_in, finished[0])
+    )(*[pltpu.with_memory_space_constraint(shared, pltpu.HBM)] * 4, grad_in, finished[0])
+    hidden_out = after([hidden_out], finished[0])[0]
     return (
         hidden_out,
         grad_in.astype(F32),

time: 536 us -> 536 us (level)
  waiting for transfers between devices: 195 us -> 184 us
    all_to_all x1 -> x0, waiting for transfers between devices: 40.8 us -> none  [local(): lax.all_to_all(add(after([part_of(y_all, member)], dq)[0], *y_near), 'seq...]
    ppermute x9 -> x12, waiting for transfers between devices: 14.3 us -> 40.2 us  [onward(): return lax.ppermute(values, 'seq', [(j, to(j)) for j in range(shards)])]
    ppermute x9, waiting for transfers between devices: 68.8 us -> 94.2 us  [row_swap(): return lax.ppermute(values, 'rows', [(j, j ^ other) for j in range(count)])]
    psum x1, waiting for transfers between devices: 23.6 us -> 0.01 us  [local(): shared = lax.psum(weights, ('rows', 'seq'))]
    ppermute x15, waiting for transfers between devices: 30.1 us -> 42 us  [across(): return lax.ppermute(values, 'seq', [(j, j ^ other) for j in range(shards)])]
    ppermute x9 -> x12, starting transfers between devices: 20.8 us -> 31.9 us  [onward(): return lax.ppermute(values, 'seq', [(j, to(j)) for j in range(shards)])]
    all_to_all x2, waiting for transfers between devices: 9.26 us -> 0.01 us  [local(): lax.all_to_all(values.reshape(rows_here, block, width), 'seq', 0, 0, tile...]
    all_to_all x1 -> x0, starting transfers between devices: 5.68 us -> none  [local(): lax.all_to_all(add(after([part_of(y_all, member)], dq)[0], *y_near), 'seq...]
  transfers between devices with their start and end apart: 39 -> 41, of which waited for: 16 -> 15; matrix products, arithmetic and copies ran while one was open for 7% -> 7% of each run, Pallas kernels for 34% -> 36%
where the time goes in v5:
time: 536 us; the launch traced here: 526 us
  Pallas kernels  195 us (36%)
  waiting for transfers between devices  184 us (34%)
  starting transfers between devices  70.3 us (13%)
  local copies, waits for them, and re-layouts  43.9 us (8%)
  other arithmetic  17.9 us (3%)
  between operations  15 us (3%)
    ppermute x9, waiting for transfers between devices, row_swap(): return lax.ppermute(values, 'rows', [(j, j ^ other) for j in range(count)])  94.2 us
    pallas_call x4, Pallas kernels, local(): pl.pallas_call(functools.partial(expert_kernel, len(kept) + len(tied)), g...  63.2 us
    ppermute x15, waiting for transfers between devices, across(): return lax.ppermute(values, 'seq', [(j, j ^ other) for j in range(shards)])  42 us
    ppermute x12, waiting for transfers between devices, onward(): return lax.ppermute(values, 'seq', [(j, to(j)) for j in range(shards)])  40.2 us
    ppermute x12, starting transfers between devices, onward(): return lax.ppermute(values, 'seq', [(j, to(j)) for j in range(shards)])  31.9 us
    pallas_call x8, Pallas kernels, plus(): pl.pallas_call(plus_kernel, grid=(parts,), out_shape=struct((parts, rows,...  31.7 us
    unnamed x96, local copies, waits for them, and re-layouts  26.9 us
    pallas_call x1, Pallas kernels, local(): pl.pallas_call(functools.partial(attention_back_kernel, members, expert_c...  23.3 us
  transfers between devices with their start and end apart: 41, of which 15 were waited for; matrix products, arithmetic and copies ran while one was open for 7% of the time, Pallas kernels for 36%

profile of v5, /device:TPU:0, one launch (start us, length us, event | category | flops | bytes accessed | tf_op | source)
XLA Modules:
  0.0 525.9 jit_solution(8843678190977216379)
XLA Ops:
  12.1 7.3 %all-to-all-start = ((s32[8,9,256]{2,1,0:T(8,128)}), s32[8,9,256]{2,1,0:T(8,128)S(1)}, u32[]{:S(2)}, u32[]{:S(2)}) async-start(s32[8,9,256]{2,1,0:T(8,128)} %after.11), calls=%async_computation | async-start | bytes 262144 | tf_op jit(solution)/shard_map/all_to_all | solution.py:682
  21.4 2.4 collective-permute-start.3
  27.7 6.6 %all-to-all-done = s32[8,9,256]{2,1,0:T(8,128)S(1)} async-done(((s32[8,9,256]{2,1,0:T(8,128)}), s32[8,9,256]{2,1,0:T(8,128)S(1)}, u32[]{:S(2)}, u32[]{:S(2)}) %all-to-all-start) | async-done | bytes 73760 | tf_op jit(solution)/shard_map/all_to_all | solution.py:682
  36.9 7.9 %collective-permute-done.3.refs_4_ = bf16[64,1024]{1,0:T(8,128)(2,1)S(1)} collective-permute-done((bf16[64,1024]{1,0:T(8,128)(2,1)}, bf16[64,1024]{1,0:T(8,128)(2,1)S(1)}, u32[]{:S(2)}, u32[]{:S(2)}) %collective-permute-start.3) | collective-permute-done | bytes 131104 | tf_op jit(solution)/shard_map/ppermute | solution.py:655
  51.8 20.5 %front.1 = (bf16[512,1024]{1,0:T(8,128)(2,1)}, bf16[256,1024]{1,0:T(8,128)(2,1)}, bf16[4,4,256,128]{3,2,1,0:T(8,128)(2,1)}, bf16[512,512]{1,0:T(8,128)(2,1)}, bf...) custom-call(s32[10]{0:T(128)} %stack.109.me_ref, ...), custom_call_target="tpu_custom_call" | custom-call | flops 9749999616 | tf_op jit(solution)/shard_map/front/pallas_call | solution.py:714
  72.9 8.1 %collective-permute-start.7 = (bf16[272,1024]{1,0:T(8,128)(2,1)}, bf16[272,1024]{1,0:T(8,128)(2,1)S(1)}, u32[]{:S(2)}, u32[]{:S(2)}) collective-permute-start(bf16[272,1024]{1,0:T(8,128)(2,1)} %get-tuple-element.85.xa_ref.xg_ref), channel_id=1, source_target_pairs={{0,2},{1,3},{2,4},{3,5},{4,6},{5,7},{6,0},{7,1},{8,10},{9,11},{10,... | collective-permute-start | bytes 1671176 | tf_op jit(solution)/shard_map/ppermute | solution.py:655
  82.1 12.9 %collective-permute-done.8.refs_1_.xb_ref = bf16[272,1024]{1,0:T(8,128)(2,1)S(1)} collective-permute-done((bf16[272,1024]{1,0:T(8,128)(2,1)}, bf16[272,1024]{1,0:T(8,128)(2,1)S(1)}, u32[]{:S(2)}, u32[]{:S(2)}) %collective-permute-start.8) | collective-permute-done | bytes 557088 | tf_op jit(solution)/shard_map/ppermute | solution.py:658
  95.0 7.7 %collective-permute-done.7.refs_0_ = bf16[272,1024]{1,0:T(8,128)(2,1)S(1)} collective-permute-done((bf16[272,1024]{1,0:T(8,128)(2,1)}, bf16[272,1024]{1,0:T(8,128)(2,1)S(1)}, u32[]{:S(2)}, u32[]{:S(2)}) %collective-permute-start.7) | collective-permute-done | bytes 557088 | tf_op jit(solution)/shard_map/ppermute | solution.py:655
  103.5 2.8 collective-permute-start.13
  110.9 15.8 %experts.4 = (bf16[272,1024]{1,0:T(8,128)(2,1)S(1)}, bf16[272,1024]{1,0:T(8,128)(2,1)S(1)}, bf16[2,4,256,1024]{3,2,1,0:T(8,128)(2,1)}, bf16[8,512,1024]{2,1,0:T(...) custom-call(s32[5]{0:T(128)S(1)} %stack.117.info_ref, ...), custom_call_target="tpu_custom_call" | custom-call | flops 8000000000 | tf_op jit(solution)/shard_map/experts/pallas_call | solution.py:774
  131.2 15.7 %experts.5 = (bf16[272,1024]{1,0:T(8,128)(2,1)S(1)}, bf16[272,1024]{1,0:T(8,128)(2,1)S(1)}, bf16[2,4,256,1024]{3,2,1,0:T(8,128)(2,1)}, bf16[8,512,1024]{2,1,0:T(...) custom-call(s32[5]{0:T(128)S(1)} %stack.123.info_ref, ...), custom_call_target="tpu_custom_call", output_to_operand_aliasing={{2}: (8, {}), {3}: (9, {}), {4}: (10, {}), {5}: (11, {}), {... | custom-call | flops 8000000000 | tf_op jit(solution)/shard_map/experts/pallas_call | solution.py:774
  149.8 15.9 %experts.6 = (bf16[272,1024]{1,0:T(8,128)(2,1)S(1)}, bf16[272,1024]{1,0:T(8,128)(2,1)}, bf16[2,4,256,1024]{3,2,1,0:T(8,128)(2,1)}, bf16[8,512,1024]{2,1,0:T(8,12...) custom-call(s32[5]{0:T(128)S(1)} %stack.120.info_ref, ...), custom_call_target="tpu_custom_call", output_to_operand_aliasing={{2}: (8, {}), {3}: (9, {}), {4}: (10, {}), {5}: (11, {}), {... | custom-call | flops 8000000000 | tf_op jit(solution)/shard_map/experts/pallas_call | solution.py:774
  169.6 15.8 %experts.7 = (bf16[272,1024]{1,0:T(8,128)(2,1)S(1)}, bf16[272,1024]{1,0:T(8,128)(2,1)S(1)}, bf16[2,4,256,1024]{3,2,1,0:T(8,128)(2,1)}, bf16[8,512,1024]{2,1,0:T(...) custom-call(s32[5]{0:T(128)S(1)} %stack.114.info_ref, ...), custom_call_target="tpu_custom_call", output_to_operand_aliasing={{2}: (8, {}), {3}: (9, {}), {4}: (10, {}), {5}: (11, {}), {... | custom-call | flops 8000000000 | tf_op jit(solution)/shard_map/experts/pallas_call | solution.py:774
  191.3 2.3 collective-permute-done.16
  193.6 2.1 add_convert_fusion.3
  197.6 7.8 %collective-permute-done.14 = bf16[272,1024]{1,0:T(8,128)(2,1)S(1)} collective-permute-done((bf16[272,1024]{1,0:T(8,128)(2,1)S(1)}, bf16[272,1024]{1,0:T(8,128)(2,1)S(1)}, u32[]{:S(2)}, u32[]{:S(2)}) %collective-permute-start.14) | collective-permute-done | bytes 557088 | tf_op jit(solution)/shard_map/ppermute | solution.py:658
  207.7 3.0 dynamic-slice_bitcast_fusion.1
  210.8 19.5 %expert_grads.1 = (bf16[4,3,512,512]{3,2,1,0:T(8,128)(2,1)}, bf16[4,3,512,512]{3,2,1,0:T(8,128)(2,1)}) custom-call(s32[4]{0:T(128)} %pad_add_fusion.2.info_ref, bf16[8,512,1024]{2,1,0:T(8,128)(2,1)} %get-tuple-element.115.xs_ref, bf16[8,512,1024]{2,1,0:T(8,128)(2,1)} %get-tuple-element.116.us_ref, bf16[8,512,512]{2,1,0:T(8,128)(2,1)} %get-tuple-element.117.hs_ref, ...), custom_call_target="tpu_custom_call" | custom-call | flops 30000001024 | tf_op jit(solution)/shard_map/expert_grads/pallas_call | solution.py:854
  232.4 4.2 collective-permute-done.21.rest_1_
  237.7 4.0 middle.1
  248.0 23.3 %attention_back.1 = (bf16[256,1024]{1,0:T(8,128)(2,1)}, bf16[2,256,1024]{2,1,0:T(8,128)(2,1)}, bf16[3200,1024]{1,0:T(8,128)(2,1)}) custom-call(s32[2]{0:T(128)} %pad_add_fusion.1.me_ref, bf16[4,4,256,128]{3,2,1,0:T(8,128)(2,1)} %get-tuple-element.108.qz_ref, bf16[4,4,256,128]{3,2,1,0:T(8,128)(2,1)} %copy-done.8, bf16[512,512]{1,0:T(8,128)(2,1)} %get-tuple-element.122.k_ref, ...), custom_call_target="tpu_custom_call" | custom-call | flops 50000000 | tf_op jit(solution)/shard_map/attention_back/pallas_call | solution.py:892
  271.4 3.9 plus.14.left_ref
  276.7 4.1 plus.12.left_ref
  281.1 4.1 plus.10.left_ref
  287.0 3.9 plus.8.left_ref
  293.2 3.2 dynamic-slice_bitcast_fusion.refs_0_
  296.4 13.3 %collective-permute-done.28.refs_1_ = bf16[256,1024]{1,0:T(8,128)(2,1)} collective-permute-done((bf16[256,1024]{1,0:T(8,128)(2,1)}, bf16[256,1024]{1,0:T(8,128)(2,1)}, u32[]{:S(2)}, u32[]{:S(2)}) %collective-permute-start.28) | collective-permute-done | bytes 524320 | tf_op jit(solution)/shard_map/ppermute | solution.py:658
  312.0 4.1 last.1
  316.2 5.7 %all-to-all-start.2 = ((bf16[4,64,1024]{2,1,0:T(8,128)(2,1)}), bf16[4,64,1024]{2,1,0:T(8,128)(2,1)S(1)}, u32[]{:S(2)}, u32[]{:S(2)}) async-start(bf16[4,64,1024]{2,1,0:T(8,128)(2,1)} %bitcast.45), calls=%async_computation.2 | async-start | bytes 1048576 | tf_op jit(solution)/shard_map/all_to_all | solution.py:951
  321.9 3.3 add_convert_fusion
  327.7 3.8 collective-permute-start.23
  332.7 3.9 plus.15.mine_ref
  336.6 27.5 %collective-permute-done.32.right_ref = bf16[3,512,512]{2,1,0:T(8,128)(2,1)} collective-permute-done((bf16[3,512,512]{2,1,0:T(8,128)(2,1)}, bf16[3,512,512]{2,1,0:T(8,128)(2,1)}, u32[]{:S(2)}, u32[]{:S(2)}) %collective-permute-start.32) | collective-permute-done | bytes 1572896 | tf_op jit(solution)/shard_map/ppermute | solution.py:662
  364.1 3.9 plus.13.mine_ref
  368.0 32.1 %collective-permute-done.30.right_ref = bf16[3,512,512]{2,1,0:T(8,128)(2,1)} collective-permute-done((bf16[3,512,512]{2,1,0:T(8,128)(2,1)}, bf16[3,512,512]{2,1,0:T(8,128)(2,1)}, u32[]{:S(2)}, u32[]{:S(2)}) %collective-permute-start.30) | collective-permute-done | bytes 1572896 | tf_op jit(solution)/shard_map/ppermute | solution.py:662
  400.1 3.9 plus.11.mine_ref
  404.0 34.6 %collective-permute-done.27.refs_0_ = bf16[3,512,512]{2,1,0:T(8,128)(2,1)} collective-permute-done((bf16[3,512,512]{2,1,0:T(8,128)(2,1)}, bf16[3,512,512]{2,1,0:T(8,128)(2,1)}, u32[]{:S(2)}, u32[]{:S(2)}) %collective-permute-start.27) | collective-permute-done | bytes 1572896 | tf_op jit(solution)/shard_map/ppermute | solution.py:662
  439.4 4.0 plus.9.mine_ref
  444.0 6.3 %collective-permute-start.25 = (bf16[256,1024]{1,0:T(8,128)(2,1)S(1)}, bf16[256,1024]{1,0:T(8,128)(2,1)S(1)}, u32[]{:S(2)}, u32[]{:S(2)}) collective-permute-start(bf16[256,1024]{1,0:T(8,128)(2,1)S(1)} %copy-done.39), channel_id=1, source_target_pairs={{0,2},{1,3},{2,4},{3,5},{4,6},{5,7},{6,0},{7,1},{8,10},{9,11},{10,... | collective-permute-start | bytes 1572872 | tf_op jit(solution)/shard_map/ppermute | solution.py:655
  450.2 24.5 %collective-permute-done.25 = bf16[256,1024]{1,0:T(8,128)(2,1)S(1)} collective-permute-done((bf16[256,1024]{1,0:T(8,128)(2,1)S(1)}, bf16[256,1024]{1,0:T(8,128)(2,1)S(1)}, u32[]{:S(2)}, u32[]{:S(2)}) %collective-permute-start.25) | collective-permute-done | bytes 524320 | tf_op jit(solution)/shard_map/ppermute | solution.py:655
  474.8 2.6 add_convert_fusion.6
  477.3 3.5 all-to-all-start.1
  483.0 4.9 finish.4
  487.9 4.9 finish.5
  492.8 4.9 finish.6
  497.7 4.9 finish.7
  502.5 3.4 copy-done
  505.9 8.8 %spread.1 = (f32[1024,1024]{1,0:T(8,128)}, f32[1024,512]{1,0:T(8,128)}, f32[1024,512]{1,0:T(8,128)}, f32[1024,1024]{1,0:T(8,128)}, f32[128,1024]{1,0:T(8,128)S(1)}) custom-call(bf16[3200,1024]{1,0:T(8,128)(2,1)} %all-reduce.2.cloned.1.call-done.query_ref.keyval_ref.output_ref.vectors_ref, ...), custom_call_target="tpu_custom_call" | custom-call | flops 50000000 | tf_op jit(solution)/shard_map/spread/pallas_call | solution.py:981
  (210 shorter events, 77.6 us)
Async XLA Ops:
  7.2 101.6 %all-gather.3.cloned.1.call-start = ((), (), s32[]{:S(2)}) async-start(), calls=%async_computation.4 | async-start | bytes 4718592 | tf_op jit(solution)/shard_map/all_gather | solution.py:692
  12.1 22.2 %all-to-all-start = ((s32[8,9,256]{2,1,0:T(8,128)}), s32[8,9,256]{2,1,0:T(8,128)S(1)}, u32[]{:S(2)}, u32[]{:S(2)}) async-start(s32[8,9,256]{2,1,0:T(8,128)} %after.11), calls=%async_computation | async-start | bytes 262144 | tf_op jit(solution)/shard_map/all_to_all | solution.py:682
  19.4 483.1 %all-reduce.2.cloned.1.call-start = ((), (), s32[]{:S(2)}) async-start(), calls=%async_computation.3 | async-start | bytes 13107200 | tf_op jit(solution)/shard_map/psum | solution.py:977
  19.5 16.3 %collective-permute-start.1 = (bf16[64,1024]{1,0:T(8,128)(2,1)}, bf16[64,1024]{1,0:T(8,128)(2,1)S(1)}, u32[]{:S(2)}, u32[]{:S(2)}) collective-permute-start(bf16[64,1024]{1,0:T(8,128)(2,1)} %get-tuple-element.166.refs_2_), channel_id=1, source_target_pairs={{0,2},{1,3},{2,4},{3,5},{4,6},{5,7},{6,0},{7,1},{8,10},{9,11},{10,... | collective-permute-start | bytes 393224 | tf_op jit(solution)/shard_map/ppermute | solution.py:655
  21.4 23.3 %collective-permute-start.3 = (bf16[64,1024]{1,0:T(8,128)(2,1)}, bf16[64,1024]{1,0:T(8,128)(2,1)S(1)}, u32[]{:S(2)}, u32[]{:S(2)}) collective-permute-start(bf16[64,1024]{1,0:T(8,128)(2,1)} %get-tuple-element.168.refs_3_), channel_id=1, source_target_pairs={{0,4},{1,5},{2,6},{3,7},{4,0},{5,1},{6,2},{7,3},{8,12},{9,13},{10,... | collective-permute-start | bytes 393224 | tf_op jit(solution)/shard_map/ppermute | solution.py:655
  23.8 21.5 %collective-permute-start.5 = (bf16[64,1024]{1,0:T(8,128)(2,1)}, bf16[64,1024]{1,0:T(8,128)(2,1)S(1)}, u32[]{:S(2)}, u32[]{:S(2)}) collective-permute-start(bf16[64,1024]{1,0:T(8,128)(2,1)} %get-tuple-element.165.refs_4_), channel_id=1, source_target_pairs={{0,6},{1,7},{2,0},{3,1},{4,2},{5,3},{6,4},{7,5},{8,14},{9,15},{10,... | collective-permute-start | bytes 393224 | tf_op jit(solution)/shard_map/ppermute | solution.py:655
  25.3 24.3 %collective-permute-start = (bf16[64,1024]{1,0:T(8,128)(2,1)}, bf16[64,1024]{1,0:T(8,128)(2,1)S(1)}, u32[]{:S(2)}, u32[]{:S(2)}) collective-permute-start(bf16[64,1024]{1,0:T(8,128)(2,1)} %get-tuple-element.167.refs_1_.refs_0_), channel_id=1, source_target_pairs={{0,1},{1,0},{2,3},{3,2},{4,5},{5,4},{6,7},{7,6},{8,9},{9,8},{10,11... | collective-permute-start | bytes 393224 | tf_op jit(solution)/shard_map/ppermute | solution.py:658
  35.7 13.8 %collective-permute-start.2 = (bf16[64,1024]{1,0:T(8,128)(2,1)S(1)}, bf16[64,1024]{1,0:T(8,128)(2,1)S(1)}, u32[]{:S(2)}, u32[]{:S(2)}) collective-permute-start(bf16[64,1024]{1,0:T(8,128)(2,1)S(1)} %collective-permute-done.1.refs_2_), channel_id=1, source_target_pairs={{0,1},{1,0},{2,3},{3,2},{4,5},{5,4},{6,7},{7,6},{8,9},{9,8},{10,11... | collective-permute-start | bytes 393224 | tf_op jit(solution)/shard_map/ppermute | solution.py:658
  44.8 5.0 collective-permute-start.4
  45.3 5.8 %collective-permute-start.6 = (bf16[64,1024]{1,0:T(8,128)(2,1)S(1)}, bf16[64,1024]{1,0:T(8,128)(2,1)S(1)}, u32[]{:S(2)}, u32[]{:S(2)}) collective-permute-start(bf16[64,1024]{1,0:T(8,128)(2,1)S(1)} %collective-permute-done.5.refs_6_), channel_id=1, source_target_pairs={{0,1},{1,0},{2,3},{3,2},{4,5},{5,4},{6,7},{7,6},{8,9},{9,8},{10,11... | collective-permute-start | bytes 393224 | tf_op jit(solution)/shard_map/ppermute | solution.py:658
  72.2 22.7 %collective-permute-start.8 = (bf16[272,1024]{1,0:T(8,128)(2,1)}, bf16[272,1024]{1,0:T(8,128)(2,1)S(1)}, u32[]{:S(2)}, u32[]{:S(2)}) collective-permute-start(bf16[272,1024]{1,0:T(8,128)(2,1)} %get-tuple-element.85.xa_ref.xg_ref), channel_id=1, source_target_pairs={{0,1},{1,0},{2,3},{3,2},{4,5},{5,4},{6,7},{7,6},{8,9},{9,8},{10,11... | collective-permute-start | bytes 1671176 | tf_op jit(solution)/shard_map/ppermute | solution.py:658
  72.9 29.8 %collective-permute-start.7 = (bf16[272,1024]{1,0:T(8,128)(2,1)}, bf16[272,1024]{1,0:T(8,128)(2,1)S(1)}, u32[]{:S(2)}, u32[]{:S(2)}) collective-permute-start(bf16[272,1024]{1,0:T(8,128)(2,1)} %get-tuple-element.85.xa_ref.xg_ref), channel_id=1, source_target_pairs={{0,2},{1,3},{2,4},{3,5},{4,6},{5,7},{6,0},{7,1},{8,10},{9,11},{10,... | collective-permute-start | bytes 1671176 | tf_op jit(solution)/shard_map/ppermute | solution.py:655
  103.5 27.7 %collective-permute-start.13 = (bf16[272,1024]{1,0:T(8,128)(2,1)}, bf16[272,1024]{1,0:T(8,128)(2,1)S(1)}, u32[]{:S(2)}, u32[]{:S(2)}) collective-permute-start(bf16[272,1024]{1,0:T(8,128)(2,1)} %after.12.xa_ref), channel_id=1, source_target_pairs={{0,1},{1,0},{2,3},{3,2},{4,5},{5,4},{6,7},{7,6},{8,9},{9,8},{10,11... | collective-permute-start | bytes 1671176 | tf_op jit(solution)/shard_map/ppermute | solution.py:658
  106.3 22.0 %collective-permute-start.9 = (bf16[272,1024]{1,0:T(8,128)(2,1)}, bf16[272,1024]{1,0:T(8,128)(2,1)S(1)}, u32[]{:S(2)}, u32[]{:S(2)}) collective-permute-start(bf16[272,1024]{1,0:T(8,128)(2,1)} %after.12.xa_ref), channel_id=1, source_target_pairs={{0,2},{1,3},{2,4},{3,5},{4,6},{5,7},{6,0},{7,1},{8,10},{9,11},{10,... | collective-permute-start | bytes 1671176 | tf_op jit(solution)/shard_map/ppermute | solution.py:655
  129.1 20.7 %collective-permute-start.12 = (bf16[272,1024]{1,0:T(8,128)(2,1)}, bf16[272,1024]{1,0:T(8,128)(2,1)S(1)}, u32[]{:S(2)}, u32[]{:S(2)}) collective-permute-start(bf16[272,1024]{1,0:T(8,128)(2,1)} %after.13.xa_ref), channel_id=1, source_target_pairs={{0,1},{1,0},{2,3},{3,2},{4,5},{5,4},{6,7},{7,6},{8,9},{9,8},{10,11... | collective-permute-start | bytes 1671176 | tf_op jit(solution)/shard_map/ppermute | solution.py:658
  130.3 17.4 %collective-permute-start.10 = (bf16[272,1024]{1,0:T(8,128)(2,1)}, bf16[272,1024]{1,0:T(8,128)(2,1)S(1)}, u32[]{:S(2)}, u32[]{:S(2)}) collective-permute-start(bf16[272,1024]{1,0:T(8,128)(2,1)} %after.13.xa_ref), channel_id=1, source_target_pairs={{0,2},{1,3},{2,4},{3,5},{4,6},{5,7},{6,0},{7,1},{8,10},{9,11},{10,... | collective-permute-start | bytes 1671176 | tf_op jit(solution)/shard_map/ppermute | solution.py:655
  147.8 18.0 %collective-permute-start.11 = (bf16[272,1024]{1,0:T(8,128)(2,1)S(1)}, bf16[272,1024]{1,0:T(8,128)(2,1)S(1)}, u32[]{:S(2)}, u32[]{:S(2)}) collective-permute-start(bf16[272,1024]{1,0:T(8,128)(2,1)S(1)} %collective-permute-done.10.xa_ref), channel_id=1, source_target_pairs={{0,1},{1,0},{2,3},{3,2},{4,5},{5,4},{6,7},{7,6},{8,9},{9,8},{10,11... | collective-permute-start | bytes 1671176 | tf_op jit(solution)/shard_map/ppermute | solution.py:658
  165.8 20.8 %collective-permute-start.18 = (bf16[272,1024]{1,0:T(8,128)(2,1)}, bf16[272,1024]{1,0:T(8,128)(2,1)}, u32[]{:S(2)}, u32[]{:S(2)}) collective-permute-start(bf16[272,1024]{1,0:T(8,128)(2,1)} %get-tuple-element.113), channel_id=1, source_target_pairs={{0,1},{1,0},{2,3},{3,2},{4,5},{5,4},{6,7},{7,6},{8,9},{9,8},{10,11... | collective-permute-start | bytes 1671176 | tf_op jit(solution)/shard_map/ppermute | solution.py:658
  166.6 27.0 %collective-permute-start.16 = (bf16[272,1024]{1,0:T(8,128)(2,1)}, bf16[272,1024]{1,0:T(8,128)(2,1)}, u32[]{:S(2)}, u32[]{:S(2)}) collective-permute-start(bf16[272,1024]{1,0:T(8,128)(2,1)} %after.16), channel_id=1, source_target_pairs={{0,1},{1,0},{2,3},{3,2},{4,5},{5,4},{6,7},{7,6},{8,9},{9,8},{10,11... | collective-permute-start | bytes 1671176 | tf_op jit(solution)/shard_map/ppermute | solution.py:658
  185.4 20.0 %collective-permute-start.14 = (bf16[272,1024]{1,0:T(8,128)(2,1)S(1)}, bf16[272,1024]{1,0:T(8,128)(2,1)S(1)}, u32[]{:S(2)}, u32[]{:S(2)}) collective-permute-start(bf16[272,1024]{1,0:T(8,128)(2,1)S(1)} %get-tuple-element.107), channel_id=1, source_target_pairs={{0,1},{1,0},{2,3},{3,2},{4,5},{5,4},{6,7},{7,6},{8,9},{9,8},{10,11... | collective-permute-start | bytes 1671176 | tf_op jit(solution)/shard_map/ppermute | solution.py:658
  188.6 41.7 %collective-permute-start.19 = (bf16[272,1024]{1,0:T(8,128)(2,1)}, bf16[272,1024]{1,0:T(8,128)(2,1)}, u32[]{:S(2)}, u32[]{:S(2)}) collective-permute-start(bf16[272,1024]{1,0:T(8,128)(2,1)} %add_convert_fusion.2.rest_0_), channel_id=1, source_target_pairs={{0,4},{1,5},{2,6},{3,7},{4,0},{5,1},{6,2},{7,3},{8,12},{9,13},{10,... | collective-permute-start | bytes 1671176 | tf_op jit(solution)/shard_map/ppermute | solution.py:655
  189.3 41.0 %collective-permute-start.15 = (bf16[272,1024]{1,0:T(8,128)(2,1)}, bf16[272,1024]{1,0:T(8,128)(2,1)}, u32[]{:S(2)}, u32[]{:S(2)}) collective-permute-start(bf16[272,1024]{1,0:T(8,128)(2,1)} %after.15), channel_id=1, source_target_pairs={{0,1},{1,0},{2,3},{3,2},{4,5},{5,4},{6,7},{7,6},{8,9},{9,8},{10,11... | collective-permute-start | bytes 1671176 | tf_op jit(solution)/shard_map/ppermute | solution.py:658
  195.7 34.7 %collective-permute-start.17 = (bf16[272,1024]{1,0:T(8,128)(2,1)}, bf16[272,1024]{1,0:T(8,128)(2,1)}, u32[]{:S(2)}, u32[]{:S(2)}) collective-permute-start(bf16[272,1024]{1,0:T(8,128)(2,1)} %add_convert_fusion.3), channel_id=1, source_target_pairs={{0,6},{1,7},{2,0},{3,1},{4,2},{5,3},{6,4},{7,5},{8,14},{9,15},{10,... | collective-permute-start | bytes 1671176 | tf_op jit(solution)/shard_map/ppermute | solution.py:655
  206.5 23.9 %collective-permute-start.20 = (bf16[272,1024]{1,0:T(8,128)(2,1)}, bf16[272,1024]{1,0:T(8,128)(2,1)}, u32[]{:S(2)}, u32[]{:S(2)}) collective-permute-start(bf16[272,1024]{1,0:T(8,128)(2,1)} %add_convert_fusion.5.refs_1_.rest_1_), channel_id=1, source_target_pairs={{0,2},{1,3},{2,4},{3,5},{4,6},{5,7},{6,0},{7,1},{8,10},{9,11},{10,... | collective-permute-start | bytes 1671176 | tf_op jit(solution)/shard_map/ppermute | solution.py:655
  210.7 25.9 %collective-permute-start.21 = (bf16[2,256,1024]{2,1,0:T(8,128)(2,1)}, bf16[2,256,1024]{2,1,0:T(8,128)(2,1)S(1)}, u32[]{:S(2)}, u32[]{:S(2)}) collective-permute-start(bf16[2,256,1024]{2,1,0:T(8,128)(2,1)} %get-tuple-element.157), channel_id=1, source_target_pairs={{0,1},{1,0},{2,3},{3,2},{4,5},{5,4},{6,7},{7,6},{8,9},{9,8},{10,11... | collective-permute-start | bytes 3145736 | tf_op jit(solution)/shard_map/ppermute | solution.py:658
  210.7 26.9 %copy-start.9 = (f32[256,1024]{1,0:T(8,128)S(1)}, f32[256,1024]{1,0:T(8,128)}, u32[]{:S(2)}) copy-start(f32[256,1024]{1,0:T(8,128)} %get-tuple-element.84.res_ref) | copy-start | bytes 3145732
  210.7 26.9 %copy-start.20 = (bf16[272,1024]{1,0:T(8,128)(2,1)S(1)}, bf16[272,1024]{1,0:T(8,128)(2,1)}, u32[]{:S(2)}) copy-start(bf16[272,1024]{1,0:T(8,128)(2,1)} %get-tuple-element.85.xa_ref.xg_ref) | copy-start | bytes 1671172
  210.7 26.9 %copy-start.28 = (bf16[1024,32]{0,1:T(8,128)(2,1)S(1)}, bf16[1024,32]{0,1:T(8,128)(2,1)}, u32[]{:S(2)}) copy-start(bf16[1024,32]{0,1:T(8,128)(2,1)} %param.24) | copy-start | bytes 196612
  210.8 26.9 %copy-start.30 = (f32[32,256]{1,0:T(8,128)S(1)}, f32[32,256]{1,0:T(8,128)}, u32[]{:S(2)}) copy-start(f32[32,256]{1,0:T(8,128)} %get-tuple-element.114.gates_ref) | copy-start | bytes 98308
  210.8 26.9 %copy-start.31 = (f32[1024]{0:T(1024)S(1)}, f32[1024]{0:T(1024)}, u32[]{:S(2)}) copy-start(f32[1024]{0:T(1024)} %param.23) | copy-start | bytes 12292
  245.2 26.1 %collective-permute-start.26 = (bf16[4,3,512,512]{3,2,1,0:T(8,128)(2,1)}, bf16[4,3,512,512]{3,2,1,0:T(8,128)(2,1)}, u32[]{:S(2)}, u32[]{:S(2)}) collective-permute-start(bf16[4,3,512,512]{3,2,1,0:T(8,128)(2,1)} %after.19), channel_id=1, source_target_pairs={{0,8},{8,0},{16,24},{24,16},{1,9},{9,1},{17,25},{25,17},{2,10},{10... | collective-permute-start | bytes 18874376 | tf_op jit(solution)/shard_map/ppermute | solution.py:662
  246.4 45.7 %collective-permute-start.22 = (bf16[2,256,1024]{2,1,0:T(8,128)(2,1)S(1)}, bf16[2,256,1024]{2,1,0:T(8,128)(2,1)S(1)}, u32[]{:S(2)}, u32[]{:S(2)}) collective-permute-start(bf16[2,256,1024]{2,1,0:T(8,128)(2,1)S(1)} %copy-done.37), channel_id=1, source_target_pairs={{0,1},{1,0},{2,3},{3,2},{4,5},{5,4},{6,7},{7,6},{8,9},{9,8},{10,11... | collective-permute-start | bytes 3145736 | tf_op jit(solution)/shard_map/ppermute | solution.py:658
  275.2 56.2 %collective-permute-start.34 = (bf16[3,512,512]{2,1,0:T(8,128)(2,1)}, bf16[3,512,512]{2,1,0:T(8,128)(2,1)}, u32[]{:S(2)}, u32[]{:S(2)}) collective-permute-start(bf16[3,512,512]{2,1,0:T(8,128)(2,1)} %plus.14.left_ref), channel_id=1, source_target_pairs={{0,16},{8,24},{16,0},{24,8},{1,17},{9,25},{17,1},{25,9},{2,18},{10... | collective-permute-start | bytes 4718600 | tf_op jit(solution)/shard_map/ppermute | solution.py:662
  280.8 83.4 %collective-permute-start.32 = (bf16[3,512,512]{2,1,0:T(8,128)(2,1)}, bf16[3,512,512]{2,1,0:T(8,128)(2,1)}, u32[]{:S(2)}, u32[]{:S(2)}) collective-permute-start(bf16[3,512,512]{2,1,0:T(8,128)(2,1)} %plus.12.left_ref), channel_id=1, source_target_pairs={{0,16},{8,24},{16,0},{24,8},{1,17},{9,25},{17,1},{25,9},{2,18},{10... | collective-permute-start | bytes 4718600 | tf_op jit(solution)/shard_map/ppermute | solution.py:662
  285.2 114.9 %collective-permute-start.30 = (bf16[3,512,512]{2,1,0:T(8,128)(2,1)}, bf16[3,512,512]{2,1,0:T(8,128)(2,1)}, u32[]{:S(2)}, u32[]{:S(2)}) collective-permute-start(bf16[3,512,512]{2,1,0:T(8,128)(2,1)} %plus.10.left_ref), channel_id=1, source_target_pairs={{0,16},{8,24},{16,0},{24,8},{1,17},{9,25},{17,1},{25,9},{2,18},{10... | collective-permute-start | bytes 4718600 | tf_op jit(solution)/shard_map/ppermute | solution.py:662
  290.9 147.7 %collective-permute-start.27 = (bf16[3,512,512]{2,1,0:T(8,128)(2,1)}, bf16[3,512,512]{2,1,0:T(8,128)(2,1)}, u32[]{:S(2)}, u32[]{:S(2)}) collective-permute-start(bf16[3,512,512]{2,1,0:T(8,128)(2,1)} %plus.8.left_ref), channel_id=1, source_target_pairs={{0,16},{8,24},{16,0},{24,8},{1,17},{9,25},{17,1},{25,9},{2,18},{10... | collective-permute-start | bytes 4718600 | tf_op jit(solution)/shard_map/ppermute | solution.py:662
  292.1 17.6 %collective-permute-start.28 = (bf16[256,1024]{1,0:T(8,128)(2,1)}, bf16[256,1024]{1,0:T(8,128)(2,1)}, u32[]{:S(2)}, u32[]{:S(2)}) collective-permute-start(bf16[256,1024]{1,0:T(8,128)(2,1)} %get-tuple-element.161), channel_id=1, source_target_pairs={{0,1},{1,0},{2,3},{3,2},{4,5},{5,4},{6,7},{7,6},{8,9},{9,8},{10,11... | collective-permute-start | bytes 1572872 | tf_op jit(solution)/shard_map/ppermute | solution.py:658
  316.2 122.4 %all-to-all-start.2 = ((bf16[4,64,1024]{2,1,0:T(8,128)(2,1)}), bf16[4,64,1024]{2,1,0:T(8,128)(2,1)S(1)}, u32[]{:S(2)}, u32[]{:S(2)}) async-start(bf16[4,64,1024]{2,1,0:T(8,128)(2,1)} %bitcast.45), calls=%async_computation.2 | async-start | bytes 1048576 | tf_op jit(solution)/shard_map/all_to_all | solution.py:951
  327.7 115.7 %collective-permute-start.23 = (bf16[256,1024]{1,0:T(8,128)(2,1)}, bf16[256,1024]{1,0:T(8,128)(2,1)}, u32[]{:S(2)}, u32[]{:S(2)}) collective-permute-start(bf16[256,1024]{1,0:T(8,128)(2,1)} %get-tuple-element.158), channel_id=1, source_target_pairs={{0,6},{1,7},{2,0},{3,1},{4,2},{5,3},{6,4},{7,5},{8,14},{9,15},{10,... | collective-permute-start | bytes 1572872 | tf_op jit(solution)/shard_map/ppermute | solution.py:655
  331.5 112.5 %collective-permute-start.24 = (bf16[256,1024]{1,0:T(8,128)(2,1)}, bf16[256,1024]{1,0:T(8,128)(2,1)}, u32[]{:S(2)}, u32[]{:S(2)}) collective-permute-start(bf16[256,1024]{1,0:T(8,128)(2,1)} %get-tuple-element.160), channel_id=1, source_target_pairs={{0,4},{1,5},{2,6},{3,7},{4,0},{5,1},{6,2},{7,3},{8,12},{9,13},{10,... | collective-permute-start | bytes 1572872 | tf_op jit(solution)/shard_map/ppermute | solution.py:655
  364.1 117.8 %collective-permute-start.35 = (bf16[3,512,512]{2,1,0:T(8,128)(2,1)}, bf16[3,512,512]{2,1,0:T(8,128)(2,1)S(1)}, u32[]{:S(2)}, u32[]{:S(2)}) collective-permute-start(bf16[3,512,512]{2,1,0:T(8,128)(2,1)} %plus.15.mine_ref), channel_id=1, source_target_pairs={{0,8},{8,0},{16,24},{24,16},{1,9},{9,1},{17,25},{25,17},{2,10},{10... | collective-permute-start | bytes 4718600 | tf_op jit(solution)/shard_map/ppermute | solution.py:662
  400.1 87.8 %collective-permute-start.33 = (bf16[3,512,512]{2,1,0:T(8,128)(2,1)}, bf16[3,512,512]{2,1,0:T(8,128)(2,1)}, u32[]{:S(2)}, u32[]{:S(2)}) collective-permute-start(bf16[3,512,512]{2,1,0:T(8,128)(2,1)} %plus.13.mine_ref), channel_id=1, source_target_pairs={{0,8},{8,0},{16,24},{24,16},{1,9},{9,1},{17,25},{25,17},{2,10},{10... | collective-permute-start | bytes 4718600 | tf_op jit(solution)/shard_map/ppermute | solution.py:662
  404.0 70.8 %copy-start.10 = (f32[256,1024]{1,0:T(8,128)S(1)}, f32[256,1024]{1,0:T(8,128)}, u32[]{:S(2)}) copy-start(f32[256,1024]{1,0:T(8,128)} %get-tuple-element.84.res_ref) | copy-start | bytes 3145732
  438.6 54.2 %collective-permute-start.31 = (bf16[3,512,512]{2,1,0:T(8,128)(2,1)}, bf16[3,512,512]{2,1,0:T(8,128)(2,1)}, u32[]{:S(2)}, u32[]{:S(2)}) collective-permute-start(bf16[3,512,512]{2,1,0:T(8,128)(2,1)} %plus.11.mine_ref), channel_id=1, source_target_pairs={{0,8},{8,0},{16,24},{24,16},{1,9},{9,1},{17,25},{25,17},{2,10},{10... | collective-permute-start | bytes 4718600 | tf_op jit(solution)/shard_map/ppermute | solution.py:662
  439.4 41.4 %copy-start.2 = (bf16[4,64,1024]{2,1,0:T(8,128)(2,1)S(1)}, bf16[4,64,1024]{2,1,0:T(8,128)(2,1)}, u32[]{:S(2)}) copy-start(bf16[4,64,1024]{2,1,0:T(8,128)(2,1)} %copy-done.1) | copy-start | bytes 1572868
  443.4 54.2 %collective-permute-start.29 = (bf16[3,512,512]{2,1,0:T(8,128)(2,1)}, bf16[3,512,512]{2,1,0:T(8,128)(2,1)}, u32[]{:S(2)}, u32[]{:S(2)}) collective-permute-start(bf16[3,512,512]{2,1,0:T(8,128)(2,1)} %plus.9.mine_ref), channel_id=1, source_target_pairs={{0,8},{8,0},{16,24},{24,16},{1,9},{9,1},{17,25},{25,17},{2,10},{10... | collective-permute-start | bytes 4718600 | tf_op jit(solution)/shard_map/ppermute | solution.py:662
  444.0 30.8 %collective-permute-start.25 = (bf16[256,1024]{1,0:T(8,128)(2,1)S(1)}, bf16[256,1024]{1,0:T(8,128)(2,1)S(1)}, u32[]{:S(2)}, u32[]{:S(2)}) collective-permute-start(bf16[256,1024]{1,0:T(8,128)(2,1)S(1)} %copy-done.39), channel_id=1, source_target_pairs={{0,2},{1,3},{2,4},{3,5},{4,6},{5,7},{6,0},{7,1},{8,10},{9,11},{10,... | collective-permute-start | bytes 1572872 | tf_op jit(solution)/shard_map/ppermute | solution.py:655
  477.3 38.7 %all-to-all-start.1 = ((bf16[4,64,1024]{2,1,0:T(8,128)(2,1)}), bf16[4,64,1024]{2,1,0:T(8,128)(2,1)S(1)}, u32[]{:S(2)}, u32[]{:S(2)}) async-start(bf16[4,64,1024]{2,1,0:T(8,128)(2,1)} %bitcast.42), calls=%async_computation.1 | async-start | bytes 1048576 | tf_op jit(solution)/shard_map/all_to_all | solution.py:951
  (40 other events, 200.5 us)
Sparse Core Ops, SparseCore 0:
  10.1 98.6 all-gather.2
  271.4 209.8 all-reduce.1

commit v6 on v5

--- a/solution.py
+++ b/solution.py
@@ -989,7 +989,7 @@
             struct((EXTRA, width), F32),
         ],
         in_specs=[part(0), part(1), part(2), pl.BlockSpec((EXTRA, width), lambda r: (3 * width // EXTRA, 0))]
-        + [pl.BlockSpec(memory_space=pl.ANY)] * 2,
+        + [pl.BlockSpec(memory_space=pl.ANY)] * 3,
         out_specs=[
             rows_of(width),
             rows_of(inner),
@@ -1000,8 +1000,7 @@
         compiler_params=params(24),
         cost_estimate=took(0.1),
         name="spread",
-    )(*[pltpu.with_memory_space_constraint(shared, pltpu.HBM)] * 4, grad_in, finished[0])
-    hidden_out = after([hidden_out], finished[0])[0]
+    )(*[pltpu.with_memory_space_constraint(shared, pltpu.HBM)] * 4, hidden_out, grad_in, finished[0])
     return (
         hidden_out,
         grad_in.astype(F32),

time: 536 us -> 524 us (0.978)
  local copies, waits for them, and re-layouts: 43.9 us -> 35.2 us
    all_to_all x2, waiting for transfers between devices: 0.01 us -> 19.3 us  [local(): lax.all_to_all(values.reshape(rows_here, block, width), 'seq', 0, 0, tile...]
    ppermute x15, waiting for transfers between devices: 42 us -> 28.6 us  [across(): return lax.ppermute(values, 'seq', [(j, j ^ other) for j in range(shards)])]
    unnamed x96 -> x82, local copies, waits for them, and re-layouts: 26.9 us -> 18.6 us
    ppermute x12, waiting for transfers between devices: 40.2 us -> 32.9 us  [onward(): return lax.ppermute(values, 'seq', [(j, to(j)) for j in range(shards)])]
  transfers between devices with their start and end apart: 41 -> 41, of which waited for: 15 -> 15; matrix products, arithmetic and copies ran while one was open for 7% -> 7% of each run, Pallas kernels for 36% -> 35%
where the time goes in v6:
time: 524 us; the launch traced here: 514 us
  Pallas kernels  194 us (37%)
  waiting for transfers between devices  183 us (35%)
  starting transfers between devices  68.2 us (13%)
  local copies, waits for them, and re-layouts  35.2 us (7%)
  other arithmetic  18.7 us (4%)
  between operations  15 us (3%)
    ppermute x9, waiting for transfers between devices, row_swap(): return lax.ppermute(values, 'rows', [(j, j ^ other) for j in range(count)])  94.1 us
    pallas_call x4, Pallas kernels, local(): pl.pallas_call(functools.partial(expert_kernel, len(kept) + len(tied)), g...  63.3 us
    ppermute x12, waiting for transfers between devices, onward(): return lax.ppermute(values, 'seq', [(j, to(j)) for j in range(shards)])  32.9 us
    pallas_call x8, Pallas kernels, plus(): pl.pallas_call(plus_kernel, grid=(parts,), out_shape=struct((parts, rows,...  31.6 us
    ppermute x12, starting transfers between devices, onward(): return lax.ppermute(values, 'seq', [(j, to(j)) for j in range(shards)])  29.3 us
    ppermute x15, waiting for transfers between devices, across(): return lax.ppermute(values, 'seq', [(j, j ^ other) for j in range(shards)])  28.6 us
    pallas_call x1, Pallas kernels, local(): pl.pallas_call(functools.partial(attention_back_kernel, members, expert_c...  23.3 us
    pallas_call x1, Pallas kernels, local(): pl.pallas_call(functools.partial(front_kernel, members, shards), out_shap...  20.4 us
  transfers between devices with their start and end apart: 41, of which 15 were waited for; matrix products, arithmetic and copies ran while one was open for 7% of the time, Pallas kernels for 35%

profile of v6, /device:TPU:0, one launch (start us, length us, event | category | flops | bytes accessed | tf_op | source)
XLA Modules:
  0.0 514.1 jit_solution(6017369878184707881)
XLA Ops:
  12.1 7.3 %all-to-all-start = ((s32[8,9,256]{2,1,0:T(8,128)}), s32[8,9,256]{2,1,0:T(8,128)S(1)}, u32[]{:S(2)}, u32[]{:S(2)}) async-start(s32[8,9,256]{2,1,0:T(8,128)} %after.10), calls=%async_computation | async-start | bytes 262144 | tf_op jit(solution)/shard_map/all_to_all | solution.py:682
  21.4 2.4 collective-permute-start.3
  27.7 6.6 %all-to-all-done = s32[8,9,256]{2,1,0:T(8,128)S(1)} async-done(((s32[8,9,256]{2,1,0:T(8,128)}), s32[8,9,256]{2,1,0:T(8,128)S(1)}, u32[]{:S(2)}, u32[]{:S(2)}) %all-to-all-start) | async-done | bytes 73760 | tf_op jit(solution)/shard_map/all_to_all | solution.py:682
  36.9 7.9 %collective-permute-done.3.refs_4_ = bf16[64,1024]{1,0:T(8,128)(2,1)S(1)} collective-permute-done((bf16[64,1024]{1,0:T(8,128)(2,1)}, bf16[64,1024]{1,0:T(8,128)(2,1)S(1)}, u32[]{:S(2)}, u32[]{:S(2)}) %collective-permute-start.3) | collective-permute-done | bytes 131104 | tf_op jit(solution)/shard_map/ppermute | solution.py:655
  51.8 20.4 %front.1 = (bf16[512,1024]{1,0:T(8,128)(2,1)}, bf16[256,1024]{1,0:T(8,128)(2,1)}, bf16[4,4,256,128]{3,2,1,0:T(8,128)(2,1)}, bf16[512,512]{1,0:T(8,128)(2,1)}, bf...) custom-call(s32[10]{0:T(128)} %stack.109.me_ref, ...), custom_call_target="tpu_custom_call" | custom-call | flops 9749999616 | tf_op jit(solution)/shard_map/front/pallas_call | solution.py:714
  72.9 8.1 %collective-permute-start.7 = (bf16[272,1024]{1,0:T(8,128)(2,1)}, bf16[272,1024]{1,0:T(8,128)(2,1)S(1)}, u32[]{:S(2)}, u32[]{:S(2)}) collective-permute-start(bf16[272,1024]{1,0:T(8,128)(2,1)} %get-tuple-element.85.xa_ref.xg_ref), channel_id=1, source_target_pairs={{0,2},{1,3},{2,4},{3,5},{4,6},{5,7},{6,0},{7,1},{8,10},{9,11},{10,... | collective-permute-start | bytes 1671176 | tf_op jit(solution)/shard_map/ppermute | solution.py:655
  82.1 12.9 %collective-permute-done.8.refs_1_.xb_ref = bf16[272,1024]{1,0:T(8,128)(2,1)S(1)} collective-permute-done((bf16[272,1024]{1,0:T(8,128)(2,1)}, bf16[272,1024]{1,0:T(8,128)(2,1)S(1)}, u32[]{:S(2)}, u32[]{:S(2)}) %collective-permute-start.8) | collective-permute-done | bytes 557088 | tf_op jit(solution)/shard_map/ppermute | solution.py:658
  95.0 7.7 %collective-permute-done.7.refs_0_ = bf16[272,1024]{1,0:T(8,128)(2,1)S(1)} collective-permute-done((bf16[272,1024]{1,0:T(8,128)(2,1)}, bf16[272,1024]{1,0:T(8,128)(2,1)S(1)}, u32[]{:S(2)}, u32[]{:S(2)}) %collective-permute-start.7) | collective-permute-done | bytes 557088 | tf_op jit(solution)/shard_map/ppermute | solution.py:655
  103.5 2.8 collective-permute-start.13
  110.9 15.8 %experts.4 = (bf16[272,1024]{1,0:T(8,128)(2,1)S(1)}, bf16[272,1024]{1,0:T(8,128)(2,1)S(1)}, bf16[2,4,256,1024]{3,2,1,0:T(8,128)(2,1)}, bf16[8,512,1024]{2,1,0:T(...) custom-call(s32[5]{0:T(128)S(1)} %stack.117.info_ref, ...), custom_call_target="tpu_custom_call" | custom-call | flops 8000000000 | tf_op jit(solution)/shard_map/experts/pallas_call | solution.py:774
  131.2 15.8 %experts.5 = (bf16[272,1024]{1,0:T(8,128)(2,1)S(1)}, bf16[272,1024]{1,0:T(8,128)(2,1)S(1)}, bf16[2,4,256,1024]{3,2,1,0:T(8,128)(2,1)}, bf16[8,512,1024]{2,1,0:T(...) custom-call(s32[5]{0:T(128)S(1)} %stack.123.info_ref, ...), custom_call_target="tpu_custom_call", output_to_operand_aliasing={{2}: (8, {}), {3}: (9, {}), {4}: (10, {}), {5}: (11, {}), {... | custom-call | flops 8000000000 | tf_op jit(solution)/shard_map/experts/pallas_call | solution.py:774
  149.8 16.0 %experts.6 = (bf16[272,1024]{1,0:T(8,128)(2,1)S(1)}, bf16[272,1024]{1,0:T(8,128)(2,1)}, bf16[2,4,256,1024]{3,2,1,0:T(8,128)(2,1)}, bf16[8,512,1024]{2,1,0:T(8,12...) custom-call(s32[5]{0:T(128)S(1)} %stack.120.info_ref, ...), custom_call_target="tpu_custom_call", output_to_operand_aliasing={{2}: (8, {}), {3}: (9, {}), {4}: (10, {}), {5}: (11, {}), {... | custom-call | flops 8000000000 | tf_op jit(solution)/shard_map/experts/pallas_call | solution.py:774
  169.7 15.7 %experts.7 = (bf16[272,1024]{1,0:T(8,128)(2,1)S(1)}, bf16[272,1024]{1,0:T(8,128)(2,1)S(1)}, bf16[2,4,256,1024]{3,2,1,0:T(8,128)(2,1)}, bf16[8,512,1024]{2,1,0:T(...) custom-call(s32[5]{0:T(128)S(1)} %stack.114.info_ref, ...), custom_call_target="tpu_custom_call", output_to_operand_aliasing={{2}: (8, {}), {3}: (9, {}), {4}: (10, {}), {5}: (11, {}), {... | custom-call | flops 8000000000 | tf_op jit(solution)/shard_map/experts/pallas_call | solution.py:774
  191.3 2.3 collective-permute-done.16
  193.6 2.1 add_convert_fusion.3
  197.6 7.9 %collective-permute-done.14 = bf16[272,1024]{1,0:T(8,128)(2,1)} collective-permute-done((bf16[272,1024]{1,0:T(8,128)(2,1)S(1)}, bf16[272,1024]{1,0:T(8,128)(2,1)}, u32[]{:S(2)}, u32[]{:S(2)}) %collective-permute-start.14) | collective-permute-done | bytes 557088 | tf_op jit(solution)/shard_map/ppermute | solution.py:658
  208.1 3.0 dynamic-slice_bitcast_fusion.1
  211.2 19.5 %expert_grads.1 = (bf16[4,3,512,512]{3,2,1,0:T(8,128)(2,1)}, bf16[4,3,512,512]{3,2,1,0:T(8,128)(2,1)}) custom-call(s32[4]{0:T(128)} %pad_add_fusion.2.info_ref, bf16[8,512,1024]{2,1,0:T(8,128)(2,1)} %get-tuple-element.115.xs_ref, bf16[8,512,1024]{2,1,0:T(8,128)(2,1)} %get-tuple-element.116.us_ref, bf16[8,512,512]{2,1,0:T(8,128)(2,1)} %get-tuple-element.117.hs_ref, ...), custom_call_target="tpu_custom_call" | custom-call | flops 30000001024 | tf_op jit(solution)/shard_map/expert_grads/pallas_call | solution.py:854
  232.9 3.9 collective-permute-done.21.rest_1_
  236.8 4.0 middle.1
  244.9 23.3 %attention_back.1 = (bf16[256,1024]{1,0:T(8,128)(2,1)}, bf16[2,256,1024]{2,1,0:T(8,128)(2,1)}, bf16[3200,1024]{1,0:T(8,128)(2,1)}) custom-call(s32[2]{0:T(128)} %pad_add_fusion.1.me_ref, bf16[4,4,256,128]{3,2,1,0:T(8,128)(2,1)} %get-tuple-element.108.qz_ref, bf16[4,4,256,128]{3,2,1,0:T(8,128)(2,1)} %copy-done.8, bf16[512,512]{1,0:T(8,128)(2,1)} %get-tuple-element.122.k_ref, ...), custom_call_target="tpu_custom_call" | custom-call | flops 50000000 | tf_op jit(solution)/shard_map/attention_back/pallas_call | solution.py:892
  268.2 2.1 dynamic-slice_bitcast_fusion.3
  271.3 3.9 plus.14.left_ref
  276.6 4.1 plus.12.left_ref
  281.1 4.1 plus.10.left_ref
  286.8 3.9 plus.8.left_ref
  292.9 3.3 add_convert_fusion
  298.0 5.1 collective-permute-start.23
  303.1 3.9 last.1
  307.0 3.5 all-to-all-start.2
  310.5 17.3 %collective-permute-done.23 = bf16[256,1024]{1,0:T(8,128)(2,1)} collective-permute-done((bf16[256,1024]{1,0:T(8,128)(2,1)}, bf16[256,1024]{1,0:T(8,128)(2,1)}, u32[]{:S(2)}, u32[]{:S(2)}) %collective-permute-start.23) | collective-permute-done | bytes 524320 | tf_op jit(solution)/shard_map/ppermute | solution.py:655
  328.9 2.4 collective-permute-start.25
  331.4 3.9 plus.15.mine_ref
  335.2 24.9 %collective-permute-done.32.right_ref = bf16[3,512,512]{2,1,0:T(8,128)(2,1)} collective-permute-done((bf16[3,512,512]{2,1,0:T(8,128)(2,1)}, bf16[3,512,512]{2,1,0:T(8,128)(2,1)}, u32[]{:S(2)}, u32[]{:S(2)}) %collective-permute-start.32) | collective-permute-done | bytes 1572896 | tf_op jit(solution)/shard_map/ppermute | solution.py:662
  360.1 3.9 plus.13.mine_ref
  364.0 35.0 %collective-permute-done.30.right_ref = bf16[3,512,512]{2,1,0:T(8,128)(2,1)} collective-permute-done((bf16[3,512,512]{2,1,0:T(8,128)(2,1)}, bf16[3,512,512]{2,1,0:T(8,128)(2,1)}, u32[]{:S(2)}, u32[]{:S(2)}) %collective-permute-start.30) | collective-permute-done | bytes 1572896 | tf_op jit(solution)/shard_map/ppermute | solution.py:662
  399.0 3.9 plus.11.mine_ref
  402.9 34.2 %collective-permute-done.28.refs_0_ = bf16[3,512,512]{2,1,0:T(8,128)(2,1)} collective-permute-done((bf16[3,512,512]{2,1,0:T(8,128)(2,1)}, bf16[3,512,512]{2,1,0:T(8,128)(2,1)}, u32[]{:S(2)}, u32[]{:S(2)}) %collective-permute-start.28) | collective-permute-done | bytes 1572896 | tf_op jit(solution)/shard_map/ppermute | solution.py:662
  437.9 3.9 plus.9.mine_ref
  442.3 3.0 add_convert_fusion.6
  445.3 6.1 %all-to-all-start.1 = ((bf16[4,64,1024]{2,1,0:T(8,128)(2,1)}), bf16[4,64,1024]{2,1,0:T(8,128)(2,1)S(1)}, u32[]{:S(2)}, u32[]{:S(2)}) async-start(bf16[4,64,1024]{2,1,0:T(8,128)(2,1)} %bitcast.42), calls=%async_computation.1 | async-start | bytes 1048576 | tf_op jit(solution)/shard_map/all_to_all | solution.py:951
  452.5 19.3 %all-to-all-done.1.rest_0_ = bf16[4,64,1024]{2,1,0:T(8,128)(2,1)S(1)} async-done(((bf16[4,64,1024]{2,1,0:T(8,128)(2,1)}), bf16[4,64,1024]{2,1,0:T(8,128)(2,1)S(1)}, u32[]{:S(2)}, u32[]{:S(2)}) %all-to-all-start.1) | async-done | bytes 524320 | tf_op jit(solution)/shard_map/all_to_all | solution.py:951
  473.0 4.9 finish.4
  477.9 4.9 finish.5
  482.8 4.9 finish.6
  487.7 4.9 finish.7
  492.6 3.4 copy-done
  495.9 8.8 %spread.1 = (f32[1024,1024]{1,0:T(8,128)}, f32[1024,512]{1,0:T(8,128)}, f32[1024,512]{1,0:T(8,128)}, f32[1024,1024]{1,0:T(8,128)}, f32[128,1024]{1,0:T(8,128)S(1)}) custom-call(bf16[3200,1024]{1,0:T(8,128)(2,1)} %all-reduce.2.cloned.1.call-done.query_ref.keyval_ref.output_ref.vectors_ref, ...), custom_call_target="tpu_custom_call" | custom-call | flops 50000000 | tf_op jit(solution)/shard_map/spread/pallas_call | solution.py:981
  (195 shorter events, 70.3 us)
Async XLA Ops:
  7.2 101.6 %all-gather.3.cloned.1.call-start = ((), (), s32[]{:S(2)}) async-start(), calls=%async_computation.4 | async-start | bytes 4718592 | tf_op jit(solution)/shard_map/all_gather | solution.py:692
  12.1 22.2 %all-to-all-start = ((s32[8,9,256]{2,1,0:T(8,128)}), s32[8,9,256]{2,1,0:T(8,128)S(1)}, u32[]{:S(2)}, u32[]{:S(2)}) async-start(s32[8,9,256]{2,1,0:T(8,128)} %after.10), calls=%async_computation | async-start | bytes 262144 | tf_op jit(solution)/shard_map/all_to_all | solution.py:682
  19.4 473.1 %all-reduce.2.cloned.1.call-start = ((), (), s32[]{:S(2)}) async-start(), calls=%async_computation.3 | async-start | bytes 13107200 | tf_op jit(solution)/shard_map/psum | solution.py:977
  19.5 16.3 %collective-permute-start.1 = (bf16[64,1024]{1,0:T(8,128)(2,1)}, bf16[64,1024]{1,0:T(8,128)(2,1)S(1)}, u32[]{:S(2)}, u32[]{:S(2)}) collective-permute-start(bf16[64,1024]{1,0:T(8,128)(2,1)} %get-tuple-element.166.refs_2_), channel_id=1, source_target_pairs={{0,2},{1,3},{2,4},{3,5},{4,6},{5,7},{6,0},{7,1},{8,10},{9,11},{10,... | collective-permute-start | bytes 393224 | tf_op jit(solution)/shard_map/ppermute | solution.py:655
  21.4 23.3 %collective-permute-start.3 = (bf16[64,1024]{1,0:T(8,128)(2,1)}, bf16[64,1024]{1,0:T(8,128)(2,1)S(1)}, u32[]{:S(2)}, u32[]{:S(2)}) collective-permute-start(bf16[64,1024]{1,0:T(8,128)(2,1)} %get-tuple-element.168.refs_3_), channel_id=1, source_target_pairs={{0,4},{1,5},{2,6},{3,7},{4,0},{5,1},{6,2},{7,3},{8,12},{9,13},{10,... | collective-permute-start | bytes 393224 | tf_op jit(solution)/shard_map/ppermute | solution.py:655
  23.8 21.5 %collective-permute-start.5 = (bf16[64,1024]{1,0:T(8,128)(2,1)}, bf16[64,1024]{1,0:T(8,128)(2,1)S(1)}, u32[]{:S(2)}, u32[]{:S(2)}) collective-permute-start(bf16[64,1024]{1,0:T(8,128)(2,1)} %get-tuple-element.165.refs_4_), channel_id=1, source_target_pairs={{0,6},{1,7},{2,0},{3,1},{4,2},{5,3},{6,4},{7,5},{8,14},{9,15},{10,... | collective-permute-start | bytes 393224 | tf_op jit(solution)/shard_map/ppermute | solution.py:655
  25.3 24.3 %collective-permute-start = (bf16[64,1024]{1,0:T(8,128)(2,1)}, bf16[64,1024]{1,0:T(8,128)(2,1)S(1)}, u32[]{:S(2)}, u32[]{:S(2)}) collective-permute-start(bf16[64,1024]{1,0:T(8,128)(2,1)} %get-tuple-element.167.refs_1_.refs_0_), channel_id=1, source_target_pairs={{0,1},{1,0},{2,3},{3,2},{4,5},{5,4},{6,7},{7,6},{8,9},{9,8},{10,11... | collective-permute-start | bytes 393224 | tf_op jit(solution)/shard_map/ppermute | solution.py:658
  35.7 13.8 %collective-permute-start.2 = (bf16[64,1024]{1,0:T(8,128)(2,1)S(1)}, bf16[64,1024]{1,0:T(8,128)(2,1)S(1)}, u32[]{:S(2)}, u32[]{:S(2)}) collective-permute-start(bf16[64,1024]{1,0:T(8,128)(2,1)S(1)} %collective-permute-done.1.refs_2_), channel_id=1, source_target_pairs={{0,1},{1,0},{2,3},{3,2},{4,5},{5,4},{6,7},{7,6},{8,9},{9,8},{10,11... | collective-permute-start | bytes 393224 | tf_op jit(solution)/shard_map/ppermute | solution.py:658
  44.8 5.0 collective-permute-start.4
  45.3 5.8 %collective-permute-start.6 = (bf16[64,1024]{1,0:T(8,128)(2,1)S(1)}, bf16[64,1024]{1,0:T(8,128)(2,1)S(1)}, u32[]{:S(2)}, u32[]{:S(2)}) collective-permute-start(bf16[64,1024]{1,0:T(8,128)(2,1)S(1)} %collective-permute-done.5.refs_6_), channel_id=1, source_target_pairs={{0,1},{1,0},{2,3},{3,2},{4,5},{5,4},{6,7},{7,6},{8,9},{9,8},{10,11... | collective-permute-start | bytes 393224 | tf_op jit(solution)/shard_map/ppermute | solution.py:658
  72.2 22.7 %collective-permute-start.8 = (bf16[272,1024]{1,0:T(8,128)(2,1)}, bf16[272,1024]{1,0:T(8,128)(2,1)S(1)}, u32[]{:S(2)}, u32[]{:S(2)}) collective-permute-start(bf16[272,1024]{1,0:T(8,128)(2,1)} %get-tuple-element.85.xa_ref.xg_ref), channel_id=1, source_target_pairs={{0,1},{1,0},{2,3},{3,2},{4,5},{5,4},{6,7},{7,6},{8,9},{9,8},{10,11... | collective-permute-start | bytes 1671176 | tf_op jit(solution)/shard_map/ppermute | solution.py:658
  72.9 29.8 %collective-permute-start.7 = (bf16[272,1024]{1,0:T(8,128)(2,1)}, bf16[272,1024]{1,0:T(8,128)(2,1)S(1)}, u32[]{:S(2)}, u32[]{:S(2)}) collective-permute-start(bf16[272,1024]{1,0:T(8,128)(2,1)} %get-tuple-element.85.xa_ref.xg_ref), channel_id=1, source_target_pairs={{0,2},{1,3},{2,4},{3,5},{4,6},{5,7},{6,0},{7,1},{8,10},{9,11},{10,... | collective-permute-start | bytes 1671176 | tf_op jit(solution)/shard_map/ppermute | solution.py:655
  103.5 27.7 %collective-permute-start.13 = (bf16[272,1024]{1,0:T(8,128)(2,1)}, bf16[272,1024]{1,0:T(8,128)(2,1)S(1)}, u32[]{:S(2)}, u32[]{:S(2)}) collective-permute-start(bf16[272,1024]{1,0:T(8,128)(2,1)} %after.11.xa_ref), channel_id=1, source_target_pairs={{0,1},{1,0},{2,3},{3,2},{4,5},{5,4},{6,7},{7,6},{8,9},{9,8},{10,11... | collective-permute-start | bytes 1671176 | tf_op jit(solution)/shard_map/ppermute | solution.py:658
  106.3 22.0 %collective-permute-start.9 = (bf16[272,1024]{1,0:T(8,128)(2,1)}, bf16[272,1024]{1,0:T(8,128)(2,1)S(1)}, u32[]{:S(2)}, u32[]{:S(2)}) collective-permute-start(bf16[272,1024]{1,0:T(8,128)(2,1)} %after.11.xa_ref), channel_id=1, source_target_pairs={{0,2},{1,3},{2,4},{3,5},{4,6},{5,7},{6,0},{7,1},{8,10},{9,11},{10,... | collective-permute-start | bytes 1671176 | tf_op jit(solution)/shard_map/ppermute | solution.py:655
  110.9 20.2 %copy-start.13 = (bf16[272,1024]{1,0:T(8,128)(2,1)S(1)}, bf16[272,1024]{1,0:T(8,128)(2,1)}, u32[]{:S(2)}) copy-start(bf16[272,1024]{1,0:T(8,128)(2,1)} %after.11.xa_ref) | copy-start | bytes 1671172
  129.1 20.7 %collective-permute-start.12 = (bf16[272,1024]{1,0:T(8,128)(2,1)}, bf16[272,1024]{1,0:T(8,128)(2,1)S(1)}, u32[]{:S(2)}, u32[]{:S(2)}) collective-permute-start(bf16[272,1024]{1,0:T(8,128)(2,1)} %after.12.xa_ref), channel_id=1, source_target_pairs={{0,1},{1,0},{2,3},{3,2},{4,5},{5,4},{6,7},{7,6},{8,9},{9,8},{10,11... | collective-permute-start | bytes 1671176 | tf_op jit(solution)/shard_map/ppermute | solution.py:658
  130.3 17.5 %collective-permute-start.10 = (bf16[272,1024]{1,0:T(8,128)(2,1)}, bf16[272,1024]{1,0:T(8,128)(2,1)S(1)}, u32[]{:S(2)}, u32[]{:S(2)}) collective-permute-start(bf16[272,1024]{1,0:T(8,128)(2,1)} %after.12.xa_ref), channel_id=1, source_target_pairs={{0,2},{1,3},{2,4},{3,5},{4,6},{5,7},{6,0},{7,1},{8,10},{9,11},{10,... | collective-permute-start | bytes 1671176 | tf_op jit(solution)/shard_map/ppermute | solution.py:655
  147.8 18.1 %collective-permute-start.11 = (bf16[272,1024]{1,0:T(8,128)(2,1)S(1)}, bf16[272,1024]{1,0:T(8,128)(2,1)S(1)}, u32[]{:S(2)}, u32[]{:S(2)}) collective-permute-start(bf16[272,1024]{1,0:T(8,128)(2,1)S(1)} %collective-permute-done.10.xa_ref), channel_id=1, source_target_pairs={{0,1},{1,0},{2,3},{3,2},{4,5},{5,4},{6,7},{7,6},{8,9},{9,8},{10,11... | collective-permute-start | bytes 1671176 | tf_op jit(solution)/shard_map/ppermute | solution.py:658
  165.8 20.7 %collective-permute-start.18 = (bf16[272,1024]{1,0:T(8,128)(2,1)}, bf16[272,1024]{1,0:T(8,128)(2,1)}, u32[]{:S(2)}, u32[]{:S(2)}) collective-permute-start(bf16[272,1024]{1,0:T(8,128)(2,1)} %get-tuple-element.113), channel_id=1, source_target_pairs={{0,1},{1,0},{2,3},{3,2},{4,5},{5,4},{6,7},{7,6},{8,9},{9,8},{10,11... | collective-permute-start | bytes 1671176 | tf_op jit(solution)/shard_map/ppermute | solution.py:658
  166.6 27.0 %collective-permute-start.16 = (bf16[272,1024]{1,0:T(8,128)(2,1)}, bf16[272,1024]{1,0:T(8,128)(2,1)}, u32[]{:S(2)}, u32[]{:S(2)}) collective-permute-start(bf16[272,1024]{1,0:T(8,128)(2,1)} %after.15), channel_id=1, source_target_pairs={{0,1},{1,0},{2,3},{3,2},{4,5},{5,4},{6,7},{7,6},{8,9},{9,8},{10,11... | collective-permute-start | bytes 1671176 | tf_op jit(solution)/shard_map/ppermute | solution.py:658
  185.4 20.1 %collective-permute-start.14 = (bf16[272,1024]{1,0:T(8,128)(2,1)S(1)}, bf16[272,1024]{1,0:T(8,128)(2,1)}, u32[]{:S(2)}, u32[]{:S(2)}) collective-permute-start(bf16[272,1024]{1,0:T(8,128)(2,1)S(1)} %get-tuple-element.107), channel_id=1, source_target_pairs={{0,1},{1,0},{2,3},{3,2},{4,5},{5,4},{6,7},{7,6},{8,9},{9,8},{10,11... | collective-permute-start | bytes 1671176 | tf_op jit(solution)/shard_map/ppermute | solution.py:658
  188.6 42.1 %collective-permute-start.19 = (bf16[272,1024]{1,0:T(8,128)(2,1)}, bf16[272,1024]{1,0:T(8,128)(2,1)}, u32[]{:S(2)}, u32[]{:S(2)}) collective-permute-start(bf16[272,1024]{1,0:T(8,128)(2,1)} %add_convert_fusion.2.rest_0_), channel_id=1, source_target_pairs={{0,4},{1,5},{2,6},{3,7},{4,0},{5,1},{6,2},{7,3},{8,12},{9,13},{10,... | collective-permute-start | bytes 1671176 | tf_op jit(solution)/shard_map/ppermute | solution.py:655
  189.3 41.4 %collective-permute-start.15 = (bf16[272,1024]{1,0:T(8,128)(2,1)}, bf16[272,1024]{1,0:T(8,128)(2,1)}, u32[]{:S(2)}, u32[]{:S(2)}) collective-permute-start(bf16[272,1024]{1,0:T(8,128)(2,1)} %after.14), channel_id=1, source_target_pairs={{0,1},{1,0},{2,3},{3,2},{4,5},{5,4},{6,7},{7,6},{8,9},{9,8},{10,11... | collective-permute-start | bytes 1671176 | tf_op jit(solution)/shard_map/ppermute | solution.py:658
  195.7 35.0 %collective-permute-start.17 = (bf16[272,1024]{1,0:T(8,128)(2,1)}, bf16[272,1024]{1,0:T(8,128)(2,1)}, u32[]{:S(2)}, u32[]{:S(2)}) collective-permute-start(bf16[272,1024]{1,0:T(8,128)(2,1)} %add_convert_fusion.3), channel_id=1, source_target_pairs={{0,6},{1,7},{2,0},{3,1},{4,2},{5,3},{6,4},{7,5},{8,14},{9,15},{10,... | collective-permute-start | bytes 1671176 | tf_op jit(solution)/shard_map/ppermute | solution.py:655
  206.8 23.9 %collective-permute-start.20 = (bf16[272,1024]{1,0:T(8,128)(2,1)S(1)}, bf16[272,1024]{1,0:T(8,128)(2,1)}, u32[]{:S(2)}, u32[]{:S(2)}) collective-permute-start(bf16[272,1024]{1,0:T(8,128)(2,1)S(1)} %add_convert_fusion.5.refs_1_.rest_1_), channel_id=1, source_target_pairs={{0,2},{1,3},{2,4},{3,5},{4,6},{5,7},{6,0},{7,1},{8,10},{9,11},{10,... | collective-permute-start | bytes 1671176 | tf_op jit(solution)/shard_map/ppermute | solution.py:655
  211.1 25.6 %collective-permute-start.21 = (bf16[2,256,1024]{2,1,0:T(8,128)(2,1)}, bf16[2,256,1024]{2,1,0:T(8,128)(2,1)}, u32[]{:S(2)}, u32[]{:S(2)}) collective-permute-start(bf16[2,256,1024]{2,1,0:T(8,128)(2,1)} %get-tuple-element.157), channel_id=1, source_target_pairs={{0,1},{1,0},{2,3},{3,2},{4,5},{5,4},{6,7},{7,6},{8,9},{9,8},{10,11... | collective-permute-start | bytes 3145736 | tf_op jit(solution)/shard_map/ppermute | solution.py:658
  211.2 19.6 %copy-start.11 = (bf16[272,1024]{1,0:T(8,128)(2,1)S(1)}, bf16[272,1024]{1,0:T(8,128)(2,1)}, u32[]{:S(2)}) copy-start(bf16[272,1024]{1,0:T(8,128)(2,1)} %copy-done.10) | copy-start | bytes 1671172
  211.2 25.6 %copy-start.9 = (f32[256,1024]{1,0:T(8,128)S(1)}, f32[256,1024]{1,0:T(8,128)}, u32[]{:S(2)}) copy-start(f32[256,1024]{1,0:T(8,128)} %get-tuple-element.84.res_ref) | copy-start | bytes 3145732
  211.2 25.6 %copy-start.17 = (bf16[272,1024]{1,0:T(8,128)(2,1)S(1)}, bf16[272,1024]{1,0:T(8,128)(2,1)}, u32[]{:S(2)}) copy-start(bf16[272,1024]{1,0:T(8,128)(2,1)} %get-tuple-element.85.xa_ref.xg_ref) | copy-start | bytes 1671172
  211.2 25.6 %copy-start.25 = (bf16[1024,32]{0,1:T(8,128)(2,1)S(1)}, bf16[1024,32]{0,1:T(8,128)(2,1)}, u32[]{:S(2)}) copy-start(bf16[1024,32]{0,1:T(8,128)(2,1)} %param.24) | copy-start | bytes 196612
  211.2 25.6 %copy-start.27 = (f32[32,256]{1,0:T(8,128)S(1)}, f32[32,256]{1,0:T(8,128)}, u32[]{:S(2)}) copy-start(f32[32,256]{1,0:T(8,128)} %get-tuple-element.114.gates_ref) | copy-start | bytes 98308
  211.2 25.6 %copy-start.28 = (f32[1024]{0:T(1024)S(1)}, f32[1024]{0:T(1024)}, u32[]{:S(2)}) copy-start(f32[1024]{0:T(1024)} %param.23) | copy-start | bytes 12292
  243.3 28.0 %collective-permute-start.27 = (bf16[4,3,512,512]{3,2,1,0:T(8,128)(2,1)}, bf16[4,3,512,512]{3,2,1,0:T(8,128)(2,1)}, u32[]{:S(2)}, u32[]{:S(2)}) collective-permute-start(bf16[4,3,512,512]{3,2,1,0:T(8,128)(2,1)} %after.18), channel_id=1, source_target_pairs={{0,8},{8,0},{16,24},{24,16},{1,9},{9,1},{17,25},{25,17},{2,10},{10... | collective-permute-start | bytes 18874376 | tf_op jit(solution)/shard_map/ppermute | solution.py:662
  243.3 47.4 %collective-permute-start.22 = (bf16[2,256,1024]{2,1,0:T(8,128)(2,1)}, bf16[2,256,1024]{2,1,0:T(8,128)(2,1)}, u32[]{:S(2)}, u32[]{:S(2)}) collective-permute-start(bf16[2,256,1024]{2,1,0:T(8,128)(2,1)} %get-tuple-element.156), channel_id=1, source_target_pairs={{0,1},{1,0},{2,3},{3,2},{4,5},{5,4},{6,7},{7,6},{8,9},{9,8},{10,11... | collective-permute-start | bytes 3145736 | tf_op jit(solution)/shard_map/ppermute | solution.py:658
  270.2 27.2 %collective-permute-start.26 = (bf16[256,1024]{1,0:T(8,128)(2,1)}, bf16[256,1024]{1,0:T(8,128)(2,1)S(1)}, u32[]{:S(2)}, u32[]{:S(2)}) collective-permute-start(bf16[256,1024]{1,0:T(8,128)(2,1)} %get-tuple-element.161), channel_id=1, source_target_pairs={{0,1},{1,0},{2,3},{3,2},{4,5},{5,4},{6,7},{7,6},{8,9},{9,8},{10,11... | collective-permute-start | bytes 1572872 | tf_op jit(solution)/shard_map/ppermute | solution.py:658
  275.2 53.7 %collective-permute-start.34 = (bf16[3,512,512]{2,1,0:T(8,128)(2,1)}, bf16[3,512,512]{2,1,0:T(8,128)(2,1)}, u32[]{:S(2)}, u32[]{:S(2)}) collective-permute-start(bf16[3,512,512]{2,1,0:T(8,128)(2,1)} %plus.14.left_ref), channel_id=1, source_target_pairs={{0,16},{8,24},{16,0},{24,8},{1,17},{9,25},{17,1},{25,9},{2,18},{10... | collective-permute-start | bytes 4718600 | tf_op jit(solution)/shard_map/ppermute | solution.py:662
  280.6 79.5 %collective-permute-start.32 = (bf16[3,512,512]{2,1,0:T(8,128)(2,1)}, bf16[3,512,512]{2,1,0:T(8,128)(2,1)}, u32[]{:S(2)}, u32[]{:S(2)}) collective-permute-start(bf16[3,512,512]{2,1,0:T(8,128)(2,1)} %plus.12.left_ref), channel_id=1, source_target_pairs={{0,16},{8,24},{16,0},{24,8},{1,17},{9,25},{17,1},{25,9},{2,18},{10... | collective-permute-start | bytes 4718600 | tf_op jit(solution)/shard_map/ppermute | solution.py:662
  285.2 113.8 %collective-permute-start.30 = (bf16[3,512,512]{2,1,0:T(8,128)(2,1)}, bf16[3,512,512]{2,1,0:T(8,128)(2,1)}, u32[]{:S(2)}, u32[]{:S(2)}) collective-permute-start(bf16[3,512,512]{2,1,0:T(8,128)(2,1)} %plus.10.left_ref), channel_id=1, source_target_pairs={{0,16},{8,24},{16,0},{24,8},{1,17},{9,25},{17,1},{25,9},{2,18},{10... | collective-permute-start | bytes 4718600 | tf_op jit(solution)/shard_map/ppermute | solution.py:662
  290.7 146.4 %collective-permute-start.28 = (bf16[3,512,512]{2,1,0:T(8,128)(2,1)}, bf16[3,512,512]{2,1,0:T(8,128)(2,1)}, u32[]{:S(2)}, u32[]{:S(2)}) collective-permute-start(bf16[3,512,512]{2,1,0:T(8,128)(2,1)} %plus.8.left_ref), channel_id=1, source_target_pairs={{0,16},{8,24},{16,0},{24,8},{1,17},{9,25},{17,1},{25,9},{2,18},{10... | collective-permute-start | bytes 4718600 | tf_op jit(solution)/shard_map/ppermute | solution.py:662
  298.0 29.8 %collective-permute-start.23 = (bf16[256,1024]{1,0:T(8,128)(2,1)}, bf16[256,1024]{1,0:T(8,128)(2,1)}, u32[]{:S(2)}, u32[]{:S(2)}) collective-permute-start(bf16[256,1024]{1,0:T(8,128)(2,1)} %get-tuple-element.158), channel_id=1, source_target_pairs={{0,6},{1,7},{2,0},{3,1},{4,2},{5,3},{6,4},{7,5},{8,14},{9,15},{10,... | collective-permute-start | bytes 1572872 | tf_op jit(solution)/shard_map/ppermute | solution.py:655
  307.0 130.1 %all-to-all-start.2 = ((bf16[4,64,1024]{2,1,0:T(8,128)(2,1)}), bf16[4,64,1024]{2,1,0:T(8,128)(2,1)S(1)}, u32[]{:S(2)}, u32[]{:S(2)}) async-start(bf16[4,64,1024]{2,1,0:T(8,128)(2,1)} %bitcast.45), calls=%async_computation.2 | async-start | bytes 1048576 | tf_op jit(solution)/shard_map/all_to_all | solution.py:951
  327.8 114.0 %collective-permute-start.24 = (bf16[256,1024]{1,0:T(8,128)(2,1)}, bf16[256,1024]{1,0:T(8,128)(2,1)}, u32[]{:S(2)}, u32[]{:S(2)}) collective-permute-start(bf16[256,1024]{1,0:T(8,128)(2,1)} %get-tuple-element.160), channel_id=1, source_target_pairs={{0,4},{1,5},{2,6},{3,7},{4,0},{5,1},{6,2},{7,3},{8,12},{9,13},{10,... | collective-permute-start | bytes 1572872 | tf_op jit(solution)/shard_map/ppermute | solution.py:655
  328.9 113.4 %collective-permute-start.25 = (bf16[256,1024]{1,0:T(8,128)(2,1)}, bf16[256,1024]{1,0:T(8,128)(2,1)}, u32[]{:S(2)}, u32[]{:S(2)}) collective-permute-start(bf16[256,1024]{1,0:T(8,128)(2,1)} %get-tuple-element.159), channel_id=1, source_target_pairs={{0,2},{1,3},{2,4},{3,5},{4,6},{5,7},{6,0},{7,1},{8,10},{9,11},{10,... | collective-permute-start | bytes 1572872 | tf_op jit(solution)/shard_map/ppermute | solution.py:655
  360.1 111.8 %collective-permute-start.35 = (bf16[3,512,512]{2,1,0:T(8,128)(2,1)}, bf16[3,512,512]{2,1,0:T(8,128)(2,1)S(1)}, u32[]{:S(2)}, u32[]{:S(2)}) collective-permute-start(bf16[3,512,512]{2,1,0:T(8,128)(2,1)} %plus.15.mine_ref), channel_id=1, source_target_pairs={{0,8},{8,0},{16,24},{24,16},{1,9},{9,1},{17,25},{25,17},{2,10},{10... | collective-permute-start | bytes 4718600 | tf_op jit(solution)/shard_map/ppermute | solution.py:662
  399.0 78.9 %collective-permute-start.33 = (bf16[3,512,512]{2,1,0:T(8,128)(2,1)}, bf16[3,512,512]{2,1,0:T(8,128)(2,1)}, u32[]{:S(2)}, u32[]{:S(2)}) collective-permute-start(bf16[3,512,512]{2,1,0:T(8,128)(2,1)} %plus.13.mine_ref), channel_id=1, source_target_pairs={{0,8},{8,0},{16,24},{24,16},{1,9},{9,1},{17,25},{25,17},{2,10},{10... | collective-permute-start | bytes 4718600 | tf_op jit(solution)/shard_map/ppermute | solution.py:662
  437.1 45.7 %collective-permute-start.31 = (bf16[3,512,512]{2,1,0:T(8,128)(2,1)}, bf16[3,512,512]{2,1,0:T(8,128)(2,1)}, u32[]{:S(2)}, u32[]{:S(2)}) collective-permute-start(bf16[3,512,512]{2,1,0:T(8,128)(2,1)} %plus.11.mine_ref), channel_id=1, source_target_pairs={{0,8},{8,0},{16,24},{24,16},{1,9},{9,1},{17,25},{25,17},{2,10},{10... | collective-permute-start | bytes 4718600 | tf_op jit(solution)/shard_map/ppermute | solution.py:662
  441.8 45.9 %collective-permute-start.29 = (bf16[3,512,512]{2,1,0:T(8,128)(2,1)}, bf16[3,512,512]{2,1,0:T(8,128)(2,1)}, u32[]{:S(2)}, u32[]{:S(2)}) collective-permute-start(bf16[3,512,512]{2,1,0:T(8,128)(2,1)} %plus.9.mine_ref), channel_id=1, source_target_pairs={{0,8},{8,0},{16,24},{24,16},{1,9},{9,1},{17,25},{25,17},{2,10},{10... | collective-permute-start | bytes 4718600 | tf_op jit(solution)/shard_map/ppermute | solution.py:662
  445.3 26.5 %all-to-all-start.1 = ((bf16[4,64,1024]{2,1,0:T(8,128)(2,1)}), bf16[4,64,1024]{2,1,0:T(8,128)(2,1)S(1)}, u32[]{:S(2)}, u32[]{:S(2)}) async-start(bf16[4,64,1024]{2,1,0:T(8,128)(2,1)} %bitcast.42), calls=%async_computation.1 | async-start | bytes 1048576 | tf_op jit(solution)/shard_map/all_to_all | solution.py:951
  (33 other events, 149.1 us)
Sparse Core Ops, SparseCore 0:
  10.1 98.6 all-gather.2
  271.4 217.1 all-reduce.1
